TPU v7x, 32 devices: a whole 2x2x4 slice. The times are simulated.
32 devices in a mesh: dp: 16 (over z, y, x), rep: 2 (over core).
Axes of the slice: x: 2, y: 2, z: 4, core: 2. Of those that a mesh axis runs over, the one named last changes fastest.
Arguments:
- event_ids: int32 [32, 12288], P('dp'), may hold values from 0 to 4095, as said below
- row_counts: int32 [32], P('dp'), may hold values from 2 to 4096
- table_slot: int32 [26], replicated, may hold values from 0 to 31, as said below
- dense_input: float32 [12288, 13], P(('dp', 'rep')), may hold values from -6 to 6
- labels: int32 [12288], P(('dp', 'rep')), may hold values 0 or 1
- tables: float32 [32, 4096, 39], P('dp'), may hold values from -3 to 3
- tables_m: float32 [32, 4096, 39], P('dp'), may hold values from -1.5258789e-05 to 1.5258789e-05
- tables_v: float32 [32, 4096, 39], P('dp'), may hold values from 5.9604643e-12 to 2.3841857e-11
- cross_uv: float32 [3, 2, 1027, 256], P(None, None, None, ('dp', 'rep')), may hold values from -0.375 to 0.375
- cross_m: float32 [3, 2, 1027, 256], P(None, None, None, ('dp', 'rep')), may hold values from -0.00010681152 to 0.00010681152
- cross_v: float32 [3, 2, 1027, 256], P(None, None, None, ('dp', 'rep')), may hold values from 3.2552083e-10 to 1.3020833e-09
- tower_in: float32 [1027, 1024], P(None, ('dp', 'rep')), may hold values from -0.1875 to 0.1875
- tower_in_m: float32 [1027, 1024], P(None, ('dp', 'rep')), may hold values from -0.00021362305 to 0.00021362305
- tower_in_v: float32 [1027, 1024], P(None, ('dp', 'rep')), may hold values from 1.3020833e-09 to 5.2083333e-09
- tower_mid: float32 [1024, 1024], P(None, ('dp', 'rep')), may hold values from -0.1875 to 0.1875
- tower_mid_m: float32 [1024, 1024], P(None, ('dp', 'rep')), may hold values from -0.0009765625 to 0.0009765625
- tower_mid_v: float32 [1024, 1024], P(None, ('dp', 'rep')), may hold values from 3.2552084e-08 to 5.2083334e-07
- head_weight: float32 [1024], P(('dp', 'rep')), may hold values from -0.1875 to 0.1875
- head_m: float32 [1024], P(('dp', 'rep')), may hold values from -0.0390625 to 0.0390625
- head_v: float32 [1024], P(('dp', 'rep')), may hold values from 3.98763e-05 to 0.0006380208
- biases: float32 [5130], replicated, may hold values from -0.625 to 0.625
- biases_m: float32 [5130], replicated, may hold values from -0.00030517578 to 0.00030517578
- biases_v: float32 [5130], replicated, may hold values from 2.9296876e-09 to 1.171875e-08
Outputs:
- loss_sum: float32 [], replicated
- new_tables: float32 [32, 4096, 39], P('dp')
- new_tables_m: float32 [32, 4096, 39], P('dp')
- new_tables_v: float32 [32, 4096, 39], P('dp')
- tables_low: bfloat16 [32, 4096, 39], P('dp')
- new_cross: float32 [3, 2, 1027, 256], P(None, None, None, ('dp', 'rep'))
- new_cross_m: float32 [3, 2, 1027, 256], P(None, None, None, ('dp', 'rep'))
- new_cross_v: float32 [3, 2, 1027, 256], P(None, None, None, ('dp', 'rep'))
- cross_low: bfloat16 [3, 2, 1027, 256], P(None, None, None, ('dp', 'rep'))
- new_tower_in: float32 [1027, 1024], P(None, ('dp', 'rep'))
- new_tower_in_m: float32 [1027, 1024], P(None, ('dp', 'rep'))
- new_tower_in_v: float32 [1027, 1024], P(None, ('dp', 'rep'))
- tower_in_low: bfloat16 [1027, 1024], P(None, ('dp', 'rep'))
- new_tower_mid: float32 [1024, 1024], P(None, ('dp', 'rep'))
- new_tower_mid_m: float32 [1024, 1024], P(None, ('dp', 'rep'))
- new_tower_mid_v: float32 [1024, 1024], P(None, ('dp', 'rep'))
- tower_mid_low: bfloat16 [1024, 1024], P(None, ('dp', 'rep'))
- new_head: float32 [1024], P(('dp', 'rep'))
- new_head_m: float32 [1024], P(('dp', 'rep'))
- new_head_v: float32 [1024], P(('dp', 'rep'))
- head_low: bfloat16 [1024], P(('dp', 'rep'))
- new_biases: float32 [5130], replicated
- new_biases_m: float32 [5130], replicated
- new_biases_v: float32 [5130], replicated
- biases_low: bfloat16 [5130], replicated
Inputs may be any that keep to these rules, and one draw needn't show every extreme that they name: event_ids[s, e] is below row_counts[s]; small ids are rare and ids near the table's end common. `table_slot`: all 26 entries differ.
All inputs are finite; a program needn't handle non-finite values. No bound on the sum of `labels` on one device may be relied on, other than what follows from the above.
Results may differ from a plain program's by a relative error of at most 0.012.
The roundings to bfloat16 on the way count: a program that leaves them out, or rounds other values in their place, can miss the bound.
Values may be sent and summed in bfloat16 or wider, within the bound.
A program may use at most 128 MiB of HBM per device.

v0:
```python
import math

import jax
import jax.numpy as jnp
from jax import lax
from jax.sharding import PartitionSpec as P

TABLES = 26
EMB = 39
HIDDEN_SIZE = 1024
LAYERS = 3
MICRO = 3
STEP = 5
WIDTH = 1027


BETA_ONE = 0.5
BETA_TWO = 0.5
EPSILON = 1e-10
WEIGHT_DECAY = 0.01
RATE_DENSE = 0.01
RATE_BIAS = 0.05
RATE_TABLE = 0.2
HIGHEST_PRECISION = lax.Precision.HIGHEST


def adamw_update(weight, moment_one, moment_two, gradient, step_rate):
    moment_new = BETA_ONE * moment_one + (1 - BETA_ONE) * gradient
    second = BETA_TWO * moment_two + (1 - BETA_TWO) * gradient * gradient
    scaled_one = moment_new / (1 - BETA_ONE**STEP)
    scaled_two = second / (1 - BETA_TWO**STEP)
    fresh = weight - step_rate * (
        scaled_one / (jnp.sqrt(scaled_two) + EPSILON) + WEIGHT_DECAY * weight
    )
    return (fresh, moment_new, second)


def silu_slope(pre_value):
    sigmoid_value = jax.nn.sigmoid(pre_value)
    return sigmoid_value * (1.0 + pre_value * (1.0 - sigmoid_value))


def contract_rows(left_side, right_side):
    return lax.dot_general(
        left_side, right_side, (((0,), (0,)), ((), ())), preferred_element_type=jnp.float32
    )


def contract_cols(left_side, right_side):
    return lax.dot_general(
        left_side, right_side, (((1,), (1,)), ((), ())), preferred_element_type=jnp.float32
    )


def one_hot_rows(positions, row_total):
    return (positions[:, None] == jnp.arange(row_total, dtype=jnp.int32)[None, :]).astype(
        jnp.bfloat16
    )


def lookup_rows(table_piece, positions):
    count = positions.shape[0]
    block = math.gcd(count, 512)
    blocks = positions.reshape(count // block, block)

    def one_block(block_ids):
        return jnp.dot(
            one_hot_rows(block_ids, table_piece.shape[0]),
            table_piece,
            preferred_element_type=jnp.float32,
        ).astype(jnp.bfloat16)

    return lax.map(one_block, blocks).reshape(count, table_piece.shape[1])


def accumulate_rows(entry_rows, positions, row_total):
    count = positions.shape[0]
    block = math.gcd(count, 512)
    blocks = positions.reshape(count // block, block)
    entry_blocks = entry_rows.reshape(count // block, block, entry_rows.shape[1])

    def add_block(running, pair):
        block_ids, block_rows = pair
        return (running + contract_rows(one_hot_rows(block_ids, row_total), block_rows), None)

    start = jnp.zeros((row_total, entry_rows.shape[1]), jnp.float32)
    summed, unused = lax.scan(add_block, start, (blocks, entry_blocks))
    return summed


def cross_forward(anchor, carried, cross_full, layer_bias, which_layer):
    carried_low = carried.astype(jnp.bfloat16)
    project = jnp.dot(
        carried_low, cross_full[which_layer, 0], preferred_element_type=jnp.float32
    ).astype(jnp.bfloat16)
    crossed = contract_cols(project, cross_full[which_layer, 1])
    return (anchor * (crossed + layer_bias[which_layer]) + carried, (carried_low, project, crossed))


def cross_backward(anchor, grad_carried, saved_values, cross_full, layer_bias, which_layer):
    carried_low, project, crossed = saved_values
    grad_cross = grad_carried * anchor
    bias_grad = jnp.sum(grad_cross, axis=0)
    grad_cross_low = grad_cross.astype(jnp.bfloat16)
    grad_up = contract_rows(grad_cross_low, project)
    grad_project = jnp.dot(
        grad_cross_low, cross_full[which_layer, 1], preferred_element_type=jnp.float32
    ).astype(jnp.bfloat16)
    grad_down = contract_rows(carried_low, grad_project)
    grad_input = contract_cols(grad_project, cross_full[which_layer, 0]) + grad_carried
    extra_grad = grad_carried * (crossed + layer_bias[which_layer])
    return (grad_input, extra_grad, jnp.stack([grad_down, grad_up]), bias_grad)


def micro_step(gathered, biases, emb_flat, dense_rows, target, total_events):
    cross_full, tower_full, mid_full, head_full = gathered
    layer_bias = biases[: LAYERS * WIDTH].reshape(LAYERS, WIDTH)
    bias_one = biases[LAYERS * WIDTH : LAYERS * WIDTH + HIDDEN_SIZE]
    bias_two = biases[LAYERS * WIDTH + HIDDEN_SIZE : LAYERS * WIDTH + 2 * HIDDEN_SIZE]
    bias_out = biases[LAYERS * WIDTH + 2 * HIDDEN_SIZE]
    dense_low = lax.optimization_barrier(dense_rows.astype(jnp.bfloat16)).astype(jnp.float32)
    anchor = jnp.concatenate([emb_flat.astype(jnp.float32), dense_low], axis=1)
    carried = anchor
    saved_all = []
    for which_layer in range(LAYERS):
        carried, saved_values = cross_forward(anchor, carried, cross_full, layer_bias, which_layer)
        saved_all.append(saved_values)
    carried_low = carried.astype(jnp.bfloat16)
    pre_one = jnp.dot(carried_low, tower_full, preferred_element_type=jnp.float32) + bias_one
    hidden_one = jax.nn.silu(pre_one).astype(jnp.bfloat16)
    pre_two = jnp.dot(hidden_one, mid_full, preferred_element_type=jnp.float32) + bias_two
    hidden_two = jax.nn.silu(pre_two).astype(jnp.bfloat16)
    logits = jnp.dot(hidden_two, head_full, preferred_element_type=jnp.float32) + bias_out
    loss_part = jnp.sum(jax.nn.softplus(logits) - target * logits)
    grad_logits = (jax.nn.sigmoid(logits) - target) / total_events
    grad_head = jnp.dot(grad_logits, hidden_two.astype(jnp.float32), precision=HIGHEST_PRECISION)
    grad_hidden_two = grad_logits[:, None] * head_full.astype(jnp.float32)[None, :]
    grad_pre_two = (grad_hidden_two * silu_slope(pre_two)).astype(jnp.bfloat16)
    grad_mid = contract_rows(hidden_one, grad_pre_two)
    grad_hidden_one = contract_cols(grad_pre_two, mid_full)
    grad_pre_one = (grad_hidden_one * silu_slope(pre_one)).astype(jnp.bfloat16)
    grad_tower = contract_rows(carried_low, grad_pre_one)
    grad_carried = contract_cols(grad_pre_one, tower_full)
    grad_anchor = jnp.zeros_like(anchor)
    cross_grads = [None] * LAYERS
    layer_grads = [None] * LAYERS
    for which_layer in reversed(range(LAYERS)):
        grad_carried, extra_grad, grad_pair, bias_grad = cross_backward(
            anchor, grad_carried, saved_all[which_layer], cross_full, layer_bias, which_layer
        )
        grad_anchor = grad_anchor + extra_grad
        cross_grads[which_layer] = grad_pair
        layer_grads[which_layer] = bias_grad
    grad_anchor = grad_anchor + grad_carried
    grad_emb = grad_anchor[:, : TABLES * EMB].astype(jnp.bfloat16)
    bias_grads = jnp.concatenate(
        [
            jnp.stack(layer_grads).reshape(-1),
            jnp.sum(grad_pre_one.astype(jnp.float32), axis=0),
            jnp.sum(grad_pre_two.astype(jnp.float32), axis=0),
            jnp.sum(grad_logits)[None],
        ]
    )
    dense_grads = (jnp.stack(cross_grads), grad_tower, grad_mid, grad_head)
    return (loss_part, grad_emb, dense_grads, bias_grads)


def shards(
    event_ids,
    row_counts,
    table_slot,
    dense_input,
    labels,
    tables,
    tables_m,
    tables_v,
    cross_uv,
    cross_m,
    cross_v,
    tower_in,
    tower_in_m,
    tower_in_v,
    tower_mid,
    tower_mid_m,
    tower_mid_v,
    head_weight,
    head_m,
    head_v,
    biases,
    biases_m,
    biases_v,
):
    dp_count = lax.axis_size("dp")
    rep_count = lax.axis_size("rep")
    rep_index = lax.axis_index("rep")
    slot_count = tables.shape[0]
    row_total = tables.shape[1]
    device_events = labels.shape[0]
    micro_events = device_events // MICRO
    total_events = float(device_events * dp_count * rep_count)
    shard_set = (cross_uv, tower_in, tower_mid, head_weight)
    shard_low = tuple((shard_piece.astype(jnp.bfloat16) for shard_piece in shard_set))
    event_grid = event_ids.reshape(slot_count, dp_count, rep_count, MICRO, micro_events)
    own_ids = lax.dynamic_index_in_dim(event_grid, rep_index, 2, keepdims=False)
    table_low = tables.astype(jnp.bfloat16)
    selector = (
        table_slot[:, None] == jnp.arange(dp_count * slot_count, dtype=jnp.int32)[None, :]
    ).astype(jnp.bfloat16)
    loss_total = jnp.zeros((), jnp.float32)
    bias_total = jnp.zeros(biases.shape, jnp.float32)
    table_grad = jnp.zeros(tables.shape, jnp.float32)
    dense_total = None
    for micro_index in range(MICRO):
        gathered = (
            lax.all_gather(shard_low[0], ("dp", "rep"), axis=3, tiled=True),
            lax.all_gather(shard_low[1], ("dp", "rep"), axis=1, tiled=True),
            lax.all_gather(shard_low[2], ("dp", "rep"), axis=1, tiled=True),
            lax.all_gather(shard_low[3], ("dp", "rep"), axis=0, tiled=True),
        )
        micro_ids = own_ids[:, :, micro_index, :].reshape(slot_count, dp_count * micro_events)
        looked = jax.vmap(lookup_rows)(table_low, micro_ids)
        outgoing = jnp.transpose(
            looked.reshape(slot_count, dp_count, micro_events, EMB), (1, 0, 2, 3)
        )
        arrived = lax.all_to_all(outgoing, "dp", split_axis=0, concat_axis=0, tiled=True)
        by_slot = arrived.reshape(dp_count * slot_count, micro_events, EMB)
        picked = jnp.einsum(
            "ts,sec->tec", selector, by_slot, preferred_element_type=jnp.float32
        ).astype(jnp.bfloat16)
        emb_flat = jnp.transpose(picked, (1, 0, 2)).reshape(micro_events, TABLES * EMB)
        row_lo = micro_index * micro_events
        dense_rows = dense_input[row_lo : row_lo + micro_events]
        target = labels[row_lo : row_lo + micro_events].astype(jnp.float32)
        loss_part, grad_emb, dense_grads, bias_grads = micro_step(
            gathered, biases, emb_flat, dense_rows, target, total_events
        )
        loss_total = loss_total + loss_part
        bias_total = bias_total + bias_grads
        if micro_index == 0:
            dense_total = dense_grads
        else:
            dense_total = tuple(
                (running + fresh_part for running, fresh_part in zip(dense_total, dense_grads))
            )
        grad_tables = jnp.transpose(grad_emb.reshape(micro_events, TABLES, EMB), (1, 0, 2))
        slot_grads = jnp.einsum(
            "ts,tec->sec", selector, grad_tables, preferred_element_type=jnp.float32
        ).astype(jnp.bfloat16)
        returned = lax.all_to_all(
            slot_grads.reshape(dp_count, slot_count, micro_events, EMB),
            "dp",
            split_axis=0,
            concat_axis=0,
            tiled=True,
        )
        entries = jnp.transpose(returned, (1, 0, 2, 3)).reshape(
            slot_count, dp_count * micro_events, EMB
        )
        table_grad = table_grad + jax.vmap(
            lambda entry_rows, positions: accumulate_rows(entry_rows, positions, row_total)
        )(entries, micro_ids)
    dense_total = (
        lax.psum_scatter(dense_total[0], ("dp", "rep"), scatter_dimension=3, tiled=True),
        lax.psum_scatter(dense_total[1], ("dp", "rep"), scatter_dimension=1, tiled=True),
        lax.psum_scatter(dense_total[2], ("dp", "rep"), scatter_dimension=1, tiled=True),
        lax.psum_scatter(dense_total[3], ("dp", "rep"), scatter_dimension=0, tiled=True),
    )
    table_grad = lax.psum(table_grad, "rep")
    bias_total, loss_total = lax.psum((bias_total, loss_total), ("dp", "rep"))
    fresh_tab, fresh_tab_m, fresh_tab_v = adamw_update(
        tables, tables_m, tables_v, table_grad, RATE_TABLE
    )
    in_use = (jnp.arange(row_total, dtype=jnp.int32)[None, :] < row_counts[:, None])[:, :, None]
    fresh_tab = jnp.where(in_use, fresh_tab, tables)
    fresh_tab_m = jnp.where(in_use, fresh_tab_m, tables_m)
    fresh_tab_v = jnp.where(in_use, fresh_tab_v, tables_v)
    weight_set = shard_set + (biases,)
    grad_set = tuple(dense_total) + (bias_total,)
    states = (
        (cross_m, cross_v, RATE_DENSE),
        (tower_in_m, tower_in_v, RATE_DENSE),
        (tower_mid_m, tower_mid_v, RATE_DENSE),
        (head_m, head_v, RATE_DENSE),
        (biases_m, biases_v, RATE_BIAS),
    )
    results = []
    for weight, gradient, state in zip(weight_set, grad_set, states):
        fresh, moment_new, second = adamw_update(weight, state[0], state[1], gradient, state[2])
        results.append((fresh, moment_new, second, fresh.astype(jnp.bfloat16)))
    return (
        loss_total,
        fresh_tab,
        fresh_tab_m,
        fresh_tab_v,
        fresh_tab.astype(jnp.bfloat16),
        results[0][0],
        results[0][1],
        results[0][2],
        results[0][3],
        results[1][0],
        results[1][1],
        results[1][2],
        results[1][3],
        results[2][0],
        results[2][1],
        results[2][2],
        results[2][3],
        results[3][0],
        results[3][1],
        results[3][2],
        results[3][3],
        results[4][0],
        results[4][1],
        results[4][2],
        results[4][3],
    )


def solution(mesh):
    placed = (
        P("dp", None),
        P("dp"),
        P(),
        P(("dp", "rep"), None),
        P(("dp", "rep")),
        P("dp", None, None),
        P("dp", None, None),
        P("dp", None, None),
        P(None, None, None, ("dp", "rep")),
        P(None, None, None, ("dp", "rep")),
        P(None, None, None, ("dp", "rep")),
        P(None, ("dp", "rep")),
        P(None, ("dp", "rep")),
        P(None, ("dp", "rep")),
        P(None, ("dp", "rep")),
        P(None, ("dp", "rep")),
        P(None, ("dp", "rep")),
        P(("dp", "rep")),
        P(("dp", "rep")),
        P(("dp", "rep")),
        P(),
        P(),
        P(),
    )
    return jax.shard_map(
        shards,
        mesh=mesh,
        in_specs=placed,
        out_specs=(
            P(),
            P("dp", None, None),
            P("dp", None, None),
            P("dp", None, None),
            P("dp", None, None),
            P(None, None, None, ("dp", "rep")),
            P(None, None, None, ("dp", "rep")),
            P(None, None, None, ("dp", "rep")),
            P(None, None, None, ("dp", "rep")),
            P(None, ("dp", "rep")),
            P(None, ("dp", "rep")),
            P(None, ("dp", "rep")),
            P(None, ("dp", "rep")),
            P(None, ("dp", "rep")),
            P(None, ("dp", "rep")),
            P(None, ("dp", "rep")),
            P(None, ("dp", "rep")),
            P(("dp", "rep")),
            P(("dp", "rep")),
            P(("dp", "rep")),
            P(("dp", "rep")),
            P(),
            P(),
            P(),
            P(),
        ),
        check_vma=False,
    )
```

profile of v0, /device:TPU:0, one launch (start us, length us, event | category | flops | bytes accessed | tf_op | source)
XLA Modules:
  0.0 852.4 jit_solution(1082371912435398303)
XLA Ops:
  12.4 13.2 %while.63 = (s32[]{:T(128)}, bf16[4,2,512,39]{2,3,1,0:T(8,128)(2,1)S(1)}, s32[4,2,512]{2,1,0:T(2,128)S(1)}, bf16[2,4096,39]{1,2,0:T(8,128)(2,1)S(1)}, s32[]{:T(128)}) while((s32[]{:T(128)}, bf16[4,2,512,39]{2,3,1,0:T(8,128)(2,1)S(1)}, s32[4,2,512]{2,1,0:T(2,128)S(1)}, bf16[2,4096,39]{1,2,0:T(8,128)(2,1)S(1)}, s32[]{:T(128)}) %tuple.203), condition=%wide.region_1.2_spmd, body=%wide.region_0.1_spmd.sunk | while | flops 331389952 | bytes 749645 | solution.py:73
  12.5 3.3 fusion.282
  15.8 3.3 fusion.282
  19.1 3.3 fusion.282
  22.4 3.3 fusion.282
  27.1 8.3 all-to-all-start
  36.2 13.2 %while.64 = (s32[]{:T(128)}, bf16[4,2,512,39]{2,3,1,0:T(8,128)(2,1)S(1)}, s32[4,2,512]{2,1,0:T(2,128)S(1)}, bf16[2,4096,39]{1,2,0:T(8,128)(2,1)S(1)}, s32[]{:T(128)}) while((s32[]{:T(128)}, bf16[4,2,512,39]{2,3,1,0:T(8,128)(2,1)S(1)}, s32[4,2,512]{2,1,0:T(2,128)S(1)}, bf16[2,4096,39]{1,2,0:T(8,128)(2,1)S(1)}, s32[]{:T(128)}) %tuple.238), condition=%wide.region_4.5_spmd, body=%wide.region_3.4_spmd.sunk | while | flops 331389952 | bytes 749645 | solution.py:73
  36.2 3.3 fusion.284
  39.5 3.3 fusion.284
  42.8 3.3 fusion.284
  46.1 3.3 fusion.284
  51.4 7.2 all-to-all-start.1
  58.6 13.2 %while.65 = (s32[]{:T(128)}, bf16[4,2,512,39]{2,3,1,0:T(8,128)(2,1)S(1)}, s32[4,2,512]{2,1,0:T(2,128)S(1)}, bf16[2,4096,39]{1,2,0:T(8,128)(2,1)S(1)}, s32[]{:T(128)}) while((s32[]{:T(128)}, bf16[4,2,512,39]{2,3,1,0:T(8,128)(2,1)S(1)}, s32[4,2,512]{2,1,0:T(2,128)S(1)}, bf16[2,4096,39]{1,2,0:T(8,128)(2,1)S(1)}, s32[]{:T(128)}) %tuple.239), condition=%wide.region_7.8_spmd, body=%wide.region_6.7_spmd.sunk | while | flops 331389952 | bytes 749645 | solution.py:73
  58.7 3.3 fusion.286
  62.0 3.3 fusion.286
  65.3 3.3 fusion.286
  68.6 3.3 fusion.286
  72.2 40.9 %all-reduce = bf16[1024]{0:T(1024)(128)(2,1)S(1)} all-reduce(bf16[1024]{0:T(1024)(128)(2,1)S(1)} %dynamic-update-slice), channel_id=1, replica_groups=mesh['dp'=16,'rep'=2] {'dp','rep'}, use_global_device_ids=true, to_apply=%add | all-reduce | flops 1024 | bytes 4096
  116.9 5.3 all-to-all-start.2
  125.8 11.1 %all-to-all-done.2 = bf16[16,2,128,39]{2,1,3,0:T(2,128)(2,1)S(1)} async-done(((bf16[16,2,128,39]{2,1,3,0:T(2,128)(2,1)}), bf16[16,2,128,39]{2,1,3,0:T(2,128)(2,1)S(1)}, u32[]{:S(2)}, u32[]{:S(2)}) %all-to-all-start.2) | async-done | bytes 319520 | tf_op jit(solution)/shard_map/all_to_all | solution.py:225
  142.1 1.7 convolution_convert_fusion.16
  147.4 3.5 convolution_add_fusion.17
  150.9 48.3 %all-gather.8.cloned.1.call-done = bf16[1024,1024]{0,1:T(8,128)(2,1)} async-done(((bf16[1024,32]{0,1:T(8,128)(2,1)}), bf16[1024,1024]{0,1:T(8,128)(2,1)}) %all-gather.8.cloned.1.call-update) | async-done | bytes 2097168 | tf_op jit(solution)/shard_map/all_gather | solution.py:217
  199.2 2.6 multiply_convert_fusion.3
  219.2 14.0 %convert_reduce_fusion.2 = (f32[1024]{0:T(1024)}, bf16[128,1024]{1,0:T(8,128)(2,1)}, f32[1024]{0:T(1024)}, bf16[128,1024]{1,0:T(8,128)(2,1)S(1)}, f32[1024]{0:T(1024)S(1)}, /*index=5*/bf16[128,1024]{1,0:T(8,128)(2,1)}) fusion(f32[128,1024]{1,0:T(8,128)S(1)} %get-tuple-element.579, f32[1024]{0:T(1024)S(1)} %copy-done.142, f32[128]{0:T(128)S(1)} %get-tuple-element.539, ...), kind=kLoop, calls=%fused_computation.184 | loop fusion | flops 4715520 | bytes 2377216 | tf_op jit(solution)/shard_map/reduce_sum | solution.py:160
  245.8 1.7 reshape.167
  249.7 4.5 all-to-all-start.5
  254.2 2.9 convert_reduce_fusion.3
  269.1 3.0 convert_reduce_fusion.5
  284.7 3.2 maximum_bitcast_fusion.8
  287.9 2.4 maximum_bitcast_fusion
  292.2 2.3 maximum_bitcast_fusion.6
  294.5 7.4 all-to-all-start.4
  304.5 2.4 maximum_bitcast_fusion.4
  306.9 6.0 all-to-all-done.4
  312.9 4.2 all-to-all-start.3
  317.8 3.6 maximum_bitcast_fusion.2
  324.3 2.3 all-to-all-done.3
  328.6 20.2 %while.68 = (s32[]{:T(128)}, f32[2,4096,39]{1,2,0:T(8,128)S(1)}, s32[4,2,512]{2,1,0:T(2,128)}, bf16[4,2,512,39]{2,3,1,0:T(8,128)(2,1)}, s32[]{:T(128)}, /*index=5*/s32[]{:T(128)}) while((s32[]{:T(128)}, f32[2,4096,39]{1,2,0:T(8,128)S(1)}, s32[4,2,512]{2,1,0:T(2,128)}, bf16[4,2,512,39]{2,3,1,0:T(8,128)(2,1)}, s32[]{:T(128)}, ...), condition=%wide.region_15.16_spmd.clone, body=%wide.region_14.15_spmd.clone.sunk | while | flops 331988992 | bytes 2650207 | solution.py:87
  329.4 4.3 fusion.292
  334.5 4.3 fusion.292
  339.5 4.3 fusion.292
  344.5 4.3 fusion.292
  350.0 20.2 %while.67 = (s32[]{:T(128)}, f32[2,4096,39]{1,2,0:T(8,128)S(1)}, s32[4,2,512]{2,1,0:T(2,128)}, bf16[4,2,512,39]{2,3,1,0:T(8,128)(2,1)}, s32[]{:T(128)}, /*index=5*/s32[]{:T(128)}) while((s32[]{:T(128)}, f32[2,4096,39]{1,2,0:T(8,128)S(1)}, s32[4,2,512]{2,1,0:T(2,128)}, bf16[4,2,512,39]{2,3,1,0:T(8,128)(2,1)}, s32[]{:T(128)}, ...), condition=%wide.region_13.14_spmd.clone, body=%wide.region_12.13_spmd.clone.sunk | while | flops 331988992 | bytes 2650207 | solution.py:87
  350.8 4.3 fusion.290
  355.8 4.3 fusion.290
  360.9 4.3 fusion.290
  365.9 4.3 fusion.290
  371.3 20.3 %while.66 = (s32[]{:T(128)}, f32[2,4096,39]{1,2,0:T(8,128)S(1)}, s32[4,2,512]{2,1,0:T(2,128)}, bf16[4,2,512,39]{2,3,1,0:T(8,128)(2,1)}, s32[]{:T(128)}, /*index=5*/s32[]{:T(128)}) while((s32[]{:T(128)}, f32[2,4096,39]{1,2,0:T(8,128)S(1)}, s32[4,2,512]{2,1,0:T(2,128)}, bf16[4,2,512,39]{2,3,1,0:T(8,128)(2,1)}, s32[]{:T(128)}, ...), condition=%wide.region_11.12_spmd.clone, body=%wide.region_10.11_spmd.clone.sunk | while | flops 331988992 | bytes 2650207 | solution.py:87
  372.0 4.3 fusion.288
  377.1 4.3 fusion.288
  382.1 4.3 fusion.288
  387.1 4.3 fusion.288
  391.6 5.2 copy_add_fusion
  396.9 9.5 %fusion.33 = f32[3,2,1027,256]{3,2,1,0:T(8,128)} fusion(f32[1,2,1027,256]{3,2,1,0:T(8,128)} %get-tuple-element.603, f32[1,2,1027,256]{3,2,1,0:T(8,128)} %get-tuple-element.602, f32[1,2,1027,256]{3,2,1,0:T(8,128)} %get-tuple-element.601, f32[1,2,1027,256]{3,2,1,0:T(8,128)} %get-tuple-element.606, f32[1,2,1027,256]{3,2,1,0:T(8,128)} %get-tuple-element.605, ...), kind=kLoop, calls=%fused_computation.46 | loop fusion | flops 12619776 | bytes 25239552 | tf_op jit(solution)/shard_map/add | solution.py:243
  406.4 12.0 %copy.297 = f32[3,2,1027,256]{2,1,0,3:T(2,128)} copy(f32[3,2,1027,256]{3,2,1,0:T(8,128)} %fusion.33) | data formatting | bytes 12619776 | tf_op jit(solution)/shard_map/add | solution.py:243
  421.3 2.9 convolution_add_fusion
  427.2 2.8 add_add_fusion
  436.5 41.3 %all-reduce.3 = (f32[]{:T(128)}, f32[1024]{0:T(1024)S(1)}, f32[5130]{0:T(1024)S(1)}) all-reduce(f32[]{:T(128)S(6)} %add.514, f32[1024]{0:T(1024)S(1)} %add_add_fusion.2, f32[5130]{0:T(1024)S(1)} %add_add_fusion.1), channel_id=1, replica_groups=mesh['dp'=16,'rep'=2] {'dp','rep'}, use_global_device_ids=true, to_apply=%region_9.10 | all-reduce | flops 6155 | bytes 49240 | tf_op jit(solution)/shard_map/psum | solution.py:269
  479.8 11.1 %fusion.167 = (bf16[2,4096,39]{1,0,2:T(2,128)(2,1)}, f32[2,4096,39]{1,0,2:T(2,128)}, f32[2,4096,39]{1,0,2:T(2,128)}, f32[2,4096,39]{1,0,2:T(2,128)}) fusion(f32[2,4096,39]{1,0,2:T(2,128)S(1)} %copy-done.21, f32[2,4096,39]{1,0,2:T(2,128)} %all-reduce.7.cloned.1.call-done, f32[2,4096,39]{1,0,2:T(2,128)S(1)} %copy-done.57, f32[2,4096,39]{1,0,2:T(2,128)} %param.41, ...), kind=kLoop, calls=%fused_computation.328 | loop fusion | flops 5750784 | bytes 9592832 | tf_op jit(solution)/shard_map/convert_element_type | solution.py:295
  490.9 96.9 %all-reduce.9.cloned.1.call-done = f32[3,2,1027,256]{2,1,0,3:T(2,128)} async-done(((f32[3,2,1027,256]{2,1,0,3:T(2,128)}), f32[3,2,1027,256]{2,1,0,3:T(2,128)}) %all-reduce.9.cloned.1.call-update) | async-done | bytes 6309904
  589.7 111.3 %reduce-scatter.3.cloned.1.call-done = f32[1027,32]{0,1:T(8,128)} async-done(((f32[1027,1024]{0,1:T(8,128)}), f32[1027,32]{0,1:T(8,128)}) %reduce-scatter.3.cloned.1.call-update) | async-done | bytes 131472 | tf_op jit(solution)/shard_map/reduce_scatter | solution.py:264
  701.1 1.8 fusion.163
  702.8 140.8 %reduce-scatter.5.cloned.1.call-done = f32[1024,32]{0,1:T(8,128)} async-done(((f32[1024,1024]{0,1:T(8,128)}), f32[1024,32]{0,1:T(8,128)}) %reduce-scatter.5.cloned.1.call-update) | async-done | bytes 131088 | tf_op jit(solution)/shard_map/reduce_scatter | solution.py:265
  (524 shorter events, 117.6 us)
Async XLA Ops:
  7.2 4.5 copy-start.20
  7.2 131.1 %all-gather.4.cloned.1.call-start = ((), (), s32[]{:S(2)}) async-start(), calls=%async_computation.8 | async-start | bytes 3649536 | tf_op jit(solution)/shard_map/all_gather | solution.py:215
  9.0 138.4 %all-gather.6.cloned.1.call-start = ((), (), s32[]{:S(2)}) async-start(), calls=%async_computation.9 | async-start | bytes 2433024 | tf_op jit(solution)/shard_map/all_gather | solution.py:216
  25.7 10.5 %copy-start.111 = (s32[4,2,512]{2,1,0:T(2,128)}, s32[4,2,512]{2,1,0:T(2,128)S(1)}, u32[]{:S(2)}) copy-start(s32[4,2,512]{2,1,0:T(2,128)S(1)} %get-tuple-element.890) | copy-start | bytes 49156
  25.7 9.7 %copy-start.87 = (f32[1024,32]{0,1:T(8,128)S(1)}, f32[1024,32]{0,1:T(8,128)}, u32[]{:S(2)}) copy-start(f32[1024,32]{0,1:T(8,128)} %param.49) | copy-start | bytes 393220
  27.1 24.3 %all-to-all-start = ((bf16[16,2,128,39]{2,1,3,0:T(2,128)(2,1)}), bf16[16,2,128,39]{2,1,3,0:T(2,128)(2,1)S(1)}, u32[]{:S(2)}, u32[]{:S(2)}) async-start(bf16[16,2,128,39]{2,1,3,0:T(2,128)(2,1)} %copy.263), calls=%async_computation | async-start | bytes 638976 | tf_op jit(solution)/shard_map/all_to_all | solution.py:225
  35.4 163.9 %all-gather.8.cloned.1.call-start = ((), (), s32[]{:S(2)}) async-start(), calls=%async_computation.10 | async-start | bytes 2162688 | tf_op jit(solution)/shard_map/all_gather | solution.py:217
  51.4 65.5 %all-to-all-start.1 = ((bf16[16,2,128,39]{2,1,3,0:T(2,128)(2,1)}), bf16[16,2,128,39]{2,1,3,0:T(2,128)(2,1)S(1)}, u32[]{:S(2)}, u32[]{:S(2)}) async-start(bf16[16,2,128,39]{2,1,3,0:T(2,128)(2,1)} %copy.269), calls=%async_computation.1 | async-start | bytes 638976 | tf_op jit(solution)/shard_map/all_to_all | solution.py:225
  58.6 13.3 %copy-start.153 = (f32[32]{0:T(128)S(1)}, f32[32]{0:T(128)}, u32[]{:S(2)}) copy-start(f32[32]{0:T(128)} %param.52) | copy-start | bytes 388
  58.6 55.6 %copy-start.116 = (f32[5130]{0:T(1024)S(1)}, f32[5130]{0:T(1024)}, u32[]{:S(2)}) copy-start(f32[5130]{0:T(1024)} %param.55) | copy-start | bytes 61564
  58.6 56.2 %copy-start.135 = (f32[384,13]{0,1:T(8,128)S(1)}, f32[384,13]{0,1:T(8,128)}, u32[]{:S(2)}) copy-start(f32[384,13]{0,1:T(8,128)} %param.38) | copy-start | bytes 59908
  71.9 43.0 %copy-start.113 = (s32[4,2,512]{2,1,0:T(2,128)}, s32[4,2,512]{2,1,0:T(2,128)S(1)}, u32[]{:S(2)}) copy-start(s32[4,2,512]{2,1,0:T(2,128)S(1)} %get-tuple-element.892) | copy-start | bytes 49156
  71.9 51.3 %copy-start.138 = (s32[26]{0:T(128)S(1)}, s32[26]{0:T(128)}, u32[]{:S(2)}) copy-start(s32[26]{0:T(128)} %param.37) | copy-start | bytes 316
  116.9 20.0 %all-to-all-start.2 = ((bf16[16,2,128,39]{2,1,3,0:T(2,128)(2,1)}), bf16[16,2,128,39]{2,1,3,0:T(2,128)(2,1)S(1)}, u32[]{:S(2)}, u32[]{:S(2)}) async-start(bf16[16,2,128,39]{2,1,3,0:T(2,128)(2,1)} %copy.275), calls=%async_computation.2 | async-start | bytes 638976 | tf_op jit(solution)/shard_map/all_to_all | solution.py:225
  138.3 5.6 copy-start.1
  138.3 5.6 copy-start.8
  138.3 5.6 copy-start.120
  199.2 4.6 copy-start.122
  212.7 54.2 %copy-start.15 = (f32[128,1027]{0,1:T(8,128)}, f32[128,1027]{0,1:T(8,128)S(1)}, u32[]{:S(2)}) copy-start(f32[128,1027]{0,1:T(8,128)S(1)} %convolution_add_fusion.13) | copy-start | bytes 1577476
  217.6 16.3 %copy-start.43 = (f32[128,1024]{1,0:T(8,128)S(1)}, f32[128,1024]{1,0:T(8,128)}, u32[]{:S(2)}) copy-start(f32[128,1024]{1,0:T(8,128)} %convolution_add_fusion.17) | copy-start | bytes 1572868
  219.2 15.9 %copy-start.147 = (f32[128]{0:T(128)}, f32[128]{0:T(128)S(1)}, u32[]{:S(2)}) copy-start(f32[128]{0:T(128)S(1)} %get-tuple-element.539) | copy-start | bytes 1540
  219.2 15.9 %copy-start.149 = (f32[128]{0:T(128)}, f32[128]{0:T(128)S(1)}, u32[]{:S(2)}) copy-start(f32[128]{0:T(128)S(1)} %get-tuple-element.571) | copy-start | bytes 1540
  219.2 15.9 %copy-start.151 = (f32[128]{0:T(128)}, f32[128]{0:T(128)S(1)}, u32[]{:S(2)}) copy-start(f32[128]{0:T(128)S(1)} %get-tuple-element.573) | copy-start | bytes 1540
  249.7 44.8 %all-to-all-start.5 = ((bf16[16,2,128,39]{2,1,3,0:T(2,128)(2,1)}), bf16[16,2,128,39]{2,1,3,0:T(2,128)(2,1)}, u32[]{:S(2)}, u32[]{:S(2)}) async-start(bf16[16,2,128,39]{2,1,3,0:T(2,128)(2,1)} %copy.292), calls=%async_computation.5 | async-start | bytes 638976 | tf_op jit(solution)/shard_map/all_to_all | solution.py:249
  269.1 4.1 copy-start.4
  273.2 8.6 %copy-start.10 = (f32[128,1027]{0,1:T(8,128)}, f32[128,1027]{0,1:T(8,128)S(1)}, u32[]{:S(2)}) copy-start(f32[128,1027]{0,1:T(8,128)S(1)} %fusion.178) | copy-start | bytes 1577476
  292.2 9.7 %copy-start.60 = (bf16[128,1027]{0,1:T(8,128)(2,1)S(1)}, bf16[128,1027]{0,1:T(8,128)(2,1)}, u32[]{:S(2)}) copy-start(bf16[128,1027]{0,1:T(8,128)(2,1)} %copy-done.59) | copy-start | bytes 788740
  294.5 8.7 %copy-start.58 = (bf16[32,128,39]{1,0,2:T(8,128)(2,1)S(1)}, bf16[32,128,39]{1,0,2:T(8,128)(2,1)}, u32[]{:S(2)}) copy-start(bf16[32,128,39]{1,0,2:T(8,128)(2,1)} %convolution_convert_fusion.2) | copy-start | bytes 958468
  294.5 9.7 %copy-start.16 = (f32[128,1027]{0,1:T(8,128)S(1)}, f32[128,1027]{0,1:T(8,128)}, u32[]{:S(2)}) copy-start(f32[128,1027]{0,1:T(8,128)} %copy-done.15) | copy-start | bytes 1577476
  294.5 9.7 %copy-start.82 = (bf16[128,256]{1,0:T(8,128)(2,1)S(1)}, bf16[128,256]{1,0:T(8,128)(2,1)}, u32[]{:S(2)}) copy-start(bf16[128,256]{1,0:T(8,128)(2,1)} %copy-done.81) | copy-start | bytes 196612
  294.5 18.4 %all-to-all-start.4 = ((bf16[16,2,128,39]{2,1,3,0:T(2,128)(2,1)}), bf16[16,2,128,39]{2,1,3,0:T(2,128)(2,1)S(1)}, u32[]{:S(2)}, u32[]{:S(2)}) async-start(bf16[16,2,128,39]{2,1,3,0:T(2,128)(2,1)} %copy.285), calls=%async_computation.4 | async-start | bytes 638976 | tf_op jit(solution)/shard_map/all_to_all | solution.py:249
  304.5 12.7 %copy-start.84 = (bf16[128,256]{1,0:T(8,128)(2,1)S(1)}, bf16[128,256]{1,0:T(8,128)(2,1)}, u32[]{:S(2)}) copy-start(bf16[128,256]{1,0:T(8,128)(2,1)} %copy-done.83) | copy-start | bytes 196612
  304.5 13.0 %copy-start.90 = (bf16[128,256]{1,0:T(8,128)(2,1)S(1)}, bf16[128,256]{1,0:T(8,128)(2,1)}, u32[]{:S(2)}) copy-start(bf16[128,256]{1,0:T(8,128)(2,1)} %copy-done.89) | copy-start | bytes 196612
  306.9 10.6 %copy-start.11 = (f32[128,1027]{0,1:T(8,128)S(1)}, f32[128,1027]{0,1:T(8,128)}, u32[]{:S(2)}) copy-start(f32[128,1027]{0,1:T(8,128)} %copy-done.10) | copy-start | bytes 1577476
  306.9 10.9 %copy-start.28 = (f32[1,1027,256]{2,1,0:T(8,128)S(1)}, f32[1,1027,256]{2,1,0:T(8,128)}, u32[]{:S(2)}) copy-start(f32[1,1027,256]{2,1,0:T(8,128)} %convolution_bitcast_fusion.10) | copy-start | bytes 3154948
  312.9 13.8 %all-to-all-start.3 = ((bf16[16,2,128,39]{2,1,3,0:T(2,128)(2,1)}), bf16[16,2,128,39]{2,1,3,0:T(2,128)(2,1)}, u32[]{:S(2)}, u32[]{:S(2)}) async-start(bf16[16,2,128,39]{2,1,3,0:T(2,128)(2,1)} %copy.280), calls=%async_computation.3 | async-start | bytes 638976 | tf_op jit(solution)/shard_map/all_to_all | solution.py:249
  317.1 162.6 %all-reduce.7.cloned.1.call-start = ((), (), s32[]{:S(2)}) async-start(), calls=%async_computation.11 | async-start | bytes 2555904 | tf_op jit(solution)/shard_map/psum | solution.py:268
  322.6 6.0 copy-start.55
  328.6 21.4 %copy-start.53 = (f32[2,4096,39]{1,2,0:T(8,128)S(1)}, f32[2,4096,39]{1,2,0:T(8,128)}, u32[]{:S(2)}) copy-start(f32[2,4096,39]{1,2,0:T(8,128)} %custom-call.1) | copy-start | bytes 3833860
  350.0 20.2 %copy-start.52 = (f32[2,4096,39]{1,2,0:T(8,128)S(1)}, f32[2,4096,39]{1,2,0:T(8,128)}, u32[]{:S(2)}) copy-start(f32[2,4096,39]{1,2,0:T(8,128)} %custom-call) | copy-start | bytes 3833860
  391.6 5.3 copy-start.19
  396.9 190.9 %all-reduce.9.cloned.1.call-start = ((), (), s32[]{:S(2)}) async-start(), calls=%async_computation.14 | async-start | bytes 14155776
  418.4 282.7 %reduce-scatter.3.cloned.1.call-start = ((), (), s32[]{:S(2)}) async-start(), calls=%async_computation.12 | async-start | bytes 4866048 | tf_op jit(solution)/shard_map/reduce_scatter | solution.py:264
  424.3 419.3 %reduce-scatter.5.cloned.1.call-start = ((), (), s32[]{:S(2)}) async-start(), calls=%async_computation.13 | async-start | bytes 4325376 | tf_op jit(solution)/shard_map/reduce_scatter | solution.py:265
  430.1 4.5 copy-start.145
  430.1 5.1 copy-start.78
  430.1 5.9 copy-start.76
  430.1 5.9 copy-start.150
  430.1 6.1 copy-start.108
  430.2 6.1 copy-start.148
  430.2 48.9 %copy-start.117 = (f32[5130]{0:T(1024)S(1)}, f32[5130]{0:T(1024)}, u32[]{:S(2)}) copy-start(f32[5130]{0:T(1024)} %param.55) | copy-start | bytes 61564
  430.2 48.9 %copy-start.136 = (f32[5130]{0:T(1024)S(1)}, f32[5130]{0:T(1024)}, u32[]{:S(2)}) copy-start(f32[5130]{0:T(1024)} %param.56) | copy-start | bytes 61564
  430.2 48.9 %copy-start.137 = (f32[5130]{0:T(1024)S(1)}, f32[5130]{0:T(1024)}, u32[]{:S(2)}) copy-start(f32[5130]{0:T(1024)} %param.57) | copy-start | bytes 61564
  430.2 49.6 %copy-start.21 = (f32[2,4096,39]{1,0,2:T(2,128)S(1)}, f32[2,4096,39]{1,0,2:T(2,128)}, u32[]{:S(2)}) copy-start(f32[2,4096,39]{1,0,2:T(2,128)} %param.40) | copy-start | bytes 3833860
  430.2 49.6 %copy-start.57 = (f32[2,4096,39]{1,0,2:T(2,128)S(1)}, f32[2,4096,39]{1,0,2:T(2,128)}, u32[]{:S(2)}) copy-start(f32[2,4096,39]{1,0,2:T(2,128)} %param.42) | copy-start | bytes 3833860
  479.7 109.0 %copy-start.79 = (f32[3,2,1027,8]{2,3,1,0:T(8,128)S(1)}, f32[3,2,1027,8]{2,3,1,0:T(8,128)}, u32[]{:S(2)}) copy-start(f32[3,2,1027,8]{2,3,1,0:T(8,128)} %param.43) | copy-start | bytes 591556
  479.7 109.0 %copy-start.109 = (f32[3,2,1027,8]{2,3,1,0:T(8,128)S(1)}, f32[3,2,1027,8]{2,3,1,0:T(8,128)}, u32[]{:S(2)}) copy-start(f32[3,2,1027,8]{2,3,1,0:T(8,128)} %param.44) | copy-start | bytes 591556
  479.7 109.0 %copy-start.110 = (f32[3,2,1027,8]{2,3,1,0:T(8,128)S(1)}, f32[3,2,1027,8]{2,3,1,0:T(8,128)}, u32[]{:S(2)}) copy-start(f32[3,2,1027,8]{2,3,1,0:T(8,128)} %param.45) | copy-start | bytes 591556
  490.9 210.2 %copy-start.80 = (f32[1027,32]{0,1:T(8,128)S(1)}, f32[1027,32]{0,1:T(8,128)}, u32[]{:S(2)}) copy-start(f32[1027,32]{0,1:T(8,128)} %param.46) | copy-start | bytes 394372
  490.9 210.2 %copy-start.114 = (f32[1027,32]{0,1:T(8,128)S(1)}, f32[1027,32]{0,1:T(8,128)}, u32[]{:S(2)}) copy-start(f32[1027,32]{0,1:T(8,128)} %param.47) | copy-start | bytes 394372
  490.9 210.2 %copy-start.115 = (f32[1027,32]{0,1:T(8,128)S(1)}, f32[1027,32]{0,1:T(8,128)}, u32[]{:S(2)}) copy-start(f32[1027,32]{0,1:T(8,128)} %param.48) | copy-start | bytes 394372
  490.9 352.7 %copy-start.88 = (f32[1024,32]{0,1:T(8,128)S(1)}, f32[1024,32]{0,1:T(8,128)}, u32[]{:S(2)}) copy-start(f32[1024,32]{0,1:T(8,128)} %param.49) | copy-start | bytes 393220
  490.9 352.7 %copy-start.123 = (f32[1024,32]{0,1:T(8,128)S(1)}, f32[1024,32]{0,1:T(8,128)}, u32[]{:S(2)}) copy-start(f32[1024,32]{0,1:T(8,128)} %param.50) | copy-start | bytes 393220
  490.9 352.7 %copy-start.124 = (f32[1024,32]{0,1:T(8,128)S(1)}, f32[1024,32]{0,1:T(8,128)}, u32[]{:S(2)}) copy-start(f32[1024,32]{0,1:T(8,128)} %param.51) | copy-start | bytes 393220
  (105 other events, 191.2 us)
Sparse Core Ops, SparseCore 0:
  11.5 67.6 all-gather.3
  82.7 57.5 all-gather.5
  143.7 55.4 all-gather.7
  397.0 18.8 all-reduce.6
  421.5 166.2 all-reduce.8
  594.0 107.0 reduce-scatter.2
  703.3 140.2 reduce-scatter.4
where the time goes:
time: 854 us; the launch traced here: 852 us
  waiting for transfers between devices  417 us (49%)
  matrix products  169 us (20%)
  blocking collectives  82.2 us (10%)
  other arithmetic  67.4 us (8%)
  local copies, waits for them, and re-layouts  60.6 us (7%)
  starting transfers between devices  37.2 us (4%)
  between operations  18.5 us (2%)
    reduce_scatter x1, waiting for transfers between devices, shards(): lax.psum_scatter(dense_total[2], ('dp', 'rep'), scatter_dimension=1, tile...  141 us
    reduce_scatter x1, waiting for transfers between devices, shards(): lax.psum_scatter(dense_total[1], ('dp', 'rep'), scatter_dimension=1, tile...  111 us
    unnamed x8, waiting for transfers between devices  97 us
    dot_general x36, matrix products, contract_rows(): lax.dot_general(left_side, right_side, (((0,), (0,)), ((), ())), preferre...  79 us
    all_gather x1, waiting for transfers between devices, shards(): lax.all_gather(shard_low[2], ('dp', 'rep'), axis=1, tiled=True)  48.3 us
    psum x1, blocking collectives, shards(): bias_total, loss_total = lax.psum((bias_total, loss_total), ('dp', 'rep'))  41.3 us
    unnamed x1, blocking collectives  40.9 us
    dot_general x12, matrix products, one_block(): jnp.dot(one_hot_rows(block_ids, table_piece.shape[0]), table_piece, prefe...  39.2 us
  transfers between devices with their start and end apart: 13, of which 7 were waited for; matrix products, arithmetic and copies ran while one was open for 20% of the time, Pallas kernels for 0%

commit v1 on v0

--- a/solution.py
+++ b/solution.py
@@ -1,8 +1,11 @@
+import functools
 import math
 
 import jax
 import jax.numpy as jnp
 from jax import lax
+from jax.experimental import pallas as pl
+from jax.experimental.pallas import tpu as pltpu
 from jax.sharding import PartitionSpec as P
 
 TABLES = 26
@@ -316,6 +319,418 @@
     )
 
 
+MESH = pl.DeviceIdType.MESH
+F32 = jnp.float32
+BF = jnp.bfloat16
+LN=1152; RB=112; ZN,YN,XN=4,2,2
+
+def k1_body(ids_ref, tab_ref, cr_ref, ti_ref, tm_ref, hd_ref, G, E, tabr, eout, ss, rs, ess, ers):
+    me=lax.axis_index("dp"); r=lax.axis_index("rep")
+    x=me%2; y=(me//2)%2; z=me//4
+    dev=lambda zz,yy,xx: zz*4+yy*2+xx
+    zp=[z+1-2*(z%2),(z+2)%4,3-z]
+    own=me*2+r
+    bar=pltpu.get_barrier_semaphore()
+    for i in range(1,16):
+        pl.semaphore_signal(bar,inc=1,device_id=((me+i)%16,r),device_id_type=MESH)
+    pl.semaphore_signal(bar,inc=1,device_id=(me,1-r),device_id_type=MESH)
+    G[own,0:48,0:1024]=cr_ref[:,0:1024].astype(BF)
+    G[own,0:48,1024:LN]=jnp.concatenate([cr_ref[:,1024:1027],jnp.zeros((48,125),F32)],axis=1).astype(BF)
+    G[own,48:80,0:1024]=ti_ref[:,0:1024].astype(BF)
+    G[own,48:80,1024:LN]=jnp.concatenate([ti_ref[:,1024:1027],jnp.zeros((32,125),F32)],axis=1).astype(BF)
+    G[own,80:112,0:1024]=tm_ref[...].astype(BF)
+    hcol=jnp.sum(jnp.where(lax.broadcasted_iota(jnp.int32,(32,32),0)==lax.broadcasted_iota(jnp.int32,(32,32),1),jnp.broadcast_to(hd_ref[...],(32,32)),0.0),axis=1,keepdims=True)
+    G[own,80:112,1024:LN]=jnp.broadcast_to(hcol,(32,128)).astype(BF)
+    pl.semaphore_wait(bar,16)
+    parts=((0,48),(48,64))
+    cnt=[0,0]; sends=[]
+    def mk(p,k,dst,si):
+        lo,n=parts[p]
+        return pltpu.make_async_remote_copy(src_ref=G.at[k,pl.ds(lo,n)],dst_ref=G.at[k,pl.ds(lo,n)],
+            send_sem=ss.at[p,si],recv_sem=rs.at[p,k],device_id=dst,device_id_type=MESH)
+    def send(p,k,dst):
+        c=mk(p,k,dst,cnt[p]); cnt[p]+=1; c.start(); sends.append(c)
+    def wait(p,k): mk(p,k,(me,1-r),0).wait_recv()
+    xpeer=(dev(z,y,1-x),r); ypeer=(dev(z,1-y,x),r); core=(me,1-r)
+    p1=(ypeer,xpeer); p2=(xpeer,ypeer)
+    key=lambda zz,yy,xx: dev(zz,yy,xx)*2+r
+    for p in (0,1):
+        send(p,own,p1[p]); send(p,own,p2[p])
+    for q in zp:
+        for p in (0,1): send(p,own,(dev(q,y,x),r))
+    for p in (0,1): send(p,own,core)
+    for s in range(2):
+        for j in range(32):
+            g,h=j//4,j%4
+            t=tab_ref[pl.ds(2*j+s,39,stride=64),:]
+            tabr[s,g*40:(g+1)*40,h*128:(h+1)*128]=jnp.concatenate([t,jnp.zeros((1,128),F32)],axis=0).astype(BF)
+    def look(i,_):
+        d=(me+i)%16
+        off=pl.multiple_of((d*2+r)*384,128)
+        idv=ids_ref[:,pl.ds(off,384)]
+        outs=[]
+        for s in range(2):
+            ids=idv[s:s+1]
+            lo=ids%512; hi=ids//512
+            oh=(lax.broadcasted_iota(jnp.int32,(512,384),0)==lo).astype(F32).astype(BF)
+            R=jnp.dot(tabr[s],oh,preferred_element_type=F32)
+            e=jnp.zeros((40,384),F32)
+            for g in range(8):
+                e=e+jnp.where(hi==g,R[g*40:(g+1)*40],0.0)
+            outs.append(e)
+        eout[d]=jnp.concatenate(outs,axis=0).astype(BF)
+        return 0
+    def ecopy(i):
+        d=(me+i)%16
+        return pltpu.make_async_remote_copy(src_ref=eout.at[d],dst_ref=E.at[me],send_sem=ess.at[d],recv_sem=ers.at[me],device_id=(d,r),device_id_type=MESH)
+    def step(i,_):
+        look(i,0)
+        ecopy(i).start()
+        return 0
+    lax.fori_loop(1,16,step,0)
+    look(0,0)
+    E[me]=eout[me]
+    for q in zp:
+        for p in (0,1):
+            k=key(q,y,x); wait(p,k)
+            send(p,k,p1[p]); send(p,k,p2[p]); send(p,k,core)
+    k1f=(lambda zz:key(zz,1-y,x), lambda zz:key(zz,y,1-x))
+    for q in [z]+zp:
+        for p in (0,1):
+            k=k1f[p](q); wait(p,k); send(p,k,p2[p]); send(p,k,core)
+    k2f=(lambda zz,o:key(zz,(y+o)%2,1-x), lambda zz,o:key(zz,1-y,(x+o)%2))
+    for q in [z]+zp:
+        for o in (0,1):
+            for p in (0,1):
+                k=k2f[p](q,o); wait(p,k); send(p,k,core)
+    def ew(i,_):
+        d=(me+i)%16
+        pltpu.make_async_remote_copy(src_ref=eout.at[d],dst_ref=E.at[d],send_sem=ess.at[d],recv_sem=ers.at[d],device_id=(d,r),device_id_type=MESH).wait()
+        return 0
+    lax.fori_loop(1,16,ew,0)
+    def cw(i,_):
+        for p in (0,1): wait(p,i*2+(1-r))
+        return 0
+    lax.fori_loop(0,16,cw,0)
+    for c in sends: c.wait_send()
+
+def k1(ids,tab,cr,ti,tm,hd):
+    vm=pl.BlockSpec(memory_space=pltpu.VMEM)
+    return pl.pallas_call(k1_body,name="k_one",
+        out_shape=(jax.ShapeDtypeStruct((32,RB,LN),BF),jax.ShapeDtypeStruct((16,80,384),BF)),
+        in_specs=[vm]*6,out_specs=(vm,vm),
+        scratch_shapes=[pltpu.VMEM((2,320,512),BF),pltpu.VMEM((16,80,384),BF),
+            pltpu.SemaphoreType.DMA((2,32)),pltpu.SemaphoreType.DMA((2,32)),pltpu.SemaphoreType.DMA((16,)),pltpu.SemaphoreType.DMA((16,))],
+        compiler_params=pltpu.CompilerParams(collective_id=0,has_side_effects=True,vmem_limit_bytes=48<<20))(ids,tab,cr,ti,tm,hd)
+
+def tab_view(t):
+    S,R,C=t.shape
+    return jnp.transpose(jnp.transpose(t,(2,0,1)).reshape(C,S,R//128,128),(0,2,1,3)).reshape(C*S*R//128,128)
+def tab_unview(v,S=2,R=4096,C=39):
+    return jnp.transpose(jnp.transpose(v.reshape(C,R//128,S,128),(0,2,1,3)).reshape(C,S,R),(1,2,0))
+CH=[(0,256),(256,256),(512,256),(768,256),(1024,128)]
+def nt(a,b): return lax.dot_general(a,b,(((1,),(1,)),((),())),preferred_element_type=F32)
+def nn(a,b): return lax.dot_general(a,b,(((1,),(0,)),((),())),preferred_element_type=F32)
+def tn(a,b): return lax.dot_general(a,b,(((0,),(0,)),((),())),preferred_element_type=F32)
+def sig(v): return 1.0/(1.0+jnp.exp(-v))
+def slope(v):
+    s=sig(v); return s*(1.0+v*(1.0-s))
+
+def k2_body(total, ts, G, E, dns, lab, bia, GA, GB, DE, M,
+            xT, x0, xr, xl, qc, pr, VT, UT, a1, a2, h1, h2, d1, d2, dx, d0, dql, dpr):
+    for t in range(26):
+        s=ts[t]
+        blk=E[s//2].astype(F32)
+        e=jnp.where(s%2==1,blk[40:80],blk[0:40])
+        xT[39*t:39*t+39,:]=e[0:39]
+    xT[1014:1027,:]=dns[...].astype(BF).astype(F32)
+    xT[1027:LN,:]=jnp.zeros((LN-1027,384),F32)
+    for i in range(9):
+        v=xT[128*i:128*i+128,:].T
+        x0[:,128*i:128*i+128]=v
+        xl[0,:,128*i:128*i+128]=v.astype(BF)
+    for l in range(3):
+        for lo,n in CH:
+            w=G[:,16*l:16*l+16,lo:lo+n].astype(F32).reshape(32,2,8,n)
+            VT[l,:,lo:lo+n]=w[:,0].reshape(256,n).astype(BF)
+            UT[l,:,lo:lo+n]=w[:,1].reshape(256,n).astype(BF)
+    for l in range(3):
+        pr[l]=nt(xl[l],VT[l]).astype(BF)
+        src=x0 if l==0 else xr
+        for lo,n in CH:
+            q=nn(pr[l],UT[l,:,lo:lo+n])+bia[l:l+1,lo:lo+n]
+            qc[l,:,lo:lo+n]=q
+            v=x0[:,lo:lo+n]*q+src[:,lo:lo+n]
+            if l<2: xr[:,lo:lo+n]=v
+            xl[l+1,:,lo:lo+n]=v.astype(BF)
+    for n in range(4):
+        c=slice(256*n,256*n+256)
+        a=nt(xl[3],G[8*n:8*n+8,48:80,:].reshape(256,LN))+bia[3:4,c]
+        a1[:,c]=a; h1[:,c]=(a*sig(a)).astype(BF)
+    for n in range(4):
+        c=slice(256*n,256*n+256)
+        a=nt(h1[...],G[8*n:8*n+8,80:112,0:1024].reshape(256,1024))+bia[4:5,c]
+        a2[:,c]=a; h2[:,c]=(a*sig(a)).astype(BF)
+    hc=G[:,80:112,1024:LN].reshape(1024,128)
+    z=nn(h2[...],hc)+bia[5:6,0:128]
+    y=jnp.broadcast_to(lab[...].astype(F32),(128,384)).T
+    lossv=jnp.maximum(z,0.0)+jnp.log1p(jnp.exp(-jnp.abs(z)))-y*z
+    dz=(sig(z)-y)/total
+    M[...]=jnp.zeros_like(M)
+    M[6:7,0:128]=jnp.sum(lossv,axis=0,keepdims=True)
+    M[7:8,0:128]=jnp.sum(dz,axis=0,keepdims=True)
+    hrow=hc.astype(F32).T[0:1]
+    for n in range(8):
+        c=slice(128*n,128*n+128)
+        M[5:6,c]=jnp.sum(dz*h2[:,c].astype(F32),axis=0,keepdims=True)
+        g=(dz*hrow[:,c]*slope(a2[:,c])).astype(BF)
+        d2[:,c]=g
+        M[4:5,c]=jnp.sum(g.astype(F32),axis=0,keepdims=True)
+    def put(ref,rows,base,nb,g):
+        for i in range(g.shape[0]//nb):
+            k=base+i; rep=k%2; d=k//2; zz,yy,xx=d//4,(d//2)%2,d%2
+            ref[rep,yy,xx,zz,rows:rows+nb,0:g.shape[1]]=g[i*nb:i*nb+nb].astype(BF)
+    for n in range(4):
+        put(GB,32,8*n,32,tn(d2[:,256*n:256*n+256],h1[...]))
+    GB[:,:,:,:,32:64,1024:LN]=jnp.zeros((2,2,2,4,32,LN-1024),BF)
+    for n in range(4):
+        c=slice(256*n,256*n+256)
+        g=(nn(d2[...],G[:,80:112,c].reshape(1024,256))*slope(a1[:,c])).astype(BF)
+        d1[:,c]=g
+        M[3:4,c]=jnp.sum(g.astype(F32),axis=0,keepdims=True)
+    for n in range(4):
+        put(GB,0,8*n,32,tn(d1[:,256*n:256*n+256],xl[3]))
+    for lo,n in CH:
+        dx[:,lo:lo+n]=nn(d1[...],G[:,48:80,lo:lo+n].reshape(1024,n))
+    for l in (2,1,0):
+        for lo,n in CH:
+            g=dx[:,lo:lo+n]; dq=g*x0[:,lo:lo+n]
+            M[l:l+1,lo:lo+n]=jnp.sum(dq,axis=0,keepdims=True)
+            dql[:,lo:lo+n]=dq.astype(BF)
+            e=g*qc[l,:,lo:lo+n]
+            d0[:,lo:lo+n]=e if l==2 else d0[:,lo:lo+n]+e
+        dpr[...]=nt(dql[...],UT[l]).astype(BF)
+        for lo,n in CH:
+            gu=tn(pr[l],dql[:,lo:lo+n]).reshape(32,8,n)
+            gv=tn(dpr[...],xl[l,:,lo:lo+n]).reshape(32,8,n)
+            gg=jnp.concatenate([gv,gu],axis=1).astype(BF)
+            for k in range(32):
+                rep=k%2; d=k//2; zz,yy,xx=d//4,(d//2)%2,d%2
+                GA[rep,xx,yy,zz,16*l:16*l+16,lo:lo+n]=gg[k]
+            v=dx[:,lo:lo+n]+nn(dpr[...],VT[l,:,lo:lo+n])
+            if l: dx[:,lo:lo+n]=v
+            else: d0[:,lo:lo+n]=d0[:,lo:lo+n]+v
+    for i in range(9):
+        xT[128*i:128*i+128,:]=d0[:,128*i:128*i+128].T
+    for t in range(26):
+        DE[t]=jnp.concatenate([xT[39*t:39*t+39,:],jnp.zeros((1,384),F32)],axis=0)
+    DE[26]=jnp.zeros((40,384),F32)
+
+def k2(total,ts,G,E,dns,lab,bia):
+    vm=pl.BlockSpec(memory_space=pltpu.VMEM)
+    V=pltpu.VMEM
+    return pl.pallas_call(functools.partial(k2_body,total),name="k_two",
+        out_shape=(jax.ShapeDtypeStruct((2,2,2,4,48,LN),BF),jax.ShapeDtypeStruct((2,2,2,4,64,LN),BF),jax.ShapeDtypeStruct((27,40,384),F32),jax.ShapeDtypeStruct((8,LN),F32)),
+        in_specs=[pl.BlockSpec(memory_space=pltpu.SMEM)]+[vm]*5,out_specs=(vm,)*4,
+        scratch_shapes=[V((LN,384),F32),V((384,LN),F32),V((384,LN),F32),V((4,384,LN),BF),V((3,384,LN),F32),V((3,384,256),BF),
+          V((3,256,LN),BF),V((3,256,LN),BF),V((384,1024),F32),V((384,1024),F32),V((384,1024),BF),V((384,1024),BF),V((384,1024),BF),V((384,1024),BF),
+          V((384,LN),F32),V((384,LN),F32),V((384,LN),BF),V((384,256),BF)],
+        compiler_params=pltpu.CompilerParams(vmem_limit_bytes=60<<20))(ts,G,E,dns,lab,bia)
+B1=0.5; C5=1-0.5**5; EPS=1e-10
+def adamw(w,m,v,g,rate):
+    mn=0.5*m+0.5*g
+    vn=0.5*v+0.5*g*g
+    return w-rate*((mn/C5)/(jnp.sqrt(vn/C5)+EPS)+0.01*w),mn,vn
+
+def k3_body(inv, rc, ids_ref, GA, GB, DE, M, tw, tm_, tv, crw,crm,crv, tiw,tim,tiv, tmw,tmm,tmv,
+        ow,om,ov,ol, cow,com,cov,col, iow,iom,iov,iol, mow,mom,mov,mol, MO,
+        eout, D, R, gt, gtc, CA, CB, SA, SB, KA, KB, RA, RB_, SA2, SB2, RA2, RB2, KA2,KB2, SA3,SB3, RA3,RB3, MC, MS, MX, MZ,
+        ss, rs, ess, ers):
+    me=lax.axis_index("dp"); r=lax.axis_index("rep")
+    x=me%2; y=(me//2)%2; z=me//4
+    dev=lambda zz,yy,xx: zz*4+yy*2+xx
+    zp=[z+1-2*(z%2),(z+2)%4,3-z]
+    bar=pltpu.get_barrier_semaphore()
+    for i in range(1,16):
+        pl.semaphore_signal(bar,inc=1,device_id=((me+i)%16,r),device_id_type=MESH)
+    pl.semaphore_signal(bar,inc=1,device_id=(me,1-r),device_id_type=MESH)
+    pl.semaphore_wait(bar,16)
+    xpeer=(dev(z,y,1-x),r); ypeer=(dev(z,1-y,x),r); core=(me,1-r)
+    sends=[]
+    def cp(src,dst,i,dev_):
+        return pltpu.make_async_remote_copy(src_ref=src,dst_ref=dst,send_sem=ss.at[i],recv_sem=rs.at[i],device_id=dev_,device_id_type=MESH)
+    def go(src,dst,i,dev_):
+        c=cp(src,dst,i,dev_); c.start(); sends.append(c); return c
+    cB=go(GB.at[1-r],CB,0,core)
+    cA=go(GA.at[1-r],CA,1,core)
+    cM=go(M,MC,2,core)
+    def blk(d):
+        return jnp.concatenate([DE[inv[2*d]],DE[inv[2*d+1]]],axis=0).astype(BF)
+    def ec(d,land):
+        return pltpu.make_async_remote_copy(src_ref=eout.at[d],dst_ref=D.at[land],send_sem=ess.at[d],recv_sem=ers.at[land],device_id=(d,r),device_id_type=MESH)
+    def estep(i,_):
+        d=(me+i)%16
+        eout[d]=blk(d)
+        ec(d,me).start()
+        return 0
+    lax.fori_loop(1,16,estep,0)
+    D[me]=blk(me)
+    cB.wait_recv()
+    SB[...]=(GB[r,1-y].astype(F32)+CB[1-y].astype(F32)).astype(BF)
+    b1=go(SB,RB_,3,ypeer)
+    cA.wait_recv()
+    SA[...]=(GA[r,1-x].astype(F32)+CA[1-x].astype(F32)).astype(BF)
+    a1=go(SA,RA,4,xpeer)
+    cM.wait_recv()
+    MS[...]=M[...]+MC[...]
+    m1=go(MS,MX.at[0],5,xpeer)
+    KB[...]=GB[r,y].astype(F32)+CB[y].astype(F32)
+    KA[...]=GA[r,x].astype(F32)+CA[x].astype(F32)
+    m1.wait_recv()
+    MZ[0]=MS[...]+MX[0]
+    m2=go(MZ.at[0],MX.at[1],6,ypeer)
+    m2.wait_recv()
+    MX[2]=MZ[0]+MX[1]
+    ms=[]
+    for i,q in enumerate(zp):
+        ms.append(go(MX.at[2],MX.at[3+i],7+i,(dev(q,y,x),r)))
+    def onehot_parts(i,s):
+        d=(me+i)%16
+        ids=ids_ref[:,pl.ds(pl.multiple_of((d*2+r)*384,128),384)][s:s+1]
+        lo=ids%512; hi=ids//512
+        oh=(lax.broadcasted_iota(jnp.int32,(512,384),0)==lo).astype(F32).astype(BF)
+        e=D[d].astype(F32)[40*s:40*s+40]
+        lhs=jnp.concatenate([jnp.where(hi==g,e,0.0) for g in range(8)],axis=0).astype(BF)
+        return lhs,oh
+    R[...]=jnp.zeros_like(R)
+    def acc(i2,_):
+        for j in range(2):
+            i=2*i2+j
+            d=(me+i)%16
+            @pl.when(i>0)
+            def _(): ec(d,d).wait_recv()
+        for s in range(2):
+            p0=onehot_parts(2*i2,s); p1=onehot_parts(2*i2+1,s)
+            R[s]+=nt(jnp.concatenate([p0[0],p1[0]],axis=1),jnp.concatenate([p0[1],p1[1]],axis=1))
+        return 0
+    lax.fori_loop(0,8,acc,0)
+    for s in range(2):
+        for j in range(32):
+            g,h=j//4,j%4
+            gt[pl.ds(2*j+s,39,stride=64),:]=R[s,g*40:g*40+39,h*128:(h+1)*128]
+    cG=go(gt,gtc,10,core)
+    b1.wait_recv()
+    SB2[...]=(KB[1-x]+RB_[1-x].astype(F32)).astype(BF)
+    b2=go(SB2,RB2,11,xpeer)
+    KB2[...]=KB[x]+RB_[x].astype(F32)
+    a1.wait_recv()
+    SA2[...]=(KA[1-y]+RA[1-y].astype(F32)).astype(BF)
+    a2=go(SA2,RA2,12,ypeer)
+    KA2[...]=KA[y]+RA[y].astype(F32)
+    cG.wait_recv()
+    rowsel=lax.broadcasted_iota(jnp.int32,(64,128),0)
+    lane=lax.broadcasted_iota(jnp.int32,(64,128),1)
+    use=((rowsel//2)*128+lane)<jnp.where(rowsel%2==0,rc[0],rc[1])
+    def tab(c,_):
+        q=pl.ds(pl.multiple_of(c*64,64),64)
+        w=tw[q,:]; m=tm_[q,:]; v=tv[q,:]; g=gt[q,:]+gtc[q,:]
+        nw,nm,nv=adamw(w,m,v,g,0.2)
+        nw=jnp.where(use,nw,w)
+        ow[q,:]=nw; om[q,:]=jnp.where(use,nm,m); ov[q,:]=jnp.where(use,nv,v); ol[q,:]=nw.astype(BF)
+        return 0
+    lax.fori_loop(0,39,tab,0)
+    b2.wait_recv()
+    SB3[...]=(KB2[...]+RB2[...].astype(F32)).astype(BF)
+    bz=[go(SB3.at[q],RB3.at[i],13+i,(dev(q,y,x),r)) for i,q in enumerate(zp)]
+    a2.wait_recv()
+    SA3[...]=(KA2[...]+RA2[...].astype(F32)).astype(BF)
+    az=[go(SA3.at[q],RA3.at[i],16+i,(dev(q,y,x),r)) for i,q in enumerate(zp)]
+    for c in ms: c.wait_recv()
+    pos=[MX[2],MX[3],MX[4],MX[5]]
+    zb=z%2; zh=z//2
+    e0=jnp.where(zb==0,pos[0],pos[1]); e1=jnp.where(zb==0,pos[1],pos[0])
+    f0=jnp.where(zb==0,pos[2],pos[3]); f1=jnp.where(zb==0,pos[3],pos[2])
+    lo_=e0+e1; hi_=f0+f1
+    MO[...]=jnp.where(zh==0,lo_,hi_)+jnp.where(zh==0,hi_,lo_)
+    for c in bz: c.wait_recv()
+    gB=KB2[z]+RB2[z].astype(F32)+(RB3[0].astype(F32)+RB3[1].astype(F32)+RB3[2].astype(F32))
+    g=gB[0:32,0:1027]
+    w,m,v=adamw(tiw[...],tim[...],tiv[...],g,0.01)
+    iow[...]=w; iom[...]=m; iov[...]=v; iol[...]=w.astype(BF)
+    g=gB[32:64,0:1024]
+    w,m,v=adamw(tmw[...],tmm[...],tmv[...],g,0.01)
+    mow[...]=w; mom[...]=m; mov[...]=v; mol[...]=w.astype(BF)
+    for c in az: c.wait_recv()
+    g=(KA2[z]+RA2[z].astype(F32)+(RA3[0].astype(F32)+RA3[1].astype(F32)+RA3[2].astype(F32)))[:,0:1027]
+    w,m,v=adamw(crw[...],crm[...],crv[...],g,0.01)
+    cow[...]=w; com[...]=m; cov[...]=v; col[...]=w.astype(BF)
+    def ew(i,_):
+        d=(me+i)%16
+        ec(d,d).wait_send()
+        return 0
+    lax.fori_loop(1,16,ew,0)
+    for c in sends: c.wait_send()
+
+def k3(inv,rc,ids,GA,GB,DE,M,tabs,crs,tis,tms):
+    vm=pl.BlockSpec(memory_space=pltpu.VMEM); sm=pl.BlockSpec(memory_space=pltpu.SMEM)
+    V=pltpu.VMEM; S=jax.ShapeDtypeStruct
+    quad=lambda a:[S(a.shape,F32)]*3+[S(a.shape,BF)]
+    outs=quad(tabs[0])+quad(crs[0])+quad(tis[0])+quad(tms[0])+[S((8,LN),F32)]
+    return pl.pallas_call(k3_body,name="k_three",out_shape=tuple(outs),
+        in_specs=[sm,sm]+[vm]*17,out_specs=(vm,)*len(outs),
+        scratch_shapes=[V((16,80,384),BF),V((16,80,384),BF),V((2,320,512),F32),V((2496,128),F32),V((2496,128),F32),
+          V((2,2,4,48,LN),BF),V((2,2,4,64,LN),BF), V((2,4,48,LN),BF),V((2,4,64,LN),BF), V((2,4,48,LN),F32),V((2,4,64,LN),F32),
+          V((2,4,48,LN),BF),V((2,4,64,LN),BF), V((4,48,LN),BF),V((4,64,LN),BF),V((4,48,LN),BF),V((4,64,LN),BF),
+          V((4,48,LN),F32),V((4,64,LN),F32), V((4,48,LN),BF),V((4,64,LN),BF),V((3,48,LN),BF),V((3,64,LN),BF),
+          V((8,LN),F32),V((8,LN),F32),V((6,8,LN),F32),V((1,8,LN),F32),
+          pltpu.SemaphoreType.DMA((20,)),pltpu.SemaphoreType.DMA((20,)),pltpu.SemaphoreType.DMA((16,)),pltpu.SemaphoreType.DMA((16,))],
+        compiler_params=pltpu.CompilerParams(collective_id=1,has_side_effects=True,vmem_limit_bytes=60<<20))(
+        inv,rc,ids,GA,GB,DE,M,*tabs,*crs,*tis,*tms)
+
+def fast_shards(
+    event_ids, row_counts, table_slot, dense_input, labels,
+    tables, tables_m, tables_v, cross_uv, cross_m, cross_v,
+    tower_in, tower_in_m, tower_in_v, tower_mid, tower_mid_m, tower_mid_v,
+    head_weight, head_m, head_v, biases, biases_m, biases_v,
+):
+    total = float(labels.shape[0] * lax.axis_size("dp") * lax.axis_size("rep"))
+    turn = lambda a: jnp.transpose(a, (0, 1, 3, 2)).reshape(48, WIDTH)
+    back = lambda a: jnp.transpose(a.reshape(LAYERS, 2, 8, WIDTH), (0, 1, 3, 2))
+    tabs = [tab_view(a) for a in (tables, tables_m, tables_v)]
+    crs = [turn(a) for a in (cross_uv, cross_m, cross_v)]
+    tis = [a.T for a in (tower_in, tower_in_m, tower_in_v)]
+    tms = [a.T for a in (tower_mid, tower_mid_m, tower_mid_v)]
+    hits = (table_slot[None, :] == jnp.arange(32, dtype=jnp.int32)[:, None])
+    inv = TABLES - jnp.sum(hits * (TABLES - jnp.arange(TABLES, dtype=jnp.int32))[None, :], axis=1)
+    wide = lambda v: jnp.pad(v, (0, LN - v.shape[0]))
+    at = LAYERS * WIDTH
+    bia = jnp.stack(
+        [wide(biases[WIDTH * i : WIDTH * i + WIDTH]) for i in range(3)]
+        + [wide(biases[at : at + 1024]), wide(biases[at + 1024 : at + 2048]),
+           jnp.broadcast_to(biases[at + 2048], (LN,)), jnp.zeros((LN,), F32), jnp.zeros((LN,), F32)]
+    )
+    G, E = k1(event_ids, tabs[0], crs[0], tis[0], tms[0], head_weight.reshape(1, 32))
+    GA, GB, DE, M = k2(total, table_slot, G, E, dense_input.T, labels.reshape(1, 384), bia)
+    o = k3(inv, row_counts, event_ids, GA, GB, DE, M, tabs, crs, tis, tms)
+    MO = o[16]
+    loss = MO[6, 0]
+    g_bias = jnp.concatenate([MO[0, :WIDTH], MO[1, :WIDTH], MO[2, :WIDTH], MO[3, :1024], MO[4, :1024], MO[7, :1]])
+    k = lax.axis_index("dp") * 2 + lax.axis_index("rep")
+    g_head = lax.dynamic_slice(MO[5], (k * 32,), (32,))
+    tail = []
+    for w, m, v, g, rate in ((head_weight, head_m, head_v, g_head, RATE_DENSE), (biases, biases_m, biases_v, g_bias, RATE_BIAS)):
+        a, b, c = adamw_update(w, m, v, g, rate)
+        tail += [a, b, c, a.astype(BF)]
+    return (
+        loss,
+        *[tab_unview(a) for a in o[0:4]],
+        *[back(a) for a in o[4:8]],
+        *[a.T for a in o[8:12]],
+        *[a.T for a in o[12:16]],
+        *tail,
+    )
+
+
 def solution(mesh):
     placed = (
         P("dp", None),
@@ -342,8 +757,9 @@
         P(),
         P(),
     )
+    fits = mesh.shape["dp"] == 16 and mesh.shape["rep"] == 2
     return jax.shard_map(
-        shards,
+        fast_shards if fits else shards,
         mesh=mesh,
         in_specs=placed,
         out_specs=(

time: 854 us -> 213 us (0.25)
  waiting for transfers between devices: 417 us -> 0 us
  Pallas kernels: 0 us -> 180 us
  matrix products: 169 us -> 0 us
  blocking collectives: 82.2 us -> 0 us
  other arithmetic: 67.4 us -> 1.9 us
  starting transfers between devices: 37.2 us -> 0 us
  local copies, waits for them, and re-layouts: 60.6 us -> 28.4 us
  between operations: 18.5 us -> 0.87 us
    reduce_scatter x2 -> x0, waiting for transfers between devices: 252 us -> none  [the longest x1 141 us: shards(): lax.psum_scatter(dense_total[2], ('dp', 'rep'), scatter_dimension=1, tile...]
    pallas_call x0 -> x3, Pallas kernels: none -> 180 us  [the longest x1 98.6 us: k3(): pl.pallas_call(k3_body, name='k_three', out_shape=tuple(outs), in_specs=[...]
    dot_general x108 -> x0, matrix products: 169 us -> none  [the longest x36 79 us: contract_rows(): lax.dot_general(left_side, right_side, (((0,), (0,)), ((), ())), preferre...]
    unnamed x8 -> x0, waiting for transfers between devices: 97 us -> none
    all_gather x3 -> x0, waiting for transfers between devices: 48.3 us -> none  [the longest x1 48.3 us: shards(): lax.all_gather(shard_low[2], ('dp', 'rep'), axis=1, tiled=True)]
    psum x1 -> x0, blocking collectives: 41.3 us -> none  [shards(): bias_total, loss_total = lax.psum((bias_total, loss_total), ('dp', 'rep'))]
    unnamed x1 -> x0, blocking collectives: 40.9 us -> none
    all_to_all x6 -> x0, starting transfers between devices: 36.9 us -> none  [the longest x3 20.8 us: shards(): lax.all_to_all(outgoing, 'dp', split_axis=0, concat_axis=0, tiled=True)]
  transfers between devices with their start and end apart: 13 -> 0, of which waited for: 7 -> 0; matrix products, arithmetic and copies ran while one was open for 20% -> 0% of each run, Pallas kernels for 0% -> 0%
where the time goes in v1:
time: 213 us; the launch traced here: 212 us
  Pallas kernels  180 us (85%)
  local copies, waits for them, and re-layouts  28.4 us (13%)
    pallas_call x1, Pallas kernels, k3(): pl.pallas_call(k3_body, name='k_three', out_shape=tuple(outs), in_specs=[...  98.6 us
    pallas_call x1, Pallas kernels, k1(): pl.pallas_call(k1_body, name='k_one', out_shape=(jax.ShapeDtypeStruct((32...  61 us
    unnamed x78, local copies, waits for them, and re-layouts  21.2 us
    pallas_call x1, Pallas kernels, k2(): pl.pallas_call(functools.partial(k2_body, total), name='k_two', out_shape...  20.8 us

profile of v1, /device:TPU:0, one launch (start us, length us, event | category | flops | bytes accessed | tf_op | source)
XLA Modules:
  0.0 211.6 jit_solution(2109801848369571355)
XLA Ops:
  0.7 0.0 copy-start.26
  0.7 0.0 copy-start.27
  0.7 0.0 copy-start
  0.7 1.3 copy-done
  2.0 0.9 copy-done.2
  2.9 0.9 copy-done.3
  3.9 0.9 copy-done.4
  4.8 0.9 copy-done.5
  5.7 0.7 copy-done.6
  6.3 61.0 %k_one.1 = (bf16[32,112,1152]{2,1,0:T(8,128)(2,1)}, bf16[16,80,384]{2,1,0:T(8,128)(2,1)S(1)}) custom-call(s32[2,12288]{1,0:T(2,128)S(1)} %copy-done.5, f32[2496,128]{1,0:T(8,128)S(1)} %bitcast.97, f32[48,1027]{1,0:T(8,128)S(1)} %bitcast.99, f32[32,1027]{1,0:T(8,128)S(1)} %bitcast.101, f32[32,1024]{1,0:T(8,128)S(1)} %bitcast.103, f32[1,32]{1,0:T(1,128)S(1)} %bitcast.104), custom_call_target="tpu_custom_call" | custom-call | tf_op jit(solution)/shard_map/k_one/pallas_call | solution.py:419
  67.3 0.0 copy-start.1
  67.4 0.9 copy-done.1
  68.3 0.0 copy-done.17
  68.3 0.1 fusion.9
  68.4 0.1 fusion.8
  68.5 0.0 copy-done.26
  68.5 0.6 slice.48
  69.1 0.6 stack_broadcast_in_dim.3
  69.8 0.7 stack.27.bia
  70.5 0.0 copy-done.27
  70.5 0.6 reshape.129.lab
  71.0 20.8 %k_two.1 = (bf16[2,2,2,4,48,1152]{5,4,3,2,1,0:T(8,128)(2,1)}, bf16[2,2,2,4,64,1152]{5,4,3,2,1,0:T(8,128)(2,1)}, f32[27,40,384]{2,1,0:T(8,128)}, f32[8,1152]{1,0:T(8,128)}) custom-call(s32[26]{0:T(128)} %ts.1, bf16[32,112,1152]{2,1,0:T(8,128)(2,1)} %get-tuple-element.48.G, bf16[16,80,384]{2,1,0:T(8,128)(2,1)} %copy-done.1, f32[13,384]{1,0:T(8,128)} %bitcast.129, ...), custom_call_target="tpu_custom_call" | custom-call | tf_op jit(solution)/shard_map/k_two/pallas_call | solution.py:532
  91.8 0.0 copy-done.28
  91.8 0.1 select_reduce_fusion
  91.9 0.5 broadcast_subtract_fusion.inv
  92.4 0.0 copy-start.30
  92.5 98.6 %k_three.1 = (f32[2496,128]{1,0:T(8,128)}, f32[2496,128]{1,0:T(8,128)}, f32[2496,128]{1,0:T(8,128)}, bf16[2496,128]{1,0:T(8,128)(2,1)}, f32[48,1027]{1,0:T(8,128...) custom-call(s32[32]{0:T(128)} %broadcast_subtract_fusion.inv, ...), custom_call_target="tpu_custom_call" | custom-call | tf_op jit(solution)/shard_map/k_three/pallas_call | solution.py:679
  191.1 0.9 slice_reduce_fusion
  192.0 0.8 fusion.7
  192.8 1.3 fusion.6
  194.1 0.7 concatenate.3
  194.8 0.0 copy-done.24
  194.8 0.0 copy-done.25
  194.8 0.6 fusion.2
  195.5 0.8 slice.50
  196.3 0.0 copy-done.7
  196.3 0.0 copy-done.29
  196.3 0.0 copy-done.30
  196.3 0.6 fusion.4
  196.9 2.6 %copy.70 = f32[2,4096,39]{1,0,2:T(2,128)} copy(f32[2,4096,39]{1,0,2:T(2,128)} %bitcast.109) | data formatting | bytes 2555904
  199.5 0.0 copy-done.9
  199.5 1.0 copy.71
  200.5 0.7 copy-done.8
  201.3 1.0 copy.72
  202.3 0.5 copy-done.10
  202.8 0.0 copy-start.15
  202.8 0.8 copy.73
  203.6 0.0 copy-done.13
  203.6 0.7 copy.74
  204.3 0.0 copy-done.12
  204.3 0.7 copy.75
  205.0 0.0 copy-done.11
  205.0 0.7 copy.76
  205.7 0.0 copy-done.21
  205.7 0.6 copy.77
  206.4 0.0 copy-done.16
  206.4 0.7 copy.78
  207.0 0.7 copy.79
  207.7 0.7 copy.80
  208.3 0.6 copy.81
  209.0 0.7 copy.82
  209.6 0.7 copy.83
  210.3 0.7 copy.84
  211.0 0.6 copy.85
  (44 shorter events, 0.1 us)
Async XLA Ops:
  0.7 67.8 %copy-start.26 = (pred[1152]{0:T(1024)(128)(4,1)S(1)}, pred[1152]{0:T(1024)(128)(4,1)}, u32[]{:S(2)}) copy-start(pred[1152]{0:T(1024)(128)(4,1)} %constant.16.clone.1) | copy-start | bytes 3460
  0.7 69.8 %copy-start.27 = (s32[384]{0:T(512)S(1)}, s32[384]{0:T(512)}, u32[]{:S(2)}) copy-start(s32[384]{0:T(512)} %param.27) | copy-start | bytes 4612
  0.7 1.3 copy-start
  2.0 0.9 copy-start.2
  2.9 0.9 copy-start.3
  3.9 0.9 copy-start.4
  4.8 0.9 copy-start.5
  5.7 0.7 copy-start.6
  6.3 62.0 %copy-start.17 = (f32[5130]{0:T(1024)S(1)}, f32[5130]{0:T(1024)}, u32[]{:S(2)}) copy-start(f32[5130]{0:T(1024)} %param.43) | copy-start | bytes 61564
  67.3 0.9 copy-start.1
  71.0 20.8 %copy-start.28 = (s32[26]{0:T(128)S(1)}, s32[26]{0:T(128)}, u32[]{:S(2)}) copy-start(s32[26]{0:T(128)} %ts.1) | copy-start | bytes 316
  92.4 102.4 %copy-start.24 = (f32[5130]{0:T(1024)S(1)}, f32[5130]{0:T(1024)}, u32[]{:S(2)}) copy-start(f32[5130]{0:T(1024)} %param.44) | copy-start | bytes 61564
  92.4 102.4 %copy-start.25 = (f32[5130]{0:T(1024)S(1)}, f32[5130]{0:T(1024)}, u32[]{:S(2)}) copy-start(f32[5130]{0:T(1024)} %param.45) | copy-start | bytes 61564
  92.4 103.8 %copy-start.7 = (f32[32]{0:T(128)S(1)}, f32[32]{0:T(128)}, u32[]{:S(2)}) copy-start(f32[32]{0:T(128)} %param.40) | copy-start | bytes 388
  92.4 103.8 %copy-start.29 = (f32[32]{0:T(128)S(1)}, f32[32]{0:T(128)}, u32[]{:S(2)}) copy-start(f32[32]{0:T(128)} %param.41) | copy-start | bytes 388
  92.4 103.8 %copy-start.30 = (f32[32]{0:T(128)S(1)}, f32[32]{0:T(128)}, u32[]{:S(2)}) copy-start(f32[32]{0:T(128)} %param.42) | copy-start | bytes 388
  196.9 2.6 %copy-start.9 = (f32[2496,128]{1,0:T(8,128)S(1)}, f32[2496,128]{1,0:T(8,128)}, u32[]{:S(2)}) copy-start(f32[2496,128]{1,0:T(8,128)} %get-tuple-element.56) | copy-start | bytes 3833860
  199.5 1.8 copy-start.8
  201.3 1.5 copy-start.10
  201.3 2.4 %copy-start.13 = (f32[48,1027]{1,0:T(8,128)S(1)}, f32[48,1027]{1,0:T(8,128)}, u32[]{:S(2)}) copy-start(f32[48,1027]{1,0:T(8,128)} %get-tuple-element.59) | copy-start | bytes 591556
  202.8 1.6 copy-start.12
  202.8 2.2 %copy-start.11 = (f32[48,1027]{1,0:T(8,128)S(1)}, f32[48,1027]{1,0:T(8,128)}, u32[]{:S(2)}) copy-start(f32[48,1027]{1,0:T(8,128)} %get-tuple-element.61) | copy-start | bytes 591556
  202.8 2.9 %copy-start.21 = (bf16[48,1027]{1,0:T(8,128)(2,1)S(1)}, bf16[48,1027]{1,0:T(8,128)(2,1)}, u32[]{:S(2)}) copy-start(bf16[48,1027]{1,0:T(8,128)(2,1)} %get-tuple-element.62) | copy-start | bytes 295780
  202.8 3.6 %copy-start.16 = (f32[32,1027]{1,0:T(8,128)S(1)}, f32[32,1027]{1,0:T(8,128)}, u32[]{:S(2)}) copy-start(f32[32,1027]{1,0:T(8,128)} %get-tuple-element.63) | copy-start | bytes 394372
  202.8 4.2 %copy-start.15 = (f32[32,1027]{1,0:T(8,128)S(1)}, f32[32,1027]{1,0:T(8,128)}, u32[]{:S(2)}) copy-start(f32[32,1027]{1,0:T(8,128)} %get-tuple-element.64) | copy-start | bytes 394372
  203.6 4.1 %copy-start.14 = (f32[32,1027]{1,0:T(8,128)S(1)}, f32[32,1027]{1,0:T(8,128)}, u32[]{:S(2)}) copy-start(f32[32,1027]{1,0:T(8,128)} %get-tuple-element.65) | copy-start | bytes 394372
  203.6 4.7 %copy-start.22 = (bf16[32,1027]{1,0:T(8,128)(2,1)S(1)}, bf16[32,1027]{1,0:T(8,128)(2,1)}, u32[]{:S(2)}) copy-start(bf16[32,1027]{1,0:T(8,128)(2,1)} %get-tuple-element.66) | copy-start | bytes 197188
  203.6 5.4 %copy-start.20 = (f32[32,1024]{1,0:T(8,128)S(1)}, f32[32,1024]{1,0:T(8,128)}, u32[]{:S(2)}) copy-start(f32[32,1024]{1,0:T(8,128)} %get-tuple-element.67) | copy-start | bytes 393220
  204.3 5.3 %copy-start.19 = (f32[32,1024]{1,0:T(8,128)S(1)}, f32[32,1024]{1,0:T(8,128)}, u32[]{:S(2)}) copy-start(f32[32,1024]{1,0:T(8,128)} %get-tuple-element.68) | copy-start | bytes 393220
  204.3 6.0 %copy-start.18 = (f32[32,1024]{1,0:T(8,128)S(1)}, f32[32,1024]{1,0:T(8,128)}, u32[]{:S(2)}) copy-start(f32[32,1024]{1,0:T(8,128)} %get-tuple-element.69) | copy-start | bytes 393220
  205.0 5.9 %copy-start.23 = (bf16[32,1024]{1,0:T(8,128)(2,1)S(1)}, bf16[32,1024]{1,0:T(8,128)(2,1)}, u32[]{:S(2)}) copy-start(bf16[32,1024]{1,0:T(8,128)(2,1)} %get-tuple-element.70) | copy-start | bytes 196612

commit v2 on v0

--- a/solution.py
+++ b/solution.py
@@ -1,8 +1,11 @@
+import functools
 import math
 
 import jax
 import jax.numpy as jnp
 from jax import lax
+from jax.experimental import pallas as pl
+from jax.experimental.pallas import tpu as pltpu
 from jax.sharding import PartitionSpec as P
 
 TABLES = 26
@@ -316,6 +319,661 @@
     )
 
 
+MESH = pl.DeviceIdType.MESH
+F32 = jnp.float32
+BF = jnp.bfloat16
+LN = 1152
+RB = 112
+CH = [(0, 256), (256, 256), (512, 256), (768, 256), (1024, 128)]
+ITEMS = {"m": (32, 1024, True), "i": (32, LN, False), "c2": (16, LN, True), "c1": (16, LN, False), "c0": (16, LN, True)}
+ORDER = ["m", "i", "c2", "c1", "c0"]
+
+
+def nt(a, b):
+    return lax.dot_general(a, b, (((1,), (1,)), ((), ())), preferred_element_type=F32)
+
+
+def nn(a, b):
+    return lax.dot_general(a, b, (((1,), (0,)), ((), ())), preferred_element_type=F32)
+
+
+def tn(a, b):
+    return lax.dot_general(a, b, (((0,), (0,)), ((), ())), preferred_element_type=F32)
+
+
+def sig(v):
+    return 1.0 / (1.0 + jnp.exp(-v))
+
+
+def slope(v):
+    s = sig(v)
+    return s * (1.0 + v * (1.0 - s))
+
+
+def place(k):
+    rep, d = k % 2, k // 2
+    return rep, d % 2, (d // 2) % 2, d // 4
+
+
+def mega_body(total, names_in, names_out, names_scr, *refs):
+    it = iter(refs)
+    R_ = {n: next(it) for n in names_in + names_out + names_scr}
+    ts, inv = R_["ts"], R_["inv"]
+    G, E, D, eout, tabr = R_["G"], R_["E"], R_["D"], R_["eout"], R_["tabr"]
+    xT, dx, xl, qc, pr = R_["xT"], R_["dx"], R_["xl"], R_["qc"], R_["pr"]
+    VT, UT, a1, a2, h1, h2 = R_["VT"], R_["UT"], R_["a1"], R_["a2"], R_["h1"], R_["h2"]
+    d0, dql, dpr, DE, M, R = R_["d0"], R_["dql"], R_["dpr"], R_["DE"], R_["M"], R_["R"]
+    ids_ref, tab_ref, bia = R_["ids_v"], R_["tab_v"], R_["bia"]
+    xr, d1, d2 = dx, h1, h2
+    gt, gtc, MO = R_["gt"], R_["gtc"], R_["MO"]
+    me = lax.axis_index("dp")
+    r = lax.axis_index("rep")
+    x, y, z = me % 2, (me // 2) % 2, me // 4
+    dev = lambda zz, yy, xx: zz * 4 + yy * 2 + xx
+    zp = [z + 1 - 2 * (z % 2), (z + 2) % 4, 3 - z]
+    own = me * 2 + r
+    xpeer, ypeer, core = (dev(z, y, 1 - x), r), (dev(z, 1 - y, x), r), (me, 1 - r)
+    zpeer = [(dev(q, y, x), r) for q in zp]
+
+    loads = {}
+    for i, n in enumerate(["cr", "ti", "tm", "hd", "tab", "ids", "dns", "lab"]):
+        c = pltpu.make_async_copy(R_[n], R_[n + "_v"], R_["lsem"].at[i])
+        c.start()
+        loads[n] = c
+    bar = pltpu.get_barrier_semaphore()
+    for i in range(1, 16):
+        pl.semaphore_signal(bar, inc=1, device_id=((me + i) % 16, r), device_id_type=MESH)
+    pl.semaphore_signal(bar, inc=1, device_id=core, device_id_type=MESH)
+
+    cr, ti, tm, hd = R_["cr_v"], R_["ti_v"], R_["tm_v"], R_["hd_v"]
+    for n in ("cr", "ti", "tm", "hd"):
+        loads[n].wait()
+    G[own, 0:48, 0:1024] = cr[:, 0:1024].astype(BF)
+    G[own, 0:48, 1024:LN] = jnp.concatenate([cr[:, 1024:1027], jnp.zeros((48, 125), F32)], axis=1).astype(BF)
+    G[own, 48:80, 0:1024] = ti[:, 0:1024].astype(BF)
+    G[own, 48:80, 1024:LN] = jnp.concatenate([ti[:, 1024:1027], jnp.zeros((32, 125), F32)], axis=1).astype(BF)
+    G[own, 80:112, 0:1024] = tm[...].astype(BF)
+    eye = lax.broadcasted_iota(jnp.int32, (32, 32), 0) == lax.broadcasted_iota(jnp.int32, (32, 32), 1)
+    hcol = jnp.sum(jnp.where(eye, jnp.broadcast_to(hd[...], (32, 32)), 0.0), axis=1, keepdims=True)
+    G[own, 80:112, 1024:LN] = jnp.broadcast_to(hcol, (32, 128)).astype(BF)
+    pl.semaphore_wait(bar, 16)
+
+    parts = ((0, 48), (48, 64))
+    cnt = [0, 0]
+    sends = []
+
+    def wcopy(p, k, dst, si):
+        lo, n = parts[p]
+        return pltpu.make_async_remote_copy(
+            src_ref=G.at[k, pl.ds(lo, n)], dst_ref=G.at[k, pl.ds(lo, n)],
+            send_sem=R_["wss"].at[p, si], recv_sem=R_["wrs"].at[p, k], device_id=dst, device_id_type=MESH)
+
+    def wsend(p, k, dst):
+        c = wcopy(p, k, dst, cnt[p])
+        cnt[p] += 1
+        c.start()
+        sends.append(c)
+
+    def wwait(p, k):
+        wcopy(p, k, core, 0).wait_recv()
+
+    p1, p2 = (ypeer, xpeer), (xpeer, ypeer)
+    key = lambda zz, yy, xx: dev(zz, yy, xx) * 2 + r
+    for p in (0, 1):
+        wsend(p, own, p1[p])
+        wsend(p, own, p2[p])
+    for q in zpeer:
+        for p in (0, 1):
+            wsend(p, own, q)
+    for p in (0, 1):
+        wsend(p, own, core)
+
+    def fwd_z(p, i):
+        k = key(zp[i], y, x)
+        wwait(p, k)
+        wsend(p, k, p1[p])
+        wsend(p, k, p2[p])
+        wsend(p, k, core)
+
+    def fwd_1(p, i):
+        q = z if i < 0 else zp[i]
+        k = key(q, 1 - y, x) if p == 0 else key(q, y, 1 - x)
+        wwait(p, k)
+        wsend(p, k, p2[p])
+        wsend(p, k, core)
+
+    def fwd_2(p, i, o):
+        q = z if i < 0 else zp[i]
+        k = key(q, (y + o) % 2, 1 - x) if p == 0 else key(q, 1 - y, (x + o) % 2)
+        wwait(p, k)
+        wsend(p, k, core)
+
+    def core_wait(p):
+        def cw(i, _):
+            wwait(p, i * 2 + (1 - r))
+            return 0
+        lax.fori_loop(0, 16, cw, 0)
+
+    loads["tab"].wait()
+    loads["ids"].wait()
+    for s in range(2):
+        for j in range(32):
+            g, h = j // 4, j % 4
+            t = tab_ref[pl.ds(2 * j + s, 39, stride=64), :]
+            tabr[s, g * 40 : (g + 1) * 40, h * 128 : (h + 1) * 128] = jnp.concatenate([t, jnp.zeros((1, 128), F32)], axis=0).astype(BF)
+
+    def id_rows(d):
+        return ids_ref[:, pl.ds(pl.multiple_of((d * 2 + r) * 384, 128), 384)]
+
+    def one_hot(lo):
+        return (lax.broadcasted_iota(jnp.int32, (512, 384), 0) == lo).astype(F32).astype(BF)
+
+    def look(d):
+        idv = id_rows(d)
+        outs = []
+        for s in range(2):
+            ids = idv[s : s + 1]
+            lo, hi = ids % 512, ids // 512
+            res = nn(tabr[s], one_hot(lo))
+            e = jnp.zeros((40, 384), F32)
+            for g in range(8):
+                e = e + jnp.where(hi == g, res[g * 40 : (g + 1) * 40], 0.0)
+            outs.append(e)
+        return jnp.concatenate(outs, axis=0).astype(BF)
+
+    def ecopy(d, land):
+        return pltpu.make_async_remote_copy(
+            src_ref=eout.at[d], dst_ref=E.at[land], send_sem=R_["ess"].at[d], recv_sem=R_["ers"].at[land], device_id=(d, r), device_id_type=MESH)
+
+    def dcopy(d, land):
+        return pltpu.make_async_remote_copy(
+            src_ref=eout.at[d], dst_ref=D.at[land], send_sem=R_["dss"].at[d], recv_sem=R_["drs"].at[land], device_id=(d, r), device_id_type=MESH)
+
+    def looks(a, b):
+        def step(i, _):
+            d = (me + i) % 16
+            eout[d] = look(d)
+            ecopy(d, me).start()
+            return 0
+        lax.fori_loop(a, b, step, 0)
+
+    looks(1, 8)
+    fwd_1(0, -1)
+    fwd_1(1, -1)
+    looks(8, 12)
+    fwd_z(0, 0)
+    fwd_z(1, 0)
+    looks(12, 16)
+    E[me] = look(me)
+    for i in (1, 2):
+        for p in (0, 1):
+            fwd_z(p, i)
+    for i in (0, 1, 2):
+        for p in (0, 1):
+            fwd_1(p, i)
+    for i in (-1, 0, 1, 2):
+        for o in (0, 1):
+            fwd_2(0, i, o)
+
+    def ew(i, _):
+        d = (me + i) % 16
+        ecopy(d, d).wait()
+        return 0
+
+    lax.fori_loop(1, 16, ew, 0)
+    loads["dns"].wait()
+    loads["lab"].wait()
+    for t in range(26):
+        s = ts[t]
+        blk = E[s // 2].astype(F32)
+        e = jnp.where(s % 2 == 1, blk[40:80], blk[0:40])
+        xT[39 * t : 39 * t + 39, :] = e[0:39]
+    xT[1014:1027, :] = R_["dns_v"][...].astype(BF).astype(F32)
+    xT[1027:LN, :] = jnp.zeros((LN - 1027, 384), F32)
+    for i in range(9):
+        c = slice(128 * i, 128 * i + 128)
+        xl[0, :, c] = xT[c, :].T.astype(BF)
+    x0 = lambda lo, n: xl[0, :, lo : lo + n].astype(F32)
+    core_wait(0)
+    for l in range(3):
+        for lo, n in CH:
+            w = G[:, 16 * l : 16 * l + 16, lo : lo + n].astype(F32).reshape(32, 2, 8, n)
+            VT[l, :, lo : lo + n] = w[:, 0].reshape(256, n).astype(BF)
+            UT[l, :, lo : lo + n] = w[:, 1].reshape(256, n).astype(BF)
+    for l in range(3):
+        pr[l] = nt(xl[l], VT[l]).astype(BF)
+        for lo, n in CH:
+            q = nn(pr[l], UT[l, :, lo : lo + n]) + bia[l : l + 1, lo : lo + n]
+            qc[l, :, lo : lo + n] = q
+            v = x0(lo, n) * q + (x0(lo, n) if l == 0 else xr[:, lo : lo + n])
+            if l < 2:
+                xr[:, lo : lo + n] = v
+            xl[l + 1, :, lo : lo + n] = v.astype(BF)
+    for i in (-1, 0, 1, 2):
+        for o in (0, 1):
+            fwd_2(1, i, o)
+    core_wait(1)
+    for n in range(4):
+        c = slice(256 * n, 256 * n + 256)
+        a = nt(xl[3], G[8 * n : 8 * n + 8, 48:80, :].reshape(256, LN)) + bia[3:4, c]
+        a1[:, c] = a
+        h1[:, c] = (a * sig(a)).astype(BF)
+    for n in range(4):
+        c = slice(256 * n, 256 * n + 256)
+        a = nt(h1[...], G[8 * n : 8 * n + 8, 80:112, 0:1024].reshape(256, 1024)) + bia[4:5, c]
+        a2[:, c] = a
+        h2[:, c] = (a * sig(a)).astype(BF)
+    hc = G[:, 80:112, 1024:LN].reshape(1024, 128)
+    zl = nn(h2[...], hc) + bia[5:6, 0:128]
+    yl = jnp.broadcast_to(R_["lab_v"][...].astype(F32), (128, 384)).T
+    lossv = jnp.maximum(zl, 0.0) + jnp.log1p(jnp.exp(-jnp.abs(zl))) - yl * zl
+    dz = (sig(zl) - yl) / total
+    M[...] = jnp.zeros_like(M)
+    M[6:7, 0:128] = jnp.sum(lossv, axis=0, keepdims=True)
+    M[7:8, 0:128] = jnp.sum(dz, axis=0, keepdims=True)
+    hrow = hc.astype(F32).T[0:1]
+    for n in range(8):
+        c = slice(128 * n, 128 * n + 128)
+        M[5:6, c] = jnp.sum(dz * h2[:, c].astype(F32), axis=0, keepdims=True)
+        g = (dz * hrow[:, c] * slope(a2[:, c])).astype(BF)
+        d2[:, c] = g
+        M[4:5, c] = jnp.sum(g.astype(F32), axis=0, keepdims=True)
+
+    nsem = [0]
+
+    def go(src, dst, dst_dev):
+        i = nsem[0]
+        nsem[0] += 1
+        c = pltpu.make_async_remote_copy(
+            src_ref=src, dst_ref=dst, send_sem=R_["rss"].at[i], recv_sem=R_["rrs"].at[i], device_id=dst_dev, device_id_type=MESH)
+        c.start()
+        sends.append(c)
+        return c
+
+    st = {}
+
+    def axes(n):
+        return (y, x, ypeer, xpeer) if ITEMS[n][2] else (x, y, xpeer, ypeer)
+
+    def s0(n):
+        g = R_["g_" + n]
+        st[n] = go(g.at[1 - r], R_["C_" + n], core)
+
+    def s1(n):
+        a, b, pa, pb = axes(n)
+        st[n].wait_recv()
+        g, c = R_["g_" + n], R_["C_" + n]
+        g[r, 1 - a] = (g[r, 1 - a].astype(F32) + c[1 - a].astype(F32)).astype(BF)
+        st[n] = go(g.at[r, 1 - a], R_["P_" + n], pa)
+
+    def s2(n):
+        a, b, pa, pb = axes(n)
+        st[n].wait_recv()
+        g, c, p = R_["g_" + n], R_["C_" + n], R_["P_" + n]
+        g[r, a, 1 - b] = (g[r, a, 1 - b].astype(F32) + c[a, 1 - b].astype(F32) + p[1 - b].astype(F32)).astype(BF)
+        st[n] = go(g.at[r, a, 1 - b], R_["Q_" + n], pb)
+
+    def s3(n):
+        a, b, pa, pb = axes(n)
+        st[n].wait_recv()
+        g, c, p, q = R_["g_" + n], R_["C_" + n], R_["P_" + n], R_["Q_" + n]
+        st[n] = []
+        for i, zz in enumerate(zp):
+            g[r, a, b, zz] = (g[r, a, b, zz].astype(F32) + c[a, b, zz].astype(F32) + p[b, zz].astype(F32) + q[zz].astype(F32)).astype(BF)
+            st[n].append(go(g.at[r, a, b, zz], R_["T_" + n].at[i], zpeer[i]))
+
+    def s4(n):
+        a, b, pa, pb = axes(n)
+        for c in st[n]:
+            c.wait_recv()
+        g, c, p, q, t = R_["g_" + n], R_["C_" + n], R_["P_" + n], R_["Q_" + n], R_["T_" + n]
+        R_["o_" + n][...] = (
+            g[r, a, b, z].astype(F32) + c[a, b, z].astype(F32) + p[b, z].astype(F32) + q[z].astype(F32)
+            + (t[0].astype(F32) + t[1].astype(F32) + t[2].astype(F32)))
+
+    def put(n, base, g):
+        nb, _, yfirst = ITEMS[n]
+        for i in range(g.shape[0] // nb):
+            rep, xx, yy, zz = place(base + i)
+            a, b = (yy, xx) if yfirst else (xx, yy)
+            R_["g_" + n][rep, a, b, zz] = g[i * nb : i * nb + nb].astype(BF)
+
+    for n in range(4):
+        put("m", 8 * n, tn(d2[:, 256 * n : 256 * n + 256], h1[...]))
+    s0("m")
+    for n in range(4):
+        c = slice(256 * n, 256 * n + 256)
+        a1[:, c] = nn(d2[...], G[:, 80:112, c].reshape(1024, 256)) * slope(a1[:, c])
+    for n in range(4):
+        c = slice(256 * n, 256 * n + 256)
+        g = a1[:, c].astype(BF)
+        d1[:, c] = g
+        M[3:4, c] = jnp.sum(g.astype(F32), axis=0, keepdims=True)
+    s1("m")
+    for n in range(4):
+        put("i", 8 * n, tn(d1[:, 256 * n : 256 * n + 256], xl[3]))
+    s0("i")
+    for lo, n in CH:
+        dx[:, lo : lo + n] = nn(d1[...], G[:, 48:80, lo : lo + n].reshape(1024, n))
+
+    def cross_back(l):
+        for lo, n in CH:
+            g = dx[:, lo : lo + n]
+            dq = g * x0(lo, n)
+            M[l : l + 1, lo : lo + n] = jnp.sum(dq, axis=0, keepdims=True)
+            dql[:, lo : lo + n] = dq.astype(BF)
+            e = g * qc[l, :, lo : lo + n]
+            d0[:, lo : lo + n] = e if l == 2 else d0[:, lo : lo + n] + e
+        dpr[...] = nt(dql[...], UT[l]).astype(BF)
+        gr = R_["g_c%d" % l]
+        yfirst = ITEMS["c%d" % l][2]
+        for lo, n in CH:
+            gu = tn(pr[l], dql[:, lo : lo + n]).reshape(32, 8, n)
+            gv = tn(dpr[...], xl[l, :, lo : lo + n]).reshape(32, 8, n)
+            gg = jnp.concatenate([gv, gu], axis=1).astype(BF)
+            for k in range(32):
+                rep, xx, yy, zz = place(k)
+                a, b = (yy, xx) if yfirst else (xx, yy)
+                gr[rep, a, b, zz, :, lo : lo + n] = gg[k]
+
+    def cross_down(l):
+        for lo, n in CH:
+            v = dx[:, lo : lo + n] + nn(dpr[...], VT[l, :, lo : lo + n])
+            if l:
+                dx[:, lo : lo + n] = v
+            else:
+                d0[:, lo : lo + n] = d0[:, lo : lo + n] + v
+
+    cross_back(2)
+    s0("c2")
+    s1("i")
+    cross_down(2)
+    cross_back(1)
+    s0("c1")
+    s1("c2")
+    cross_down(1)
+    cross_back(0)
+    s0("c0")
+    cm = go(M, R_["MC"], core)
+    s1("c1")
+    cross_down(0)
+    for i in range(9):
+        c = slice(128 * i, 128 * i + 128)
+        xT[c, :] = d0[:, c].T
+    for t in range(26):
+        DE[t] = jnp.concatenate([xT[39 * t : 39 * t + 39, :], jnp.zeros((1, 384), F32)], axis=0)
+    DE[26] = jnp.zeros((40, 384), F32)
+
+    def back_rows(d):
+        return jnp.concatenate([DE[inv[2 * d]], DE[inv[2 * d + 1]]], axis=0).astype(BF)
+
+    def dstep(i, _):
+        d = (me + i) % 16
+        eout[d] = back_rows(d)
+        dcopy(d, me).start()
+        return 0
+
+    lax.fori_loop(1, 16, dstep, 0)
+    D[me] = back_rows(me)
+    s1("c0")
+    MS, MX = R_["MS"], R_["MX"]
+    cm.wait_recv()
+    MS[0] = M[...] + R_["MC"][...]
+    m1 = go(MS.at[0], MX.at[0], xpeer)
+    R[...] = jnp.zeros_like(R)
+
+    def one_part(i, s):
+        d = (me + i) % 16
+        ids = id_rows(d)[s : s + 1]
+        lo, hi = ids % 512, ids // 512
+        e = D[d].astype(F32)[40 * s : 40 * s + 40]
+        lhs = jnp.concatenate([jnp.where(hi == g, e, 0.0) for g in range(8)], axis=0).astype(BF)
+        return lhs, one_hot(lo)
+
+    def rows_in(a, b):
+        def acc(i2, _):
+            for j in range(2):
+                i = 2 * i2 + j
+                d = (me + i) % 16
+
+                @pl.when(i > 0)
+                def _():
+                    dcopy(d, d).wait_recv()
+            for s in range(2):
+                u, v = one_part(2 * i2, s), one_part(2 * i2 + 1, s)
+                R[s] += nt(jnp.concatenate([u[0], v[0]], axis=1), jnp.concatenate([u[1], v[1]], axis=1))
+            return 0
+        lax.fori_loop(a, b, acc, 0)
+
+    s2("m")
+    m1.wait_recv()
+    MS[1] = MS[0] + MX[0]
+    m2 = go(MS.at[1], MX.at[1], ypeer)
+    rows_in(0, 1)
+    s2("i")
+    m2.wait_recv()
+    MS[2] = MS[1] + MX[1]
+    m3 = [go(MS.at[2], MX.at[2 + i], zpeer[i]) for i in range(3)]
+    rows_in(1, 2)
+    s2("c2")
+    s3("m")
+    rows_in(2, 4)
+    s2("c1")
+    s3("i")
+    rows_in(4, 6)
+    s2("c0")
+    s3("c2")
+    rows_in(6, 8)
+    for s in range(2):
+        for j in range(32):
+            g, h = j // 4, j % 4
+            gt[pl.ds(2 * j + s, 39, stride=64), :] = R[s, g * 40 : g * 40 + 39, h * 128 : (h + 1) * 128]
+    cg = go(gt, gtc, core)
+    s3("c1")
+    s3("c0")
+    for c in m3:
+        c.wait_recv()
+    pos = [MS[2], MX[2], MX[3], MX[4]]
+    u = jnp.where(z % 2 == 0, pos[0], pos[1]) + jnp.where(z % 2 == 0, pos[1], pos[0])
+    v = jnp.where(z % 2 == 0, pos[2], pos[3]) + jnp.where(z % 2 == 0, pos[3], pos[2])
+    MO[...] = jnp.where(z < 2, u, v) + jnp.where(z < 2, v, u)
+    for n in ORDER:
+        s4(n)
+    cg.wait_recv()
+
+    def dw(i, _):
+        d = (me + i) % 16
+        dcopy(d, d).wait_send()
+        return 0
+
+    lax.fori_loop(1, 16, dw, 0)
+    for c in sends:
+        c.wait_send()
+
+
+def mega(total, ts, inv, ids, tab, cr, ti, tm, hd, dns, lab, bia):
+    V, S = pltpu.VMEM, jax.ShapeDtypeStruct
+    vm, sm, an = pl.BlockSpec(memory_space=pltpu.VMEM), pl.BlockSpec(memory_space=pltpu.SMEM), pl.BlockSpec(memory_space=pl.ANY)
+    ins = {"ts": ts, "inv": inv, "bia": bia, "ids": ids, "tab": tab, "cr": cr, "ti": ti, "tm": tm, "hd": hd, "dns": dns, "lab": lab}
+    outs = {"gt": S((2496, 128), F32), "gtc": S((2496, 128), F32), "MO": S((8, LN), F32)}
+    for n in ORDER:
+        outs["o_" + n] = S(ITEMS[n][:2], F32)
+    scr = {n + "_v": V(ins[n].shape, ins[n].dtype) for n in ("ids", "tab", "cr", "ti", "tm", "hd", "dns", "lab")}
+    scr.update(
+        G=V((32, RB, LN), BF), E=V((16, 80, 384), BF), D=V((16, 80, 384), BF), eout=V((16, 80, 384), BF), tabr=V((2, 320, 512), BF),
+        xT=V((LN, 384), F32), dx=V((384, LN), F32), xl=V((4, 384, LN), BF), qc=V((3, 384, LN), F32), pr=V((3, 384, 256), BF),
+        VT=V((3, 256, LN), BF), UT=V((3, 256, LN), BF), a1=V((384, 1024), F32), a2=V((384, 1024), F32), h1=V((384, 1024), BF), h2=V((384, 1024), BF),
+        d0=V((384, LN), F32), dql=V((384, LN), BF), dpr=V((384, 256), BF), DE=V((27, 40, 384), F32), M=V((8, LN), F32), R=V((2, 320, 512), F32),
+        MC=V((8, LN), F32), MS=V((3, 8, LN), F32), MX=V((5, 8, LN), F32))
+    for n in ORDER:
+        nb, L, _ = ITEMS[n]
+        scr["g_" + n] = V((2, 2, 2, 4, nb, L), BF)
+        scr["C_" + n] = V((2, 2, 4, nb, L), BF)
+        scr["P_" + n] = V((2, 4, nb, L), BF)
+        scr["Q_" + n] = V((4, nb, L), BF)
+        scr["T_" + n] = V((3, nb, L), BF)
+    dma = pltpu.SemaphoreType.DMA
+    scr.update(lsem=dma((8,)), wss=dma((2, 32)), wrs=dma((2, 32)), ess=dma((16,)), ers=dma((16,)), dss=dma((16,)), drs=dma((16,)), rss=dma((40,)), rrs=dma((40,)))
+    res = pl.pallas_call(
+        functools.partial(mega_body, total, list(ins), list(outs), list(scr)), name="train_step",
+        out_shape=tuple(outs.values()), in_specs=[sm, sm, vm] + [an] * 8, out_specs=(vm,) * len(outs),
+        scratch_shapes=list(scr.values()),
+        compiler_params=pltpu.CompilerParams(collective_id=0, has_side_effects=True, vmem_limit_bytes=63 << 20),
+    )(*ins.values())
+    return dict(zip(outs, res))
+
+
+C5 = 1 - 0.5**5
+
+
+def adamw(w, m, v, g, rate):
+    mn = 0.5 * m + 0.5 * g
+    vn = 0.5 * v + 0.5 * g * g
+    return w - rate * ((mn / C5) / (jnp.sqrt(vn / C5) + EPSILON) + WEIGHT_DECAY * w), mn, vn
+
+
+def update_body(names_in, names_out, names_scr, *refs):
+    it = iter(refs)
+    R_ = {n: next(it) for n in names_in + names_out + names_scr}
+    rc, isem, osem = R_["rc"], R_["isem"], R_["osem"]
+    order = [k + q for k in "tcim" for q in "wnv"]
+    ld = {}
+    for i, n in enumerate(order + ["gt", "gtc"]):
+        ld[n] = pltpu.make_async_copy(R_[n], R_["v_" + n], isem.at[i])
+        ld[n].start()
+    outs = []
+
+    def out(name, rows=None):
+        i = len(outs)
+        s, d = R_["u_" + name], R_["o_" + name]
+        if rows is not None:
+            s, d = s.at[rows], d.at[rows]
+        c = pltpu.make_async_copy(s, d, osem.at[i])
+        c.start()
+        outs.append(c)
+
+    rows = {"c": [("c0", 0, 16), ("c1", 16, 16), ("c2", 32, 16)], "i": [("i", 0, 32)], "m": [("m", 0, 32)]}
+    for k in "imc":
+        for q in "wnv":
+            ld[k + q].wait()
+        for n, lo, nb in rows[k]:
+            L = R_["v_" + k + "w"].shape[1]
+            at = slice(lo, lo + nb)
+            w, m, v = adamw(R_["v_" + k + "w"][at], R_["v_" + k + "n"][at], R_["v_" + k + "v"][at], R_["g_" + n][:, 0:L], RATE_DENSE)
+            R_["u_" + k + "w"][at], R_["u_" + k + "n"][at], R_["u_" + k + "v"][at], R_["u_" + k + "l"][at] = w, m, v, w.astype(BF)
+        for q in "wnvl":
+            out(k + q)
+    for n in ("tw", "tn", "tv", "gt", "gtc"):
+        ld[n].wait()
+    row = lax.broadcasted_iota(jnp.int32, (64, 128), 0)
+    lane = lax.broadcasted_iota(jnp.int32, (64, 128), 1)
+    use = ((row // 2) * 128 + lane) < jnp.where(row % 2 == 0, rc[0], rc[1])
+    for part in range(3):
+        def tab(c, _):
+            q = pl.ds(pl.multiple_of(c * 64, 64), 64)
+            w, m, v = R_["v_tw"][q], R_["v_tn"][q], R_["v_tv"][q]
+            nw, nm, nv = adamw(w, m, v, R_["v_gt"][q] + R_["v_gtc"][q], RATE_TABLE)
+            nw = jnp.where(use, nw, w)
+            R_["u_tw"][q] = nw
+            R_["u_tn"][q] = jnp.where(use, nm, m)
+            R_["u_tv"][q] = jnp.where(use, nv, v)
+            R_["u_tl"][q] = nw.astype(BF)
+            return 0
+        lax.fori_loop(13 * part, 13 * part + 13, tab, 0)
+        for q in "wnvl":
+            out("t" + q, pl.ds(832 * part, 832))
+    for c in outs:
+        c.wait()
+
+
+def update(rc, g, state):
+    V, S = pltpu.VMEM, jax.ShapeDtypeStruct
+    vm, sm, an = pl.BlockSpec(memory_space=pltpu.VMEM), pl.BlockSpec(memory_space=pltpu.SMEM), pl.BlockSpec(memory_space=pl.ANY)
+    ins, specs = {"rc": rc}, [sm]
+    for k in "tcim":
+        for q, a in zip("wnv", state[k]):
+            ins[k + q] = a
+            specs.append(an)
+    for n in ("gt", "gtc"):
+        ins[n] = g[n]
+        specs.append(an)
+    for n in ORDER:
+        ins["g_" + n] = g["o_" + n]
+        specs.append(vm)
+    outs, scr = {}, {}
+    for k in "tcim":
+        for q in "wnvl":
+            shape, kind = state[k][0].shape, BF if q == "l" else F32
+            outs["o_" + k + q] = S(shape, kind)
+            scr["u_" + k + q] = V(shape, kind)
+            if q != "l":
+                scr["v_" + k + q] = V(shape, kind)
+    scr["v_gt"] = V((2496, 128), F32)
+    scr["v_gtc"] = V((2496, 128), F32)
+    scr["isem"] = pltpu.SemaphoreType.DMA((14,))
+    scr["osem"] = pltpu.SemaphoreType.DMA((24,))
+    return pl.pallas_call(
+        functools.partial(update_body, list(ins), list(outs), list(scr)), name="adamw_step",
+        out_shape=tuple(outs.values()), in_specs=specs, out_specs=(an,) * len(outs), scratch_shapes=list(scr.values()),
+        compiler_params=pltpu.CompilerParams(vmem_limit_bytes=63 << 20),
+    )(*ins.values())
+
+
+def tab_view(t):
+    S, n, C = t.shape
+    return jnp.transpose(jnp.transpose(t, (2, 0, 1)).reshape(C, S, n // 128, 128), (0, 2, 1, 3)).reshape(C * S * n // 128, 128)
+
+
+def tab_unview(v, S=2, n=4096, C=39):
+    return jnp.transpose(jnp.transpose(v.reshape(C, n // 128, S, 128), (0, 2, 1, 3)).reshape(C, S, n), (1, 2, 0))
+
+
+def fast_shards(
+    event_ids, row_counts, table_slot, dense_input, labels,
+    tables, tables_m, tables_v, cross_uv, cross_m, cross_v,
+    tower_in, tower_in_m, tower_in_v, tower_mid, tower_mid_m, tower_mid_v,
+    head_weight, head_m, head_v, biases, biases_m, biases_v,
+):
+    total = float(labels.shape[0] * lax.axis_size("dp") * lax.axis_size("rep"))
+    turn = lambda a: jnp.transpose(a, (0, 1, 3, 2)).reshape(48, WIDTH)
+    back = lambda a: jnp.transpose(a.reshape(LAYERS, 2, 8, WIDTH), (0, 1, 3, 2))
+    state = {
+        "t": [tab_view(a) for a in (tables, tables_m, tables_v)],
+        "c": [turn(a) for a in (cross_uv, cross_m, cross_v)],
+        "i": [a.T for a in (tower_in, tower_in_m, tower_in_v)],
+        "m": [a.T for a in (tower_mid, tower_mid_m, tower_mid_v)],
+    }
+    hits = table_slot[None, :] == jnp.arange(32, dtype=jnp.int32)[:, None]
+    inv = TABLES - jnp.sum(hits * (TABLES - jnp.arange(TABLES, dtype=jnp.int32))[None, :], axis=1)
+    wide = lambda v: jnp.pad(v, (0, LN - v.shape[0]))
+    at = LAYERS * WIDTH
+    bia = jnp.stack(
+        [wide(biases[WIDTH * i : WIDTH * i + WIDTH]) for i in range(3)]
+        + [wide(biases[at : at + 1024]), wide(biases[at + 1024 : at + 2048]),
+           jnp.broadcast_to(biases[at + 2048], (LN,)), jnp.zeros((LN,), F32), jnp.zeros((LN,), F32)]
+    )
+    g = mega(total, table_slot, inv, event_ids, state["t"][0], state["c"][0], state["i"][0], state["m"][0],
+             head_weight.reshape(1, 32), dense_input.T, labels.reshape(1, 384), bia)
+    o = update(row_counts, g, state)
+    MO = g["MO"]
+    loss = MO[6, 0]
+    g_bias = jnp.concatenate([MO[0, :WIDTH], MO[1, :WIDTH], MO[2, :WIDTH], MO[3, :1024], MO[4, :1024], MO[7, :1]])
+    k = lax.axis_index("dp") * 2 + lax.axis_index("rep")
+    g_head = lax.dynamic_slice(MO[5], (k * 32,), (32,))
+    tail = []
+    for w, m, v, gg, rate in ((head_weight, head_m, head_v, g_head, RATE_DENSE), (biases, biases_m, biases_v, g_bias, RATE_BIAS)):
+        a, b, c = adamw_update(w, m, v, gg, rate)
+        tail += [a, b, c, a.astype(BF)]
+    return (
+        loss,
+        *[tab_unview(a) for a in o[0:4]],
+        *[back(a) for a in o[4:8]],
+        *[a.T for a in o[8:12]],
+        *[a.T for a in o[12:16]],
+        *tail,
+    )
+
+
 def solution(mesh):
     placed = (
         P("dp", None),
@@ -342,8 +1000,9 @@
         P(),
         P(),
     )
+    fits = mesh.shape["dp"] == 16 and mesh.shape["rep"] == 2
     return jax.shard_map(
-        shards,
+        fast_shards if fits else shards,
         mesh=mesh,
         in_specs=placed,
         out_specs=(

time: 854 us -> 156 us (0.18)
  waiting for transfers between devices: 417 us -> 0 us
  matrix products: 169 us -> 0 us
  Pallas kernels: 0 us -> 144 us
  blocking collectives: 82.2 us -> 0 us
  other arithmetic: 67.4 us -> 3.27 us
  local copies, waits for them, and re-layouts: 60.6 us -> 6.93 us
  starting transfers between devices: 37.2 us -> 0 us
  between operations: 18.5 us -> 0.88 us
    reduce_scatter x2 -> x0, waiting for transfers between devices: 252 us -> none  [the longest x1 141 us: shards(): lax.psum_scatter(dense_total[2], ('dp', 'rep'), scatter_dimension=1, tile...]
    dot_general x108 -> x0, matrix products: 169 us -> none  [the longest x36 79 us: contract_rows(): lax.dot_general(left_side, right_side, (((0,), (0,)), ((), ())), preferre...]
    pallas_call x0 -> x2, Pallas kernels: none -> 144 us  [the longest x1 137 us: mega(): pl.pallas_call(functools.partial(mega_body, total, list(ins), list(outs),...]
    unnamed x8 -> x0, waiting for transfers between devices: 97 us -> none
    all_gather x3 -> x0, waiting for transfers between devices: 48.3 us -> none  [the longest x1 48.3 us: shards(): lax.all_gather(shard_low[2], ('dp', 'rep'), axis=1, tiled=True)]
    psum x1 -> x0, blocking collectives: 41.3 us -> none  [shards(): bias_total, loss_total = lax.psum((bias_total, loss_total), ('dp', 'rep'))]
    unnamed x1 -> x0, blocking collectives: 40.9 us -> none
    all_to_all x6 -> x0, starting transfers between devices: 36.9 us -> none  [the longest x3 20.8 us: shards(): lax.all_to_all(outgoing, 'dp', split_axis=0, concat_axis=0, tiled=True)]
  transfers between devices with their start and end apart: 13 -> 0, of which waited for: 7 -> 0; matrix products, arithmetic and copies ran while one was open for 20% -> 0% of each run, Pallas kernels for 0% -> 0%
where the time goes in v2:
time: 156 us; the launch traced here: 155 us
  Pallas kernels  144 us (92%)
  local copies, waits for them, and re-layouts  6.93 us (4%)
  other arithmetic  3.27 us (2%)
    pallas_call x1, Pallas kernels, mega(): pl.pallas_call(functools.partial(mega_body, total, list(ins), list(outs),...  137 us
    pallas_call x1, Pallas kernels, update(): pl.pallas_call(functools.partial(update_body, list(ins), list(outs), list...  7.53 us

profile of v2, /device:TPU:0, one launch (start us, length us, event | category | flops | bytes accessed | tf_op | source)
XLA Modules:
  0.0 155.2 jit_solution(3961955206194188799)
XLA Ops:
  0.7 0.9 fusion.9
  1.6 0.8 fusion.8
  2.4 0.7 slice_select_fusion
  3.2 1.3 slice.48
  4.4 0.6 stack_broadcast_in_dim.3
  5.1 0.7 stack.27.refs_2_
  5.8 0.8 select_reduce_fusion
  6.6 0.5 broadcast_subtract_fusion.refs_1_
  7.1 1.2 reshape.129.refs_10_
  8.3 136.6 %train_step.1 = (f32[2496,128]{1,0:T(8,128)}, f32[2496,128]{1,0:T(8,128)}, f32[8,1152]{1,0:T(8,128)}, f32[32,1024]{1,0:T(8,128)}, f32[32,1152]{1,0:T(8,128)}, /*...) custom-call(s32[26]{0:T(128)} %refs_0_.2, s32[32]{0:T(128)} %broadcast_subtract_fusion.refs_1_, ...), custom_call_target="tpu_custom_call" | custom-call | tf_op jit(solution)/shard_map/train_step/pallas_call | solution.py:817
  144.9 0.0 copy-start.3
  144.9 0.0 copy-start
  144.9 0.0 copy-start.1
  144.9 0.0 copy-start.2
  145.0 0.0 copy-start.4
  145.0 0.0 copy-start.5
  145.0 0.0 copy-start.6
  145.0 7.5 %adamw_step.1 = (f32[2496,128]{1,0:T(8,128)}, f32[2496,128]{1,0:T(8,128)}, f32[2496,128]{1,0:T(8,128)}, bf16[2496,128]{1,0:T(8,128)(2,1)}, f32[48,1027]{1,0:T(8,...) custom-call(s32[2]{0:T(128)} %refs_0_.3, ...), custom_call_target="tpu_custom_call" | custom-call | tf_op jit(solution)/shard_map/adamw_step/pallas_call | solution.py:915
  152.5 0.0 copy-done.3
  152.6 0.5 fusion.6
  153.1 0.7 concatenate.3
  153.8 0.0 copy-done
  153.9 0.0 copy-done.1
  153.9 0.0 copy-done.2
  153.9 0.6 fusion.2
  154.5 0.0 copy-done.4
  154.5 0.0 copy-done.5
  154.6 0.0 copy-done.6
  154.6 0.6 fusion.4
  (14 shorter events, 0.1 us)
Async XLA Ops:
  144.9 7.6 %copy-start.3 = (f32[8,1152]{1,0:T(8,128)S(1)}, f32[8,1152]{1,0:T(8,128)}, u32[]{:S(2)}) copy-start(f32[8,1152]{1,0:T(8,128)} %get-tuple-element.49) | copy-start | bytes 110596
  144.9 8.9 %copy-start = (f32[5130]{0:T(1024)S(1)}, f32[5130]{0:T(1024)}, u32[]{:S(2)}) copy-start(f32[5130]{0:T(1024)} %param.43) | copy-start | bytes 61564
  144.9 8.9 %copy-start.1 = (f32[5130]{0:T(1024)S(1)}, f32[5130]{0:T(1024)}, u32[]{:S(2)}) copy-start(f32[5130]{0:T(1024)} %param.44) | copy-start | bytes 61564
  144.9 8.9 %copy-start.2 = (f32[5130]{0:T(1024)S(1)}, f32[5130]{0:T(1024)}, u32[]{:S(2)}) copy-start(f32[5130]{0:T(1024)} %param.45) | copy-start | bytes 61564
  145.0 9.6 %copy-start.4 = (f32[32]{0:T(128)S(1)}, f32[32]{0:T(128)}, u32[]{:S(2)}) copy-start(f32[32]{0:T(128)} %param.40) | copy-start | bytes 388
  145.0 9.6 %copy-start.5 = (f32[32]{0:T(128)S(1)}, f32[32]{0:T(128)}, u32[]{:S(2)}) copy-start(f32[32]{0:T(128)} %param.41) | copy-start | bytes 388
  145.0 9.6 %copy-start.6 = (f32[32]{0:T(128)S(1)}, f32[32]{0:T(128)}, u32[]{:S(2)}) copy-start(f32[32]{0:T(128)} %param.42) | copy-start | bytes 388

commit v3 on v2

--- a/solution.py
+++ b/solution.py
@@ -324,9 +324,32 @@
 BF = jnp.bfloat16
 LN = 1152
 RB = 112
+BIASES = 5130
 CH = [(0, 256), (256, 256), (512, 256), (768, 256), (1024, 128)]
-ITEMS = {"m": (32, 1024, True), "i": (32, LN, False), "c2": (16, LN, True), "c1": (16, LN, False), "c0": (16, LN, True)}
-ORDER = ["m", "i", "c2", "c1", "c0"]
+ITEMS = {
+    "m0": (16, 1024, True, "m", 0),
+    "m1": (16, 1024, False, "m", 16),
+    "i": (32, LN, True, "i", 0),
+    "c2": (16, LN, False, "c2", 0),
+    "c1": (16, LN, True, "c1", 0),
+    "c0": (16, LN, False, "c0", 0),
+}
+ORDER = list(ITEMS)
+SUMS = {"m": (32, 1024), "i": (32, LN), "c2": (16, LN), "c1": (16, LN), "c0": (16, LN)}
+PARTS = {"A": (0, 48, True), "I": (48, 48, False), "U": (96, 16, False)}
+LAST_Z = "U"
+FORWARD = [
+    "ownU", "ownI", "ownA", "prep", "L0", "L1", "f1I-", "f1U-", "corU", "fzI0", "fzA0", "fzI1", "fzA1", "f1A-", "L2", "L3",
+    "f2U-1", "f2U-0", "fzI2", "f1A0", "corI", "f1I1", "L4", "L5", "L6", "fzA2", "f1A1", "fzU1", "fzU0", "f2A00", "f2I-0",
+    "L7", "L8", "f1I0", "f1I2", "f2I10", "corA", "L9", "fzU2", "f2A20", "L10", "f1A2", "f2A10", "f2A-0", "f2A11", "L11",
+    "f2I-1", "f2I20", "L12", "L13", "L14", "f2I01", "f2A-1", "f2A01", "L15", "f2I11", "f2A21", "f2I21", "dei", "f2I00",
+    "x0", "cf", "a1", "a2",
+]
+BACKWARD = [
+    "dTm", "dh1", "dx3", "s1m0", "s1m1", "ch2", "cg2", "ch1", "ch0", "cg0", "s2m1", "M1", "D", "dTi", "s3m1", "M2", "s1c2",
+    "s1i", "cg1", "s2m0", "M3", "s2i", "s3m0", "s1c0", "s2c2", "s1c1", "s3i", "sc0", "sc1", "s4m1", "sc2", "sc3", "sc4",
+    "s4m0", "s3c2", "s2c1", "s2c0", "s3c1", "sc5", "sc6", "s3c0", "sc7", "s4c2", "gt", "M4", "s4c1", "s4i", "gts", "s4c0",
+]
 
 
 def nt(a, b):
@@ -361,11 +384,11 @@
     ts, inv = R_["ts"], R_["inv"]
     G, E, D, eout, tabr = R_["G"], R_["E"], R_["D"], R_["eout"], R_["tabr"]
     xT, dx, xl, qc, pr = R_["xT"], R_["dx"], R_["xl"], R_["qc"], R_["pr"]
-    VT, UT, a1, a2, h1, h2 = R_["VT"], R_["UT"], R_["a1"], R_["a2"], R_["h1"], R_["h2"]
+    VT, UT, h1, h2 = R_["VT"], R_["UT"], R_["h1"], R_["h2"]
     d0, dql, dpr, DE, M, R = R_["d0"], R_["dql"], R_["dpr"], R_["DE"], R_["M"], R_["R"]
-    ids_ref, tab_ref, bia = R_["ids_v"], R_["tab_v"], R_["bia"]
-    xr, d1, d2 = dx, h1, h2
-    gt, gtc, MO = R_["gt"], R_["gtc"], R_["MO"]
+    ids_ref, tab_ref, bia = R_["ids_v"], R_["gg"], R_["bia"]
+    xr, a1, a2, d1, d2 = dx, dx, d0, h1, h2
+    gt, gg_, gtc, MO = R_["gt"], R_["gg"], R_["gtc"], R_["MO"]
     me = lax.axis_index("dp")
     r = lax.axis_index("rep")
     x, y, z = me % 2, (me // 2) % 2, me // 4
@@ -376,8 +399,8 @@
     zpeer = [(dev(q, y, x), r) for q in zp]
 
     loads = {}
-    for i, n in enumerate(["cr", "ti", "tm", "hd", "tab", "ids", "dns", "lab"]):
-        c = pltpu.make_async_copy(R_[n], R_[n + "_v"], R_["lsem"].at[i])
+    for i, n in enumerate(["cr", "ti", "tm", "hd", "tab", "ids", "dns", "lab", "bi"]):
+        c = pltpu.make_async_copy(R_[n], R_["gg" if n == "tab" else n + "_v"], R_["lsem"].at[i])
         c.start()
         loads[n] = c
     bar = pltpu.get_barrier_semaphore()
@@ -394,19 +417,19 @@
     G[own, 48:80, 1024:LN] = jnp.concatenate([ti[:, 1024:1027], jnp.zeros((32, 125), F32)], axis=1).astype(BF)
     G[own, 80:112, 0:1024] = tm[...].astype(BF)
     eye = lax.broadcasted_iota(jnp.int32, (32, 32), 0) == lax.broadcasted_iota(jnp.int32, (32, 32), 1)
-    hcol = jnp.sum(jnp.where(eye, jnp.broadcast_to(hd[...], (32, 32)), 0.0), axis=1, keepdims=True)
+    hcol = jnp.sum(jnp.where(eye, jnp.broadcast_to(hd[...].reshape(1, 32), (32, 32)), 0.0), axis=1, keepdims=True)
     G[own, 80:112, 1024:LN] = jnp.broadcast_to(hcol, (32, 128)).astype(BF)
     pl.semaphore_wait(bar, 16)
 
-    parts = ((0, 48), (48, 64))
-    cnt = [0, 0]
+    cnt = {p: 0 for p in PARTS}
+    pnum = {p: i for i, p in enumerate(PARTS)}
     sends = []
 
     def wcopy(p, k, dst, si):
-        lo, n = parts[p]
+        lo, n, _ = PARTS[p]
         return pltpu.make_async_remote_copy(
             src_ref=G.at[k, pl.ds(lo, n)], dst_ref=G.at[k, pl.ds(lo, n)],
-            send_sem=R_["wss"].at[p, si], recv_sem=R_["wrs"].at[p, k], device_id=dst, device_id_type=MESH)
+            send_sem=R_["wss"].at[pnum[p], si], recv_sem=R_["wrs"].at[pnum[p], k], device_id=dst, device_id_type=MESH)
 
     def wsend(p, k, dst):
         c = wcopy(p, k, dst, cnt[p])
@@ -417,35 +440,64 @@
     def wwait(p, k):
         wcopy(p, k, core, 0).wait_recv()
 
-    p1, p2 = (ypeer, xpeer), (xpeer, ypeer)
+    p1 = {p: ypeer if PARTS[p][2] else xpeer for p in PARTS}
+    p2 = {p: xpeer if PARTS[p][2] else ypeer for p in PARTS}
     key = lambda zz, yy, xx: dev(zz, yy, xx) * 2 + r
-    for p in (0, 1):
+    inner = (z == 1) | (z == 2)
+    zq = [zp[0], jnp.where(inner, zp[2], zp[1]), jnp.where(inner, zp[1], zp[2])]
+    on_to = [zp[2], zp[0], zp[0]]
+    isends = []
+
+    def isend(p, k, zz):
+        c = wcopy(p, k, (dev(zz, y, x), r), cnt[p])
+        cnt[p] += 1
+        isends.append(c)
+
+        @pl.when(inner)
+        def _():
+            c.start()
+
+    def f_own(p):
+        wsend(p, own, (dev(zp[0], y, x), r))
+        isend(p, own, zp[2])
         wsend(p, own, p1[p])
         wsend(p, own, p2[p])
-    for q in zpeer:
-        for p in (0, 1):
-            wsend(p, own, q)
-    for p in (0, 1):
+
+    def f_core(p):
         wsend(p, own, core)
 
     def fwd_z(p, i):
-        k = key(zp[i], y, x)
+        k = key(zq[i], y, x)
         wwait(p, k)
+        isend(p, k, on_to[i])
         wsend(p, k, p1[p])
         wsend(p, k, p2[p])
         wsend(p, k, core)
 
+    def up_down(p, k):
+        if p in LAST_Z:
+            wsend(p, k, (dev(zp[0], y, x), r))
+            isend(p, k, zp[2])
+
+    def fwd_zl(p, i, c):
+        k = key(zq[i], (y + c // 2) % 2, (x + c % 2) % 2)
+        wwait(p, k)
+        isend(p, k, on_to[i])
+        wsend(p, k, core)
+
     def fwd_1(p, i):
-        q = z if i < 0 else zp[i]
-        k = key(q, 1 - y, x) if p == 0 else key(q, y, 1 - x)
+        q = z if i < 0 else zq[i]
+        k = key(q, 1 - y, x) if PARTS[p][2] else key(q, y, 1 - x)
         wwait(p, k)
+        up_down(p, k)
         wsend(p, k, p2[p])
         wsend(p, k, core)
 
     def fwd_2(p, i, o):
-        q = z if i < 0 else zp[i]
-        k = key(q, (y + o) % 2, 1 - x) if p == 0 else key(q, 1 - y, (x + o) % 2)
+        q = z if i < 0 else zq[i]
+        k = key(q, (y + o) % 2, 1 - x) if PARTS[p][2] else key(q, 1 - y, (x + o) % 2)
         wwait(p, k)
+        up_down(p, k)
         wsend(p, k, core)
 
     def core_wait(p):
@@ -454,13 +506,14 @@
             return 0
         lax.fori_loop(0, 16, cw, 0)
 
-    loads["tab"].wait()
-    loads["ids"].wait()
-    for s in range(2):
-        for j in range(32):
-            g, h = j // 4, j % 4
-            t = tab_ref[pl.ds(2 * j + s, 39, stride=64), :]
-            tabr[s, g * 40 : (g + 1) * 40, h * 128 : (h + 1) * 128] = jnp.concatenate([t, jnp.zeros((1, 128), F32)], axis=0).astype(BF)
+    def f_prep():
+        loads["tab"].wait()
+        loads["ids"].wait()
+        for s in range(2):
+            for j in range(32):
+                g, h = j // 4, j % 4
+                t = tab_ref[pl.ds(2 * j + s, 39, stride=64), :]
+                tabr[s, g * 40 : (g + 1) * 40, h * 128 : (h + 1) * 128] = jnp.concatenate([t, jnp.zeros((1, 128), F32)], axis=0).astype(BF)
 
     def id_rows(d):
         return ids_ref[:, pl.ds(pl.multiple_of((d * 2 + r) * 384, 128), 384)]
@@ -489,83 +542,124 @@
         return pltpu.make_async_remote_copy(
             src_ref=eout.at[d], dst_ref=D.at[land], send_sem=R_["dss"].at[d], recv_sem=R_["drs"].at[land], device_id=(d, r), device_id_type=MESH)
 
+    def nth(i):
+        j, w = i // 4, i % 4
+        zz = jnp.where(j == 0, zp[1], jnp.where(j == 1, zp[2], jnp.where(j == 2, zp[0], z)))
+        return dev(zz, (y + w // 2) % 2, (x + w) % 2)
+
     def looks(a, b):
         def step(i, _):
-            d = (me + i) % 16
+            d = nth(i)
             eout[d] = look(d)
-            ecopy(d, me).start()
+
+            @pl.when(i != 12)
+            def _():
+                ecopy(d, me).start()
             return 0
         lax.fori_loop(a, b, step, 0)
 
-    looks(1, 8)
-    fwd_1(0, -1)
-    fwd_1(1, -1)
-    looks(8, 12)
-    fwd_z(0, 0)
-    fwd_z(1, 0)
-    looks(12, 16)
-    E[me] = look(me)
-    for i in (1, 2):
-        for p in (0, 1):
-            fwd_z(p, i)
-    for i in (0, 1, 2):
-        for p in (0, 1):
-            fwd_1(p, i)
-    for i in (-1, 0, 1, 2):
-        for o in (0, 1):
-            fwd_2(0, i, o)
-
-    def ew(i, _):
-        d = (me + i) % 16
-        ecopy(d, d).wait()
-        return 0
-
-    lax.fori_loop(1, 16, ew, 0)
-    loads["dns"].wait()
-    loads["lab"].wait()
-    for t in range(26):
-        s = ts[t]
-        blk = E[s // 2].astype(F32)
-        e = jnp.where(s % 2 == 1, blk[40:80], blk[0:40])
-        xT[39 * t : 39 * t + 39, :] = e[0:39]
-    xT[1014:1027, :] = R_["dns_v"][...].astype(BF).astype(F32)
-    xT[1027:LN, :] = jnp.zeros((LN - 1027, 384), F32)
-    for i in range(9):
-        c = slice(128 * i, 128 * i + 128)
-        xl[0, :, c] = xT[c, :].T.astype(BF)
     x0 = lambda lo, n: xl[0, :, lo : lo + n].astype(F32)
-    core_wait(0)
-    for l in range(3):
-        for lo, n in CH:
-            w = G[:, 16 * l : 16 * l + 16, lo : lo + n].astype(F32).reshape(32, 2, 8, n)
-            VT[l, :, lo : lo + n] = w[:, 0].reshape(256, n).astype(BF)
-            UT[l, :, lo : lo + n] = w[:, 1].reshape(256, n).astype(BF)
-    for l in range(3):
-        pr[l] = nt(xl[l], VT[l]).astype(BF)
-        for lo, n in CH:
-            q = nn(pr[l], UT[l, :, lo : lo + n]) + bia[l : l + 1, lo : lo + n]
-            qc[l, :, lo : lo + n] = q
-            v = x0(lo, n) * q + (x0(lo, n) if l == 0 else xr[:, lo : lo + n])
-            if l < 2:
-                xr[:, lo : lo + n] = v
-            xl[l + 1, :, lo : lo + n] = v.astype(BF)
-    for i in (-1, 0, 1, 2):
-        for o in (0, 1):
-            fwd_2(1, i, o)
-    core_wait(1)
-    for n in range(4):
-        c = slice(256 * n, 256 * n + 256)
-        a = nt(xl[3], G[8 * n : 8 * n + 8, 48:80, :].reshape(256, LN)) + bia[3:4, c]
-        a1[:, c] = a
-        h1[:, c] = (a * sig(a)).astype(BF)
-    for n in range(4):
-        c = slice(256 * n, 256 * n + 256)
-        a = nt(h1[...], G[8 * n : 8 * n + 8, 80:112, 0:1024].reshape(256, 1024)) + bia[4:5, c]
-        a2[:, c] = a
-        h2[:, c] = (a * sig(a)).astype(BF)
+
+    def f_rows():
+        E[me] = eout[me]
+        for n in range(32):
+            slot_table = jnp.int32(TABLES)
+            for t in range(TABLES):
+                slot_table = jnp.where(ts[t] == n, t, slot_table)
+            inv[n] = slot_table
+        loads["bi"].wait()
+        bv = R_["bi_v"][...].reshape(1, BIASES)
+        bia[...] = jnp.zeros_like(bia)
+        for i in range(3):
+            bia[i : i + 1, 0:1027] = bv[:, 1027 * i : 1027 * i + 1027]
+        bia[3:4, 0:1024] = bv[:, 3081:4105]
+        bia[4:5, 0:1024] = bv[:, 4105:5129]
+        bia[5:6, :] = jnp.broadcast_to(bv[:, 5129:5130], (1, LN))
+        loads["dns"].wait()
+        loads["lab"].wait()
+
+        def ew(i, _):
+            d = (me + i) % 16
+            ecopy(d, d).wait()
+            return 0
+
+        lax.fori_loop(1, 16, ew, 0)
+        for t in range(26):
+            s = ts[t]
+            blk = E[s // 2].astype(F32)
+            e = jnp.where(s % 2 == 1, blk[40:80], blk[0:40])
+            xT[39 * t : 39 * t + 39, :] = e[0:39]
+        xT[1014:1027, :] = R_["dns_v"][...].astype(BF).astype(F32)
+        xT[1027:LN, :] = jnp.zeros((LN - 1027, 384), F32)
+        for i in range(9):
+            c = slice(128 * i, 128 * i + 128)
+            xl[0, :, c] = xT[c, :].T.astype(BF)
+
+    def f_split():
+        core_wait("A")
+        for l in range(3):
+            for lo, n in CH:
+                w = G[:, 16 * l : 16 * l + 16, lo : lo + n].astype(F32).reshape(32, 2, 8, n)
+                VT[l, :, lo : lo + n] = w[:, 0].reshape(256, n).astype(BF)
+                UT[l, :, lo : lo + n] = w[:, 1].reshape(256, n).astype(BF)
+
+    def f_cross():
+        for l in range(3):
+            pr[l] = nt(xl[l], VT[l]).astype(BF)
+            for lo, n in CH:
+                q = nn(pr[l], UT[l, :, lo : lo + n]) + bia[l : l + 1, lo : lo + n]
+                qc[l, :, lo : lo + n] = q
+                v = x0(lo, n) * q + (x0(lo, n) if l == 0 else xr[:, lo : lo + n])
+                if l < 2:
+                    xr[:, lo : lo + n] = v
+                xl[l + 1, :, lo : lo + n] = v.astype(BF)
+
+    def f_tower_one():
+        core_wait("I")
+        for n in range(4):
+            c = slice(256 * n, 256 * n + 256)
+            a = nt(xl[3], G[8 * n : 8 * n + 8, 48:80, :].reshape(256, LN)) + bia[3:4, c]
+            a1[:, c] = a
+            h1[:, c] = (a * sig(a)).astype(BF)
+
+    def f_tower_two():
+        for q in PARTS:
+            if q not in "AI":
+                core_wait(q)
+        for n in range(4):
+            c = slice(256 * n, 256 * n + 256)
+            a = nt(h1[...], G[8 * n : 8 * n + 8, 80:112, 0:1024].reshape(256, 1024)) + bia[4:5, c]
+            a2[:, c] = a
+            h2[:, c] = (a * sig(a)).astype(BF)
+
+    plain = {"prep": f_prep, "x0": f_rows, "dei": f_split, "cf": f_cross, "a1": f_tower_one, "a2": f_tower_two}
+    step_of = lambda c: -1 if c == "-" else int(c)
+    todo = list(FORWARD)
+    while todo:
+        op = todo.pop(0)
+        if op in plain:
+            plain[op]()
+        elif op[0] == "L":
+            a = b = int(op[1:])
+            while todo and todo[0][0] == "L":
+                b = int(todo.pop(0)[1:])
+            looks(a, b + 1)
+        elif op[:3] == "own":
+            f_own(op[3])
+        elif op[:3] == "cor":
+            f_core(op[3])
+        elif op[:2] == "fz" and op[2] in LAST_Z:
+            for c in range(4):
+                fwd_zl(op[2], int(op[3]), c)
+        elif op[:2] == "fz":
+            fwd_z(op[2], int(op[3]))
+        elif op[:2] == "f1":
+            fwd_1(op[2], step_of(op[3]))
+        else:
+            fwd_2(op[2], step_of(op[3]), int(op[4]))
     hc = G[:, 80:112, 1024:LN].reshape(1024, 128)
     zl = nn(h2[...], hc) + bia[5:6, 0:128]
-    yl = jnp.broadcast_to(R_["lab_v"][...].astype(F32), (128, 384)).T
+    yl = jnp.broadcast_to(R_["lab_v"][...].reshape(1, 384).astype(F32), (128, 384)).T
     lossv = jnp.maximum(zl, 0.0) + jnp.log1p(jnp.exp(-jnp.abs(zl))) - yl * zl
     dz = (sig(zl) - yl) / total
     M[...] = jnp.zeros_like(M)
@@ -603,19 +697,22 @@
         a, b, pa, pb = axes(n)
         st[n].wait_recv()
         g, c = R_["g_" + n], R_["C_" + n]
-        g[r, 1 - a] = (g[r, 1 - a].astype(F32) + c[1 - a].astype(F32)).astype(BF)
-        st[n] = go(g.at[r, 1 - a], R_["P_" + n], pa)
+        st[n] = []
+        for bb in (1 - b, b):
+            g[r, 1 - a, bb] = (g[r, 1 - a, bb].astype(F32) + c[1 - a, bb].astype(F32)).astype(BF)
+            st[n].append(go(g.at[r, 1 - a, bb], R_["P_" + n].at[bb], pa))
 
     def s2(n):
         a, b, pa, pb = axes(n)
-        st[n].wait_recv()
+        st[n][0].wait_recv()
         g, c, p = R_["g_" + n], R_["C_" + n], R_["P_" + n]
         g[r, a, 1 - b] = (g[r, a, 1 - b].astype(F32) + c[a, 1 - b].astype(F32) + p[1 - b].astype(F32)).astype(BF)
-        st[n] = go(g.at[r, a, 1 - b], R_["Q_" + n], pb)
+        st[n].append(go(g.at[r, a, 1 - b], R_["Q_" + n], pb))
 
     def s3(n):
         a, b, pa, pb = axes(n)
-        st[n].wait_recv()
+        st[n][1].wait_recv()
+        st[n][2].wait_recv()
         g, c, p, q = R_["g_" + n], R_["C_" + n], R_["P_" + n], R_["Q_" + n]
         st[n] = []
         for i, zz in enumerate(zp):
@@ -627,159 +724,165 @@
         for c in st[n]:
             c.wait_recv()
         g, c, p, q, t = R_["g_" + n], R_["C_" + n], R_["P_" + n], R_["Q_" + n], R_["T_" + n]
-        R_["o_" + n][...] = (
+        nb, _, _, out, at = ITEMS[n]
+        R_["o_" + out][at : at + nb] = (
             g[r, a, b, z].astype(F32) + c[a, b, z].astype(F32) + p[b, z].astype(F32) + q[z].astype(F32)
             + (t[0].astype(F32) + t[1].astype(F32) + t[2].astype(F32)))
 
-    def put(n, base, g):
-        nb, _, yfirst = ITEMS[n]
-        for i in range(g.shape[0] // nb):
-            rep, xx, yy, zz = place(base + i)
-            a, b = (yy, xx) if yfirst else (xx, yy)
-            R_["g_" + n][rep, a, b, zz] = g[i * nb : i * nb + nb].astype(BF)
-
-    for n in range(4):
-        put("m", 8 * n, tn(d2[:, 256 * n : 256 * n + 256], h1[...]))
-    s0("m")
-    for n in range(4):
-        c = slice(256 * n, 256 * n + 256)
-        a1[:, c] = nn(d2[...], G[:, 80:112, c].reshape(1024, 256)) * slope(a1[:, c])
-    for n in range(4):
-        c = slice(256 * n, 256 * n + 256)
-        g = a1[:, c].astype(BF)
-        d1[:, c] = g
-        M[3:4, c] = jnp.sum(g.astype(F32), axis=0, keepdims=True)
-    s1("m")
-    for n in range(4):
-        put("i", 8 * n, tn(d1[:, 256 * n : 256 * n + 256], xl[3]))
-    s0("i")
-    for lo, n in CH:
-        dx[:, lo : lo + n] = nn(d1[...], G[:, 48:80, lo : lo + n].reshape(1024, n))
-
-    def cross_back(l):
+    def parts_of(out):
+        return [n for n in ITEMS if ITEMS[n][3] == out]
+
+    def put(out, base, g):
+        for n in parts_of(out):
+            nb, _, yfirst, _, at = ITEMS[n]
+            for i in range(g.shape[0] // 32):
+                rep, xx, yy, zz = place(base + i)
+                a, b = (yy, xx) if yfirst else (xx, yy)
+                R_["g_" + n][rep, a, b, zz] = g[i * 32 + at : i * 32 + at + nb].astype(BF)
+
+    MS, MX = R_["MS"], R_["MX"]
+
+    def grad_mid():
+        for n in range(4):
+            put("m", 8 * n, tn(d2[:, 256 * n : 256 * n + 256], h1[...]))
+        for n in parts_of("m"):
+            s0(n)
+
+    def down_one():
+        for n in range(4):
+            c = slice(256 * n, 256 * n + 256)
+            a1[:, c] = nn(d2[...], G[:, 80:112, c].reshape(1024, 256)) * slope(a1[:, c])
+        for n in range(4):
+            c = slice(256 * n, 256 * n + 256)
+            g = a1[:, c].astype(BF)
+            d1[:, c] = g
+            M[3:4, c] = jnp.sum(g.astype(F32), axis=0, keepdims=True)
+
+    def grad_in():
+        for n in range(4):
+            put("i", 8 * n, tn(d1[:, 256 * n : 256 * n + 256], xl[3]))
+        for n in parts_of("i"):
+            s0(n)
+
+    def down_x():
+        for lo, n in CH:
+            dx[:, lo : lo + n] = nn(d1[...], G[:, 48:80, lo : lo + n].reshape(1024, n))
+
+    def chain(l):
+        dq_ref = dql.at[l]
         for lo, n in CH:
             g = dx[:, lo : lo + n]
             dq = g * x0(lo, n)
             M[l : l + 1, lo : lo + n] = jnp.sum(dq, axis=0, keepdims=True)
-            dql[:, lo : lo + n] = dq.astype(BF)
+            dq_ref[:, lo : lo + n] = dq.astype(BF)
             e = g * qc[l, :, lo : lo + n]
             d0[:, lo : lo + n] = e if l == 2 else d0[:, lo : lo + n] + e
-        dpr[...] = nt(dql[...], UT[l]).astype(BF)
+        dpr[l] = nt(dq_ref[...], UT[l]).astype(BF)
+        for lo, n in CH:
+            v = dx[:, lo : lo + n] + nn(dpr[l], VT[l, :, lo : lo + n])
+            if l:
+                dx[:, lo : lo + n] = v
+            else:
+                d0[:, lo : lo + n] = d0[:, lo : lo + n] + v
+        if l == 0:
+            st["M"] = go(M, R_["MC"], core)
+
+    def cross_grads(l):
         gr = R_["g_c%d" % l]
         yfirst = ITEMS["c%d" % l][2]
         for lo, n in CH:
-            gu = tn(pr[l], dql[:, lo : lo + n]).reshape(32, 8, n)
-            gv = tn(dpr[...], xl[l, :, lo : lo + n]).reshape(32, 8, n)
+            gu = tn(pr[l], dql[l, :, lo : lo + n]).reshape(32, 8, n)
+            gv = tn(dpr[l], xl[l, :, lo : lo + n]).reshape(32, 8, n)
             gg = jnp.concatenate([gv, gu], axis=1).astype(BF)
             for k in range(32):
                 rep, xx, yy, zz = place(k)
                 a, b = (yy, xx) if yfirst else (xx, yy)
                 gr[rep, a, b, zz, :, lo : lo + n] = gg[k]
-
-    def cross_down(l):
-        for lo, n in CH:
-            v = dx[:, lo : lo + n] + nn(dpr[...], VT[l, :, lo : lo + n])
-            if l:
-                dx[:, lo : lo + n] = v
-            else:
-                d0[:, lo : lo + n] = d0[:, lo : lo + n] + v
-
-    cross_back(2)
-    s0("c2")
-    s1("i")
-    cross_down(2)
-    cross_back(1)
-    s0("c1")
-    s1("c2")
-    cross_down(1)
-    cross_back(0)
-    s0("c0")
-    cm = go(M, R_["MC"], core)
-    s1("c1")
-    cross_down(0)
-    for i in range(9):
-        c = slice(128 * i, 128 * i + 128)
-        xT[c, :] = d0[:, c].T
-    for t in range(26):
-        DE[t] = jnp.concatenate([xT[39 * t : 39 * t + 39, :], jnp.zeros((1, 384), F32)], axis=0)
-    DE[26] = jnp.zeros((40, 384), F32)
+        s0("c%d" % l)
 
     def back_rows(d):
         return jnp.concatenate([DE[inv[2 * d]], DE[inv[2 * d + 1]]], axis=0).astype(BF)
 
-    def dstep(i, _):
-        d = (me + i) % 16
-        eout[d] = back_rows(d)
-        dcopy(d, me).start()
-        return 0
-
-    lax.fori_loop(1, 16, dstep, 0)
-    D[me] = back_rows(me)
-    s1("c0")
-    MS, MX = R_["MS"], R_["MX"]
-    cm.wait_recv()
-    MS[0] = M[...] + R_["MC"][...]
-    m1 = go(MS.at[0], MX.at[0], xpeer)
-    R[...] = jnp.zeros_like(R)
+    def rows_out():
+        for i in range(9):
+            c = slice(128 * i, 128 * i + 128)
+            xT[c, :] = d0[:, c].T
+        for t in range(26):
+            DE[t] = jnp.concatenate([xT[39 * t : 39 * t + 39, :], jnp.zeros((1, 384), F32)], axis=0)
+        DE[26] = jnp.zeros((40, 384), F32)
+
+        def dstep(i, _):
+            d = nth(i)
+            eout[d] = back_rows(d)
+
+            @pl.when(i != 12)
+            def _():
+                dcopy(d, me).start()
+            return 0
+
+        lax.fori_loop(0, 16, dstep, 0)
+        D[me] = eout[me]
 
     def one_part(i, s):
-        d = (me + i) % 16
+        d = nth(15 - i)
         ids = id_rows(d)[s : s + 1]
         lo, hi = ids % 512, ids // 512
         e = D[d].astype(F32)[40 * s : 40 * s + 40]
         lhs = jnp.concatenate([jnp.where(hi == g, e, 0.0) for g in range(8)], axis=0).astype(BF)
         return lhs, one_hot(lo)
 
-    def rows_in(a, b):
-        def acc(i2, _):
-            for j in range(2):
-                i = 2 * i2 + j
-                d = (me + i) % 16
-
-                @pl.when(i > 0)
-                def _():
-                    dcopy(d, d).wait_recv()
-            for s in range(2):
-                u, v = one_part(2 * i2, s), one_part(2 * i2 + 1, s)
-                R[s] += nt(jnp.concatenate([u[0], v[0]], axis=1), jnp.concatenate([u[1], v[1]], axis=1))
-            return 0
-        lax.fori_loop(a, b, acc, 0)
-
-    s2("m")
-    m1.wait_recv()
-    MS[1] = MS[0] + MX[0]
-    m2 = go(MS.at[1], MX.at[1], ypeer)
-    rows_in(0, 1)
-    s2("i")
-    m2.wait_recv()
-    MS[2] = MS[1] + MX[1]
-    m3 = [go(MS.at[2], MX.at[2 + i], zpeer[i]) for i in range(3)]
-    rows_in(1, 2)
-    s2("c2")
-    s3("m")
-    rows_in(2, 4)
-    s2("c1")
-    s3("i")
-    rows_in(4, 6)
-    s2("c0")
-    s3("c2")
-    rows_in(6, 8)
-    for s in range(2):
-        for j in range(32):
-            g, h = j // 4, j % 4
-            gt[pl.ds(2 * j + s, 39, stride=64), :] = R[s, g * 40 : g * 40 + 39, h * 128 : (h + 1) * 128]
-    cg = go(gt, gtc, core)
-    s3("c1")
-    s3("c0")
-    for c in m3:
-        c.wait_recv()
-    pos = [MS[2], MX[2], MX[3], MX[4]]
-    u = jnp.where(z % 2 == 0, pos[0], pos[1]) + jnp.where(z % 2 == 0, pos[1], pos[0])
-    v = jnp.where(z % 2 == 0, pos[2], pos[3]) + jnp.where(z % 2 == 0, pos[3], pos[2])
-    MO[...] = jnp.where(z < 2, u, v) + jnp.where(z < 2, v, u)
-    for n in ORDER:
-        s4(n)
-    cg.wait_recv()
+    def rows_in(k):
+        for i in (2 * k, 2 * k + 1):
+            if i != 3:
+                d = nth(15 - i)
+                dcopy(d, d).wait_recv()
+        for s in range(2):
+            u, v = one_part(2 * k, s), one_part(2 * k + 1, s)
+            p = nt(jnp.concatenate([u[0], v[0]], axis=1), jnp.concatenate([u[1], v[1]], axis=1))
+            R[s] = p if k == 0 else R[s] + p
+
+    def table_sum():
+        for s in range(2):
+            for j in range(32):
+                g, h = j // 4, j % 4
+                gg_[pl.ds(2 * j + s, 39, stride=64), :] = R[s, g * 40 : g * 40 + 39, h * 128 : (h + 1) * 128]
+        st["g"] = go(gg_, gtc, core)
+
+    def table_both():
+        st["g"].wait_recv()
+        gt[...] = gg_[...] + gtc[...]
+
+    def small(i):
+        if i == 1:
+            st["M"].wait_recv()
+            MS[0] = M[...] + R_["MC"][...]
+            st["M"] = go(MS.at[0], MX.at[0], xpeer)
+        elif i == 2:
+            st["M"].wait_recv()
+            MS[1] = MS[0] + MX[0]
+            st["M"] = go(MS.at[1], MX.at[1], ypeer)
+        elif i == 3:
+            st["M"].wait_recv()
+            MS[2] = MS[1] + MX[1]
+            st["M"] = [go(MS.at[2], MX.at[2 + j], zpeer[j]) for j in range(3)]
+        else:
+            for c in st["M"]:
+                c.wait_recv()
+            pos = [MS[2], MX[2], MX[3], MX[4]]
+            u = jnp.where(z % 2 == 0, pos[0], pos[1]) + jnp.where(z % 2 == 0, pos[1], pos[0])
+            v = jnp.where(z % 2 == 0, pos[2], pos[3]) + jnp.where(z % 2 == 0, pos[3], pos[2])
+            MO[...] = jnp.where(z < 2, u, v) + jnp.where(z < 2, v, u)
+
+    stage = {"s1": s1, "s2": s2, "s3": s3, "s4": s4}
+    plain = {"dTm": grad_mid, "dh1": down_one, "dTi": grad_in, "dx3": down_x, "D": rows_out, "gt": table_sum, "gts": table_both}
+    indexed = {"ch": chain, "cg": cross_grads, "sc": rows_in, "M": small}
+    for op in BACKWARD:
+        if op in plain:
+            plain[op]()
+        elif op[:2] in stage:
+            stage[op[:2]](op[2:])
+        else:
+            indexed[op[:-1]](int(op[-1]))
 
     def dw(i, _):
         d = (me + i) % 16
@@ -790,33 +893,38 @@
     for c in sends:
         c.wait_send()
 
-
-def mega(total, ts, inv, ids, tab, cr, ti, tm, hd, dns, lab, bia):
+    @pl.when(inner)
+    def _():
+        for c in isends:
+            c.wait_send()
+
+
+def mega(total, ts, ids, tab, cr, ti, tm, hd, dns, lab, bi):
     V, S = pltpu.VMEM, jax.ShapeDtypeStruct
     vm, sm, an = pl.BlockSpec(memory_space=pltpu.VMEM), pl.BlockSpec(memory_space=pltpu.SMEM), pl.BlockSpec(memory_space=pl.ANY)
-    ins = {"ts": ts, "inv": inv, "bia": bia, "ids": ids, "tab": tab, "cr": cr, "ti": ti, "tm": tm, "hd": hd, "dns": dns, "lab": lab}
-    outs = {"gt": S((2496, 128), F32), "gtc": S((2496, 128), F32), "MO": S((8, LN), F32)}
-    for n in ORDER:
-        outs["o_" + n] = S(ITEMS[n][:2], F32)
-    scr = {n + "_v": V(ins[n].shape, ins[n].dtype) for n in ("ids", "tab", "cr", "ti", "tm", "hd", "dns", "lab")}
+    ins = {"ts": ts, "ids": ids, "tab": tab, "cr": cr, "ti": ti, "tm": tm, "hd": hd, "dns": dns, "lab": lab, "bi": bi}
+    outs = {"gt": S((2496, 128), F32), "MO": S((8, LN), F32)}
+    for n in SUMS:
+        outs["o_" + n] = S(SUMS[n], F32)
+    scr = {n + "_v": V(ins[n].shape, ins[n].dtype) for n in ("ids", "cr", "ti", "tm", "hd", "dns", "lab", "bi")}
     scr.update(
         G=V((32, RB, LN), BF), E=V((16, 80, 384), BF), D=V((16, 80, 384), BF), eout=V((16, 80, 384), BF), tabr=V((2, 320, 512), BF),
         xT=V((LN, 384), F32), dx=V((384, LN), F32), xl=V((4, 384, LN), BF), qc=V((3, 384, LN), F32), pr=V((3, 384, 256), BF),
-        VT=V((3, 256, LN), BF), UT=V((3, 256, LN), BF), a1=V((384, 1024), F32), a2=V((384, 1024), F32), h1=V((384, 1024), BF), h2=V((384, 1024), BF),
-        d0=V((384, LN), F32), dql=V((384, LN), BF), dpr=V((384, 256), BF), DE=V((27, 40, 384), F32), M=V((8, LN), F32), R=V((2, 320, 512), F32),
-        MC=V((8, LN), F32), MS=V((3, 8, LN), F32), MX=V((5, 8, LN), F32))
+        VT=V((3, 256, LN), BF), UT=V((3, 256, LN), BF), h1=V((384, 1024), BF), h2=V((384, 1024), BF),
+        d0=V((384, LN), F32), dql=V((3, 384, LN), BF), dpr=V((3, 384, 256), BF), DE=V((27, 40, 384), F32), M=V((8, LN), F32), R=V((2, 320, 512), F32),
+        MC=V((8, LN), F32), MS=V((3, 8, LN), F32), MX=V((5, 8, LN), F32), gg=V((2496, 128), F32), gtc=V((2496, 128), F32), bia=V((8, LN), F32), inv=pltpu.SMEM((32,), jnp.int32))
     for n in ORDER:
-        nb, L, _ = ITEMS[n]
+        nb, L = ITEMS[n][:2]
         scr["g_" + n] = V((2, 2, 2, 4, nb, L), BF)
         scr["C_" + n] = V((2, 2, 4, nb, L), BF)
         scr["P_" + n] = V((2, 4, nb, L), BF)
         scr["Q_" + n] = V((4, nb, L), BF)
         scr["T_" + n] = V((3, nb, L), BF)
     dma = pltpu.SemaphoreType.DMA
-    scr.update(lsem=dma((8,)), wss=dma((2, 32)), wrs=dma((2, 32)), ess=dma((16,)), ers=dma((16,)), dss=dma((16,)), drs=dma((16,)), rss=dma((40,)), rrs=dma((40,)))
+    scr.update(lsem=dma((9,)), wss=dma((3, 40)), wrs=dma((3, 32)), ess=dma((16,)), ers=dma((16,)), dss=dma((16,)), drs=dma((16,)), rss=dma((64,)), rrs=dma((64,)))
     res = pl.pallas_call(
         functools.partial(mega_body, total, list(ins), list(outs), list(scr)), name="train_step",
-        out_shape=tuple(outs.values()), in_specs=[sm, sm, vm] + [an] * 8, out_specs=(vm,) * len(outs),
+        out_shape=tuple(outs.values()), in_specs=[sm] + [an] * 9, out_specs=(vm,) * len(outs),
         scratch_shapes=list(scr.values()),
         compiler_params=pltpu.CompilerParams(collective_id=0, has_side_effects=True, vmem_limit_bytes=63 << 20),
     )(*ins.values())
@@ -830,6 +938,9 @@
     mn = 0.5 * m + 0.5 * g
     vn = 0.5 * v + 0.5 * g * g
     return w - rate * ((mn / C5) / (jnp.sqrt(vn / C5) + EPSILON) + WEIGHT_DECAY * w), mn, vn
+
+
+SMALL = [k + q for k in "hb" for q in "wnv"]
 
 
 def update_body(names_in, names_out, names_scr, *refs):
@@ -838,9 +949,14 @@
     rc, isem, osem = R_["rc"], R_["isem"], R_["osem"]
     order = [k + q for k in "tcim" for q in "wnv"]
     ld = {}
-    for i, n in enumerate(order + ["gt", "gtc"]):
-        ld[n] = pltpu.make_async_copy(R_[n], R_["v_" + n], isem.at[i])
+    for n in SMALL + order[3:]:
+        ld[n] = pltpu.make_async_copy(R_[n], R_["v_" + n], isem.at[len(ld)])
         ld[n].start()
+    for part in range(3):
+        for n in ("tw", "tn", "tv", "gt"):
+            q = pl.ds(832 * part, 832)
+            ld[n, part] = pltpu.make_async_copy(R_[n].at[q], R_["v_" + n].at[q], isem.at[len(ld)])
+            ld[n, part].start()
     outs = []
 
     def out(name, rows=None):
@@ -852,6 +968,19 @@
         c.start()
         outs.append(c)
 
+    for n in SMALL:
+        ld[n].wait()
+    MO = R_["MO"]
+    R_["o_loss"][0, 0] = jnp.max(MO[6:7, 0:128])
+    k = lax.axis_index("dp") * 2 + lax.axis_index("rep")
+    gb = jnp.concatenate([MO[0:1, :WIDTH], MO[1:2, :WIDTH], MO[2:3, :WIDTH], MO[3:4, :1024], MO[4:5, :1024], MO[7:8, :1]], axis=1)
+    gh = pltpu.roll(MO[5:6, 0:1024], 1024 - 32 * k, 1)[:, 0:32]
+    for kk, g, rate in (("h", gh, RATE_DENSE), ("b", gb, RATE_BIAS)):
+        n = g.shape[1]
+        w, m, v = adamw(*(R_["v_" + kk + q][...].reshape(1, n) for q in "wnv"), g, rate)
+        for q, a in (("w", w), ("n", m), ("v", v), ("l", w.astype(BF))):
+            R_["u_" + kk + q][...] = a.reshape(n)
+            out(kk + q)
     rows = {"c": [("c0", 0, 16), ("c1", 16, 16), ("c2", 32, 16)], "i": [("i", 0, 32)], "m": [("m", 0, 32)]}
     for k in "imc":
         for q in "wnv":
@@ -863,23 +992,25 @@
             R_["u_" + k + "w"][at], R_["u_" + k + "n"][at], R_["u_" + k + "v"][at], R_["u_" + k + "l"][at] = w, m, v, w.astype(BF)
         for q in "wnvl":
             out(k + q)
-    for n in ("tw", "tn", "tv", "gt", "gtc"):
-        ld[n].wait()
     row = lax.broadcasted_iota(jnp.int32, (64, 128), 0)
     lane = lax.broadcasted_iota(jnp.int32, (64, 128), 1)
     use = ((row // 2) * 128 + lane) < jnp.where(row % 2 == 0, rc[0], rc[1])
     for part in range(3):
-        def tab(c, _):
-            q = pl.ds(pl.multiple_of(c * 64, 64), 64)
+        for n in ("tw", "tn", "tv", "gt"):
+            ld[n, part].wait()
+
+        def tab(c, at):
+            q = pl.ds(pl.multiple_of(at + c * 64, 64), 64)
             w, m, v = R_["v_tw"][q], R_["v_tn"][q], R_["v_tv"][q]
-            nw, nm, nv = adamw(w, m, v, R_["v_gt"][q] + R_["v_gtc"][q], RATE_TABLE)
+            nw, nm, nv = adamw(w, m, v, R_["v_gt"][q], RATE_TABLE)
             nw = jnp.where(use, nw, w)
             R_["u_tw"][q] = nw
             R_["u_tn"][q] = jnp.where(use, nm, m)
             R_["u_tv"][q] = jnp.where(use, nv, v)
             R_["u_tl"][q] = nw.astype(BF)
-            return 0
-        lax.fori_loop(13 * part, 13 * part + 13, tab, 0)
+
+        for c in range(13):
+            tab(c, 832 * part)
         for q in "wnvl":
             out("t" + q, pl.ds(832 * part, 832))
     for c in outs:
@@ -890,18 +1021,17 @@
     V, S = pltpu.VMEM, jax.ShapeDtypeStruct
     vm, sm, an = pl.BlockSpec(memory_space=pltpu.VMEM), pl.BlockSpec(memory_space=pltpu.SMEM), pl.BlockSpec(memory_space=pl.ANY)
     ins, specs = {"rc": rc}, [sm]
-    for k in "tcim":
+    for k in "tcimhb":
         for q, a in zip("wnv", state[k]):
             ins[k + q] = a
             specs.append(an)
-    for n in ("gt", "gtc"):
-        ins[n] = g[n]
-        specs.append(an)
-    for n in ORDER:
+    ins["gt"], ins["MO"] = g["gt"], g["MO"]
+    specs += [an, vm]
+    for n in SUMS:
         ins["g_" + n] = g["o_" + n]
         specs.append(vm)
     outs, scr = {}, {}
-    for k in "tcim":
+    for k in "tcimhb":
         for q in "wnvl":
             shape, kind = state[k][0].shape, BF if q == "l" else F32
             outs["o_" + k + q] = S(shape, kind)
@@ -909,12 +1039,12 @@
             if q != "l":
                 scr["v_" + k + q] = V(shape, kind)
     scr["v_gt"] = V((2496, 128), F32)
-    scr["v_gtc"] = V((2496, 128), F32)
-    scr["isem"] = pltpu.SemaphoreType.DMA((14,))
-    scr["osem"] = pltpu.SemaphoreType.DMA((24,))
+    outs["o_loss"] = S((1, 1), F32)
+    scr["isem"] = pltpu.SemaphoreType.DMA((27,))
+    scr["osem"] = pltpu.SemaphoreType.DMA((32,))
     return pl.pallas_call(
         functools.partial(update_body, list(ins), list(outs), list(scr)), name="adamw_step",
-        out_shape=tuple(outs.values()), in_specs=specs, out_specs=(an,) * len(outs), scratch_shapes=list(scr.values()),
+        out_shape=tuple(outs.values()), in_specs=specs, out_specs=(an,) * (len(outs) - 1) + (sm,), scratch_shapes=list(scr.values()),
         compiler_params=pltpu.CompilerParams(vmem_limit_bytes=63 << 20),
     )(*ins.values())
 
@@ -943,34 +1073,18 @@
         "i": [a.T for a in (tower_in, tower_in_m, tower_in_v)],
         "m": [a.T for a in (tower_mid, tower_mid_m, tower_mid_v)],
     }
-    hits = table_slot[None, :] == jnp.arange(32, dtype=jnp.int32)[:, None]
-    inv = TABLES - jnp.sum(hits * (TABLES - jnp.arange(TABLES, dtype=jnp.int32))[None, :], axis=1)
-    wide = lambda v: jnp.pad(v, (0, LN - v.shape[0]))
-    at = LAYERS * WIDTH
-    bia = jnp.stack(
-        [wide(biases[WIDTH * i : WIDTH * i + WIDTH]) for i in range(3)]
-        + [wide(biases[at : at + 1024]), wide(biases[at + 1024 : at + 2048]),
-           jnp.broadcast_to(biases[at + 2048], (LN,)), jnp.zeros((LN,), F32), jnp.zeros((LN,), F32)]
-    )
-    g = mega(total, table_slot, inv, event_ids, state["t"][0], state["c"][0], state["i"][0], state["m"][0],
-             head_weight.reshape(1, 32), dense_input.T, labels.reshape(1, 384), bia)
+    state["h"] = [head_weight, head_m, head_v]
+    state["b"] = [biases, biases_m, biases_v]
+    g = mega(total, table_slot, event_ids, state["t"][0], state["c"][0], state["i"][0], state["m"][0],
+             head_weight, dense_input.T, labels, biases)
     o = update(row_counts, g, state)
-    MO = g["MO"]
-    loss = MO[6, 0]
-    g_bias = jnp.concatenate([MO[0, :WIDTH], MO[1, :WIDTH], MO[2, :WIDTH], MO[3, :1024], MO[4, :1024], MO[7, :1]])
-    k = lax.axis_index("dp") * 2 + lax.axis_index("rep")
-    g_head = lax.dynamic_slice(MO[5], (k * 32,), (32,))
-    tail = []
-    for w, m, v, gg, rate in ((head_weight, head_m, head_v, g_head, RATE_DENSE), (biases, biases_m, biases_v, g_bias, RATE_BIAS)):
-        a, b, c = adamw_update(w, m, v, gg, rate)
-        tail += [a, b, c, a.astype(BF)]
     return (
-        loss,
+        o[24].reshape(()),
         *[tab_unview(a) for a in o[0:4]],
         *[back(a) for a in o[4:8]],
         *[a.T for a in o[8:12]],
         *[a.T for a in o[12:16]],
-        *tail,
+        *o[16:24],
     )
 
 

time: 156 us -> 134 us (0.86)
  Pallas kernels: 144 us -> 133 us
  local copies, waits for them, and re-layouts: 6.93 us -> 0 us
  other arithmetic: 3.27 us -> 0 us
    pallas_call x1, Pallas kernels: 137 us -> 125 us  [mega(): pl.pallas_call(functools.partial(mega_body, total, list(ins), list(outs),...]
    slice x7 -> x0, local copies, waits for them, and re-layouts: 3.55 us -> none  [the longest x1 1.27 us: fast_shards(): biases[at + 2048]]
where the time goes in v3:
time: 134 us
  Pallas kernels  133 us (99%)
    pallas_call x1, Pallas kernels, mega(): pl.pallas_call(functools.partial(mega_body, total, list(ins), list(outs),...  125 us
    pallas_call x1, Pallas kernels, update(): pl.pallas_call(functools.partial(update_body, list(ins), list(outs), list...  8.08 us

profile of v3, /device:TPU:0, one launch (start us, length us, event | category | flops | bytes accessed | tf_op | source)
XLA Modules:
  0.0 133.5 jit_solution(3026490585210729413)
XLA Ops:
  0.7 124.5 %train_step.1 = (f32[2496,128]{1,0:T(8,128)}, f32[8,1152]{1,0:T(8,128)}, f32[32,1024]{1,0:T(8,128)}, f32[32,1152]{1,0:T(8,128)}, f32[16,1152]{1,0:T(8,128)}, /*index=5*/f32[16,1152]{1,0:T(8,128)}, f32[16,1152]{1,0:T(8,128)}) custom-call(s32[26]{0:T(128)} %refs_0_.2, s32[2,12288]{1,0:T(2,128)} %refs_1_.1, f32[2496,128]{1,0:T(8,128)} %bitcast.86, ...), custom_call_target="tpu_custom_call" | custom-call | tf_op jit(solution)/shard_map/train_step/pallas_call | solution.py:925
  125.2 8.1 %adamw_step.1 = (f32[2496,128]{1,0:T(8,128)}, f32[2496,128]{1,0:T(8,128)}, f32[2496,128]{1,0:T(8,128)}, bf16[2496,128]{1,0:T(8,128)(2,1)}, f32[48,1027]{1,0:T(8,...) custom-call(s32[2]{0:T(128)} %refs_0_.3, ...), custom_call_target="tpu_custom_call" | custom-call | tf_op jit(solution)/shard_map/adamw_step/pallas_call | solution.py:1045

commit v4 on v3

--- a/solution.py
+++ b/solution.py
@@ -1,5 +1,6 @@
 import functools
 import math
+import types
 
 import jax
 import jax.numpy as jnp
@@ -326,30 +327,18 @@
 RB = 112
 BIASES = 5130
 CH = [(0, 256), (256, 256), (512, 256), (768, 256), (1024, 128)]
-ITEMS = {
-    "m0": (16, 1024, True, "m", 0),
-    "m1": (16, 1024, False, "m", 16),
-    "i": (32, LN, True, "i", 0),
-    "c2": (16, LN, False, "c2", 0),
-    "c1": (16, LN, True, "c1", 0),
-    "c0": (16, LN, False, "c0", 0),
-}
-ORDER = list(ITEMS)
-SUMS = {"m": (32, 1024), "i": (32, LN), "c2": (16, LN), "c1": (16, LN), "c0": (16, LN)}
-PARTS = {"A": (0, 48, True), "I": (48, 48, False), "U": (96, 16, False)}
-LAST_Z = "U"
-FORWARD = [
-    "ownU", "ownI", "ownA", "prep", "L0", "L1", "f1I-", "f1U-", "corU", "fzI0", "fzA0", "fzI1", "fzA1", "f1A-", "L2", "L3",
-    "f2U-1", "f2U-0", "fzI2", "f1A0", "corI", "f1I1", "L4", "L5", "L6", "fzA2", "f1A1", "fzU1", "fzU0", "f2A00", "f2I-0",
-    "L7", "L8", "f1I0", "f1I2", "f2I10", "corA", "L9", "fzU2", "f2A20", "L10", "f1A2", "f2A10", "f2A-0", "f2A11", "L11",
-    "f2I-1", "f2I20", "L12", "L13", "L14", "f2I01", "f2A-1", "f2A01", "L15", "f2I11", "f2A21", "f2I21", "dei", "f2I00",
-    "x0", "cf", "a1", "a2",
+M0, M1, IN, C2, C1, C0 = range(6)
+ITEMS = [
+    (16, 1024, True, 0, 0),
+    (16, 1024, False, 0, 16),
+    (32, LN, True, 1, 0),
+    (16, LN, False, 2, 0),
+    (16, LN, True, 3, 0),
+    (16, LN, False, 4, 0),
 ]
-BACKWARD = [
-    "dTm", "dh1", "dx3", "s1m0", "s1m1", "ch2", "cg2", "ch1", "ch0", "cg0", "s2m1", "M1", "D", "dTi", "s3m1", "M2", "s1c2",
-    "s1i", "cg1", "s2m0", "M3", "s2i", "s3m0", "s1c0", "s2c2", "s1c1", "s3i", "sc0", "sc1", "s4m1", "sc2", "sc3", "sc4",
-    "s4m0", "s3c2", "s2c1", "s2c0", "s3c1", "sc5", "sc6", "s3c0", "sc7", "s4c2", "gt", "M4", "s4c1", "s4i", "gts", "s4c0",
-]
+SUMS = [(32, 1024), (32, LN), (16, LN), (16, LN), (16, LN)]
+A, I, U = range(3)
+PARTS = [(0, 48, True), (48, 48, False), (96, 16, False)]
 
 
 def nt(a, b):
@@ -378,17 +367,17 @@
     return rep, d % 2, (d // 2) % 2, d // 4
 
 
-def mega_body(total, names_in, names_out, names_scr, *refs):
-    it = iter(refs)
-    R_ = {n: next(it) for n in names_in + names_out + names_scr}
-    ts, inv = R_["ts"], R_["inv"]
-    G, E, D, eout, tabr = R_["G"], R_["E"], R_["D"], R_["eout"], R_["tabr"]
-    xT, dx, xl, qc, pr = R_["xT"], R_["dx"], R_["xl"], R_["qc"], R_["pr"]
-    VT, UT, h1, h2 = R_["VT"], R_["UT"], R_["h1"], R_["h2"]
-    d0, dql, dpr, DE, M, R = R_["d0"], R_["dql"], R_["dpr"], R_["DE"], R_["M"], R_["R"]
-    ids_ref, tab_ref, bia = R_["ids_v"], R_["gg"], R_["bia"]
+def mega_body(total, names, *refs):
+    B = types.SimpleNamespace(**dict(zip(names, refs)))
+    buf = lambda kind, n: getattr(B, kind + str(n))
+    ts, inv = B.ts, B.inv
+    G, E, D, eout, tabr = B.G, B.E, B.D, B.eout, B.tabr
+    xT, dx, xl, qc, pr = B.xT, B.dx, B.xl, B.qc, B.pr
+    VT, UT, h1, h2 = B.VT, B.UT, B.h1, B.h2
+    d0, dql, dpr, DE, M, R = B.d0, B.dql, B.dpr, B.DE, B.M, B.R
+    ids_ref, tab_ref, bia = B.ids_v, B.gg, B.bia
     xr, a1, a2, d1, d2 = dx, dx, d0, h1, h2
-    gt, gg_, gtc, MO = R_["gt"], R_["gg"], R_["gtc"], R_["MO"]
+    gt, gg_, gtc, MO = B.gt, B.gg, B.gtc, B.MO
     me = lax.axis_index("dp")
     r = lax.axis_index("rep")
     x, y, z = me % 2, (me // 2) % 2, me // 4
@@ -398,19 +387,22 @@
     xpeer, ypeer, core = (dev(z, y, 1 - x), r), (dev(z, 1 - y, x), r), (me, 1 - r)
     zpeer = [(dev(q, y, x), r) for q in zp]
 
-    loads = {}
-    for i, n in enumerate(["cr", "ti", "tm", "hd", "tab", "ids", "dns", "lab", "bi"]):
-        c = pltpu.make_async_copy(R_[n], R_["gg" if n == "tab" else n + "_v"], R_["lsem"].at[i])
+    loads = [
+        pltpu.make_async_copy(src, dst, B.lsem.at[i])
+        for i, (src, dst) in enumerate(
+            ((B.cr, B.cr_v), (B.ti, B.ti_v), (B.tm, B.tm_v), (B.hd, B.hd_v), (B.tab, B.gg),
+             (B.ids, B.ids_v), (B.dns, B.dns_v), (B.lab, B.lab_v), (B.bi, B.bi_v)))
+    ]
+    for c in loads:
         c.start()
-        loads[n] = c
     bar = pltpu.get_barrier_semaphore()
     for i in range(1, 16):
         pl.semaphore_signal(bar, inc=1, device_id=((me + i) % 16, r), device_id_type=MESH)
     pl.semaphore_signal(bar, inc=1, device_id=core, device_id_type=MESH)
 
-    cr, ti, tm, hd = R_["cr_v"], R_["ti_v"], R_["tm_v"], R_["hd_v"]
-    for n in ("cr", "ti", "tm", "hd"):
-        loads[n].wait()
+    cr, ti, tm, hd = B.cr_v, B.ti_v, B.tm_v, B.hd_v
+    for c in loads[:4]:
+        c.wait()
     G[own, 0:48, 0:1024] = cr[:, 0:1024].astype(BF)
     G[own, 0:48, 1024:LN] = jnp.concatenate([cr[:, 1024:1027], jnp.zeros((48, 125), F32)], axis=1).astype(BF)
     G[own, 48:80, 0:1024] = ti[:, 0:1024].astype(BF)
@@ -421,15 +413,14 @@
     G[own, 80:112, 1024:LN] = jnp.broadcast_to(hcol, (32, 128)).astype(BF)
     pl.semaphore_wait(bar, 16)
 
-    cnt = {p: 0 for p in PARTS}
-    pnum = {p: i for i, p in enumerate(PARTS)}
+    cnt = [0, 0, 0]
     sends = []
 
     def wcopy(p, k, dst, si):
         lo, n, _ = PARTS[p]
         return pltpu.make_async_remote_copy(
             src_ref=G.at[k, pl.ds(lo, n)], dst_ref=G.at[k, pl.ds(lo, n)],
-            send_sem=R_["wss"].at[pnum[p], si], recv_sem=R_["wrs"].at[pnum[p], k], device_id=dst, device_id_type=MESH)
+            send_sem=B.wss.at[p, si], recv_sem=B.wrs.at[p, k], device_id=dst, device_id_type=MESH)
 
     def wsend(p, k, dst):
         c = wcopy(p, k, dst, cnt[p])
@@ -440,8 +431,8 @@
     def wwait(p, k):
         wcopy(p, k, core, 0).wait_recv()
 
-    p1 = {p: ypeer if PARTS[p][2] else xpeer for p in PARTS}
-    p2 = {p: xpeer if PARTS[p][2] else ypeer for p in PARTS}
+    p1 = [ypeer if p[2] else xpeer for p in PARTS]
+    p2 = [xpeer if p[2] else ypeer for p in PARTS]
     key = lambda zz, yy, xx: dev(zz, yy, xx) * 2 + r
     inner = (z == 1) | (z == 2)
     zq = [zp[0], jnp.where(inner, zp[2], zp[1]), jnp.where(inner, zp[1], zp[2])]
@@ -475,7 +466,7 @@
         wsend(p, k, core)
 
     def up_down(p, k):
-        if p in LAST_Z:
+        if p == U:
             wsend(p, k, (dev(zp[0], y, x), r))
             isend(p, k, zp[2])
 
@@ -507,8 +498,8 @@
         lax.fori_loop(0, 16, cw, 0)
 
     def f_prep():
-        loads["tab"].wait()
-        loads["ids"].wait()
+        loads[4].wait()
+        loads[5].wait()
         for s in range(2):
             for j in range(32):
                 g, h = j // 4, j % 4
@@ -536,11 +527,11 @@
 
     def ecopy(d, land):
         return pltpu.make_async_remote_copy(
-            src_ref=eout.at[d], dst_ref=E.at[land], send_sem=R_["ess"].at[d], recv_sem=R_["ers"].at[land], device_id=(d, r), device_id_type=MESH)
+            src_ref=eout.at[d], dst_ref=E.at[land], send_sem=B.ess.at[d], recv_sem=B.ers.at[land], device_id=(d, r), device_id_type=MESH)
 
     def dcopy(d, land):
         return pltpu.make_async_remote_copy(
-            src_ref=eout.at[d], dst_ref=D.at[land], send_sem=R_["dss"].at[d], recv_sem=R_["drs"].at[land], device_id=(d, r), device_id_type=MESH)
+            src_ref=eout.at[d], dst_ref=D.at[land], send_sem=B.dss.at[d], recv_sem=B.drs.at[land], device_id=(d, r), device_id_type=MESH)
 
     def nth(i):
         j, w = i // 4, i % 4
@@ -567,16 +558,16 @@
             for t in range(TABLES):
                 slot_table = jnp.where(ts[t] == n, t, slot_table)
             inv[n] = slot_table
-        loads["bi"].wait()
-        bv = R_["bi_v"][...].reshape(1, BIASES)
+        loads[8].wait()
+        bv = B.bi_v[...].reshape(1, BIASES)
         bia[...] = jnp.zeros_like(bia)
         for i in range(3):
             bia[i : i + 1, 0:1027] = bv[:, 1027 * i : 1027 * i + 1027]
         bia[3:4, 0:1024] = bv[:, 3081:4105]
         bia[4:5, 0:1024] = bv[:, 4105:5129]
         bia[5:6, :] = jnp.broadcast_to(bv[:, 5129:5130], (1, LN))
-        loads["dns"].wait()
-        loads["lab"].wait()
+        loads[6].wait()
+        loads[7].wait()
 
         def ew(i, _):
             d = (me + i) % 16
@@ -589,14 +580,14 @@
             blk = E[s // 2].astype(F32)
             e = jnp.where(s % 2 == 1, blk[40:80], blk[0:40])
             xT[39 * t : 39 * t + 39, :] = e[0:39]
-        xT[1014:1027, :] = R_["dns_v"][...].astype(BF).astype(F32)
+        xT[1014:1027, :] = B.dns_v[...].astype(BF).astype(F32)
         xT[1027:LN, :] = jnp.zeros((LN - 1027, 384), F32)
         for i in range(9):
             c = slice(128 * i, 128 * i + 128)
             xl[0, :, c] = xT[c, :].T.astype(BF)
 
     def f_split():
-        core_wait("A")
+        core_wait(A)
         for l in range(3):
             for lo, n in CH:
                 w = G[:, 16 * l : 16 * l + 16, lo : lo + n].astype(F32).reshape(32, 2, 8, n)
@@ -615,7 +606,7 @@
                 xl[l + 1, :, lo : lo + n] = v.astype(BF)
 
     def f_tower_one():
-        core_wait("I")
+        core_wait(I)
         for n in range(4):
             c = slice(256 * n, 256 * n + 256)
             a = nt(xl[3], G[8 * n : 8 * n + 8, 48:80, :].reshape(256, LN)) + bia[3:4, c]
@@ -623,43 +614,83 @@
             h1[:, c] = (a * sig(a)).astype(BF)
 
     def f_tower_two():
-        for q in PARTS:
-            if q not in "AI":
-                core_wait(q)
+        core_wait(U)
         for n in range(4):
             c = slice(256 * n, 256 * n + 256)
             a = nt(h1[...], G[8 * n : 8 * n + 8, 80:112, 0:1024].reshape(256, 1024)) + bia[4:5, c]
             a2[:, c] = a
             h2[:, c] = (a * sig(a)).astype(BF)
 
-    plain = {"prep": f_prep, "x0": f_rows, "dei": f_split, "cf": f_cross, "a1": f_tower_one, "a2": f_tower_two}
-    step_of = lambda c: -1 if c == "-" else int(c)
-    todo = list(FORWARD)
-    while todo:
-        op = todo.pop(0)
-        if op in plain:
-            plain[op]()
-        elif op[0] == "L":
-            a = b = int(op[1:])
-            while todo and todo[0][0] == "L":
-                b = int(todo.pop(0)[1:])
-            looks(a, b + 1)
-        elif op[:3] == "own":
-            f_own(op[3])
-        elif op[:3] == "cor":
-            f_core(op[3])
-        elif op[:2] == "fz" and op[2] in LAST_Z:
-            for c in range(4):
-                fwd_zl(op[2], int(op[3]), c)
-        elif op[:2] == "fz":
-            fwd_z(op[2], int(op[3]))
-        elif op[:2] == "f1":
-            fwd_1(op[2], step_of(op[3]))
-        else:
-            fwd_2(op[2], step_of(op[3]), int(op[4]))
+    f_own(U)
+    f_own(I)
+    f_own(A)
+    f_prep()
+    looks(0, 1)
+    looks(1, 2)
+    fwd_1(I, -1)
+    fwd_1(U, -1)
+    f_core(U)
+    fwd_z(I, 0)
+    fwd_z(A, 0)
+    fwd_z(I, 1)
+    fwd_z(A, 1)
+    fwd_1(A, -1)
+    looks(2, 3)
+    looks(3, 4)
+    fwd_2(U, -1, 1)
+    fwd_2(U, -1, 0)
+    fwd_z(I, 2)
+    fwd_1(A, 0)
+    f_core(I)
+    fwd_1(I, 1)
+    looks(4, 5)
+    looks(5, 6)
+    looks(6, 7)
+    fwd_z(A, 2)
+    fwd_1(A, 1)
+    for c in range(4):
+        fwd_zl(U, 1, c)
+    for c in range(4):
+        fwd_zl(U, 0, c)
+    fwd_2(A, 0, 0)
+    fwd_2(I, -1, 0)
+    looks(7, 8)
+    looks(8, 9)
+    fwd_1(I, 0)
+    fwd_1(I, 2)
+    fwd_2(I, 1, 0)
+    f_core(A)
+    looks(9, 10)
+    for c in range(4):
+        fwd_zl(U, 2, c)
+    fwd_2(A, 2, 0)
+    looks(10, 11)
+    fwd_1(A, 2)
+    fwd_2(A, 1, 0)
+    fwd_2(A, -1, 0)
+    fwd_2(A, 1, 1)
+    looks(11, 12)
+    fwd_2(I, -1, 1)
+    fwd_2(I, 2, 0)
+    looks(12, 13)
+    looks(13, 14)
+    looks(14, 15)
+    fwd_2(I, 0, 1)
+    fwd_2(A, -1, 1)
+    fwd_2(A, 0, 1)
+    looks(15, 16)
+    fwd_2(I, 1, 1)
+    fwd_2(A, 2, 1)
+    fwd_2(I, 2, 1)
+    f_split()
+    fwd_2(I, 0, 0)
+    f_rows()
+    f_cross()
+    f_tower_one()
+    f_tower_two()
     hc = G[:, 80:112, 1024:LN].reshape(1024, 128)
     zl = nn(h2[...], hc) + bia[5:6, 0:128]
-    yl = jnp.broadcast_to(R_["lab_v"][...].reshape(1, 384).astype(F32), (128, 384)).T
+    yl = jnp.broadcast_to(B.lab_v[...].reshape(1, 384).astype(F32), (128, 384)).T
     lossv = jnp.maximum(zl, 0.0) + jnp.log1p(jnp.exp(-jnp.abs(zl))) - yl * zl
     dz = (sig(zl) - yl) / total
     M[...] = jnp.zeros_like(M)
@@ -679,7 +710,7 @@
         i = nsem[0]
         nsem[0] += 1
         c = pltpu.make_async_remote_copy(
-            src_ref=src, dst_ref=dst, send_sem=R_["rss"].at[i], recv_sem=R_["rrs"].at[i], device_id=dst_dev, device_id_type=MESH)
+            src_ref=src, dst_ref=dst, send_sem=B.rss.at[i], recv_sem=B.rrs.at[i], device_id=dst_dev, device_id_type=MESH)
         c.start()
         sends.append(c)
         return c
@@ -690,47 +721,56 @@
         return (y, x, ypeer, xpeer) if ITEMS[n][2] else (x, y, xpeer, ypeer)
 
     def s0(n):
-        g = R_["g_" + n]
-        st[n] = go(g.at[1 - r], R_["C_" + n], core)
+        g = buf("g", n)
+        st[n] = go(g.at[1 - r], buf("C", n), core)
 
     def s1(n):
         a, b, pa, pb = axes(n)
         st[n].wait_recv()
-        g, c = R_["g_" + n], R_["C_" + n]
+        g, c = buf("g", n), buf("C", n)
         st[n] = []
         for bb in (1 - b, b):
             g[r, 1 - a, bb] = (g[r, 1 - a, bb].astype(F32) + c[1 - a, bb].astype(F32)).astype(BF)
-            st[n].append(go(g.at[r, 1 - a, bb], R_["P_" + n].at[bb], pa))
+            st[n].append(go(g.at[r, 1 - a, bb], buf("P", n).at[bb], pa))
 
     def s2(n):
         a, b, pa, pb = axes(n)
         st[n][0].wait_recv()
-        g, c, p = R_["g_" + n], R_["C_" + n], R_["P_" + n]
+        g, c, p = buf("g", n), buf("C", n), buf("P", n)
         g[r, a, 1 - b] = (g[r, a, 1 - b].astype(F32) + c[a, 1 - b].astype(F32) + p[1 - b].astype(F32)).astype(BF)
-        st[n].append(go(g.at[r, a, 1 - b], R_["Q_" + n], pb))
+        st[n].append(go(g.at[r, a, 1 - b], buf("Q", n), pb))
 
     def s3(n):
         a, b, pa, pb = axes(n)
         st[n][1].wait_recv()
         st[n][2].wait_recv()
-        g, c, p, q = R_["g_" + n], R_["C_" + n], R_["P_" + n], R_["Q_" + n]
+        g, c, p, q = buf("g", n), buf("C", n), buf("P", n), buf("Q", n)
         st[n] = []
         for i, zz in enumerate(zp):
             g[r, a, b, zz] = (g[r, a, b, zz].astype(F32) + c[a, b, zz].astype(F32) + p[b, zz].astype(F32) + q[zz].astype(F32)).astype(BF)
-            st[n].append(go(g.at[r, a, b, zz], R_["T_" + n].at[i], zpeer[i]))
+            st[n].append(go(g.at[r, a, b, zz], buf("T", n).at[i], zpeer[i]))
+
+    writes = []
+
+    def write(src, dst):
+        c = pltpu.make_async_copy(src, dst, B.osem.at[len(writes)])
+        c.start()
+        writes.append(c)
 
     def s4(n):
         a, b, pa, pb = axes(n)
         for c in st[n]:
             c.wait_recv()
-        g, c, p, q, t = R_["g_" + n], R_["C_" + n], R_["P_" + n], R_["Q_" + n], R_["T_" + n]
+        g, c, p, q, t = buf("g", n), buf("C", n), buf("P", n), buf("Q", n), buf("T", n)
         nb, _, _, out, at = ITEMS[n]
-        R_["o_" + out][at : at + nb] = (
+        gradient = (
             g[r, a, b, z].astype(F32) + c[a, b, z].astype(F32) + p[b, z].astype(F32) + q[z].astype(F32)
             + (t[0].astype(F32) + t[1].astype(F32) + t[2].astype(F32)))
+        buf("w", out)[at : at + nb] = gradient
+        write(buf("w", out).at[pl.ds(at, nb)], buf("o", out).at[pl.ds(at, nb)])
 
     def parts_of(out):
-        return [n for n in ITEMS if ITEMS[n][3] == out]
+        return [n for n, item in enumerate(ITEMS) if item[3] == out]
 
     def put(out, base, g):
         for n in parts_of(out):
@@ -738,14 +778,14 @@
             for i in range(g.shape[0] // 32):
                 rep, xx, yy, zz = place(base + i)
                 a, b = (yy, xx) if yfirst else (xx, yy)
-                R_["g_" + n][rep, a, b, zz] = g[i * 32 + at : i * 32 + at + nb].astype(BF)
-
-    MS, MX = R_["MS"], R_["MX"]
+                buf("g", n)[rep, a, b, zz] = g[i * 32 + at : i * 32 + at + nb].astype(BF)
+
+    MS, MX = B.MS, B.MX
 
     def grad_mid():
         for n in range(4):
-            put("m", 8 * n, tn(d2[:, 256 * n : 256 * n + 256], h1[...]))
-        for n in parts_of("m"):
+            put(0, 8 * n, tn(d2[:, 256 * n : 256 * n + 256], h1[...]))
+        for n in parts_of(0):
             s0(n)
 
     def down_one():
@@ -760,8 +800,8 @@
 
     def grad_in():
         for n in range(4):
-            put("i", 8 * n, tn(d1[:, 256 * n : 256 * n + 256], xl[3]))
-        for n in parts_of("i"):
+            put(1, 8 * n, tn(d1[:, 256 * n : 256 * n + 256], xl[3]))
+        for n in parts_of(1):
             s0(n)
 
     def down_x():
@@ -785,11 +825,11 @@
             else:
                 d0[:, lo : lo + n] = d0[:, lo : lo + n] + v
         if l == 0:
-            st["M"] = go(M, R_["MC"], core)
+            st[-1] = go(M, B.MC, core)
 
     def cross_grads(l):
-        gr = R_["g_c%d" % l]
-        yfirst = ITEMS["c%d" % l][2]
+        gr = buf("g", C0 - l)
+        yfirst = ITEMS[C0 - l][2]
         for lo, n in CH:
             gu = tn(pr[l], dql[l, :, lo : lo + n]).reshape(32, 8, n)
             gv = tn(dpr[l], xl[l, :, lo : lo + n]).reshape(32, 8, n)
@@ -798,7 +838,7 @@
                 rep, xx, yy, zz = place(k)
                 a, b = (yy, xx) if yfirst else (xx, yy)
                 gr[rep, a, b, zz, :, lo : lo + n] = gg[k]
-        s0("c%d" % l)
+        s0(C0 - l)
 
     def back_rows(d):
         return jnp.concatenate([DE[inv[2 * d]], DE[inv[2 * d + 1]]], axis=0).astype(BF)
@@ -846,43 +886,84 @@
             for j in range(32):
                 g, h = j // 4, j % 4
                 gg_[pl.ds(2 * j + s, 39, stride=64), :] = R[s, g * 40 : g * 40 + 39, h * 128 : (h + 1) * 128]
-        st["g"] = go(gg_, gtc, core)
+        st[-2] = go(gg_, gtc, core)
 
     def table_both():
-        st["g"].wait_recv()
-        gt[...] = gg_[...] + gtc[...]
+        st[-2].wait_recv()
+        gtc[...] = gg_[...] + gtc[...]
+        write(gtc, gt)
 
     def small(i):
         if i == 1:
-            st["M"].wait_recv()
-            MS[0] = M[...] + R_["MC"][...]
-            st["M"] = go(MS.at[0], MX.at[0], xpeer)
+            st[-1].wait_recv()
+            MS[0] = M[...] + B.MC[...]
+            st[-1] = go(MS.at[0], MX.at[0], xpeer)
         elif i == 2:
-            st["M"].wait_recv()
+            st[-1].wait_recv()
             MS[1] = MS[0] + MX[0]
-            st["M"] = go(MS.at[1], MX.at[1], ypeer)
+            st[-1] = go(MS.at[1], MX.at[1], ypeer)
         elif i == 3:
-            st["M"].wait_recv()
+            st[-1].wait_recv()
             MS[2] = MS[1] + MX[1]
-            st["M"] = [go(MS.at[2], MX.at[2 + j], zpeer[j]) for j in range(3)]
+            st[-1] = [go(MS.at[2], MX.at[2 + j], zpeer[j]) for j in range(3)]
         else:
-            for c in st["M"]:
+            for c in st[-1]:
                 c.wait_recv()
             pos = [MS[2], MX[2], MX[3], MX[4]]
             u = jnp.where(z % 2 == 0, pos[0], pos[1]) + jnp.where(z % 2 == 0, pos[1], pos[0])
             v = jnp.where(z % 2 == 0, pos[2], pos[3]) + jnp.where(z % 2 == 0, pos[3], pos[2])
-            MO[...] = jnp.where(z < 2, u, v) + jnp.where(z < 2, v, u)
-
-    stage = {"s1": s1, "s2": s2, "s3": s3, "s4": s4}
-    plain = {"dTm": grad_mid, "dh1": down_one, "dTi": grad_in, "dx3": down_x, "D": rows_out, "gt": table_sum, "gts": table_both}
-    indexed = {"ch": chain, "cg": cross_grads, "sc": rows_in, "M": small}
-    for op in BACKWARD:
-        if op in plain:
-            plain[op]()
-        elif op[:2] in stage:
-            stage[op[:2]](op[2:])
-        else:
-            indexed[op[:-1]](int(op[-1]))
+            B.MC[...] = jnp.where(z < 2, u, v) + jnp.where(z < 2, v, u)
+            write(B.MC, MO)
+
+    grad_mid()
+    down_one()
+    down_x()
+    s1(M0)
+    s1(M1)
+    chain(2)
+    cross_grads(2)
+    chain(1)
+    chain(0)
+    cross_grads(0)
+    s2(M1)
+    small(1)
+    rows_out()
+    grad_in()
+    s3(M1)
+    small(2)
+    s1(C2)
+    s1(IN)
+    cross_grads(1)
+    s2(M0)
+    small(3)
+    s2(IN)
+    s3(M0)
+    s1(C0)
+    s2(C2)
+    s1(C1)
+    s3(IN)
+    rows_in(0)
+    rows_in(1)
+    s4(M1)
+    rows_in(2)
+    rows_in(3)
+    rows_in(4)
+    s4(M0)
+    s3(C2)
+    s2(C1)
+    s2(C0)
+    s3(C1)
+    rows_in(5)
+    rows_in(6)
+    s3(C0)
+    rows_in(7)
+    s4(C2)
+    table_sum()
+    small(4)
+    s4(C1)
+    s4(IN)
+    table_both()
+    s4(C0)
 
     def dw(i, _):
         d = (me + i) % 16
@@ -892,6 +973,8 @@
     lax.fori_loop(1, 16, dw, 0)
     for c in sends:
         c.wait_send()
+    for c in writes:
+        c.wait()
 
     @pl.when(inner)
     def _():
@@ -902,117 +985,113 @@
 def mega(total, ts, ids, tab, cr, ti, tm, hd, dns, lab, bi):
     V, S = pltpu.VMEM, jax.ShapeDtypeStruct
     vm, sm, an = pl.BlockSpec(memory_space=pltpu.VMEM), pl.BlockSpec(memory_space=pltpu.SMEM), pl.BlockSpec(memory_space=pl.ANY)
-    ins = {"ts": ts, "ids": ids, "tab": tab, "cr": cr, "ti": ti, "tm": tm, "hd": hd, "dns": dns, "lab": lab, "bi": bi}
-    outs = {"gt": S((2496, 128), F32), "MO": S((8, LN), F32)}
-    for n in SUMS:
-        outs["o_" + n] = S(SUMS[n], F32)
-    scr = {n + "_v": V(ins[n].shape, ins[n].dtype) for n in ("ids", "cr", "ti", "tm", "hd", "dns", "lab", "bi")}
-    scr.update(
+    ins = dict(ts=ts, ids=ids, tab=tab, cr=cr, ti=ti, tm=tm, hd=hd, dns=dns, lab=lab, bi=bi)
+    outs = dict(gt=S((2496, 128), F32), MO=S((8, LN), F32))
+    for n, shape in enumerate(SUMS):
+        outs["o" + str(n)] = S(shape, F32)
+    like = lambda a: V(a.shape, a.dtype)
+    dma = pltpu.SemaphoreType.DMA
+    scr = dict(
+        ids_v=like(ids), cr_v=like(cr), ti_v=like(ti), tm_v=like(tm), hd_v=like(hd), dns_v=like(dns), lab_v=like(lab), bi_v=like(bi),
         G=V((32, RB, LN), BF), E=V((16, 80, 384), BF), D=V((16, 80, 384), BF), eout=V((16, 80, 384), BF), tabr=V((2, 320, 512), BF),
         xT=V((LN, 384), F32), dx=V((384, LN), F32), xl=V((4, 384, LN), BF), qc=V((3, 384, LN), F32), pr=V((3, 384, 256), BF),
         VT=V((3, 256, LN), BF), UT=V((3, 256, LN), BF), h1=V((384, 1024), BF), h2=V((384, 1024), BF),
         d0=V((384, LN), F32), dql=V((3, 384, LN), BF), dpr=V((3, 384, 256), BF), DE=V((27, 40, 384), F32), M=V((8, LN), F32), R=V((2, 320, 512), F32),
-        MC=V((8, LN), F32), MS=V((3, 8, LN), F32), MX=V((5, 8, LN), F32), gg=V((2496, 128), F32), gtc=V((2496, 128), F32), bia=V((8, LN), F32), inv=pltpu.SMEM((32,), jnp.int32))
-    for n in ORDER:
-        nb, L = ITEMS[n][:2]
-        scr["g_" + n] = V((2, 2, 2, 4, nb, L), BF)
-        scr["C_" + n] = V((2, 2, 4, nb, L), BF)
-        scr["P_" + n] = V((2, 4, nb, L), BF)
-        scr["Q_" + n] = V((4, nb, L), BF)
-        scr["T_" + n] = V((3, nb, L), BF)
-    dma = pltpu.SemaphoreType.DMA
-    scr.update(lsem=dma((9,)), wss=dma((3, 40)), wrs=dma((3, 32)), ess=dma((16,)), ers=dma((16,)), dss=dma((16,)), drs=dma((16,)), rss=dma((64,)), rrs=dma((64,)))
-    res = pl.pallas_call(
-        functools.partial(mega_body, total, list(ins), list(outs), list(scr)), name="train_step",
-        out_shape=tuple(outs.values()), in_specs=[sm] + [an] * 9, out_specs=(vm,) * len(outs),
+        MC=V((8, LN), F32), MS=V((3, 8, LN), F32), MX=V((5, 8, LN), F32), gg=V((2496, 128), F32), gtc=V((2496, 128), F32), bia=V((8, LN), F32),
+        inv=pltpu.SMEM((32,), jnp.int32), lsem=dma((9,)), wss=dma((3, 40)), wrs=dma((3, 32)), ess=dma((16,)), ers=dma((16,)), dss=dma((16,)), drs=dma((16,)),
+        rss=dma((64,)), rrs=dma((64,)), osem=dma((9,)))
+    for n, shape in enumerate(SUMS):
+        scr["w" + str(n)] = V(shape, F32)
+    for n, (nb, L, *_) in enumerate(ITEMS):
+        for kind, lead in (("g", (2, 2, 2, 4)), ("C", (2, 2, 4)), ("P", (2, 4)), ("Q", (4,)), ("T", (3,))):
+            scr[kind + str(n)] = V(lead + (nb, L), BF)
+    return pl.pallas_call(
+        functools.partial(mega_body, total, list(ins) + list(outs) + list(scr)), name="train_step",
+        out_shape=tuple(outs.values()), in_specs=[sm] + [an] * 9, out_specs=(an,) * len(outs),
         scratch_shapes=list(scr.values()),
         compiler_params=pltpu.CompilerParams(collective_id=0, has_side_effects=True, vmem_limit_bytes=63 << 20),
     )(*ins.values())
-    return dict(zip(outs, res))
-
-
-C5 = 1 - 0.5**5
+
+
+IC5 = 1 / (1 - 0.5**5)
 
 
 def adamw(w, m, v, g, rate):
     mn = 0.5 * m + 0.5 * g
     vn = 0.5 * v + 0.5 * g * g
-    return w - rate * ((mn / C5) / (jnp.sqrt(vn / C5) + EPSILON) + WEIGHT_DECAY * w), mn, vn
-
-
-SMALL = [k + q for k in "hb" for q in "wnv"]
-
-
-def update_body(names_in, names_out, names_scr, *refs):
-    it = iter(refs)
-    R_ = {n: next(it) for n in names_in + names_out + names_scr}
-    rc, isem, osem = R_["rc"], R_["isem"], R_["osem"]
-    order = [k + q for k in "tcim" for q in "wnv"]
-    ld = {}
-    for n in SMALL + order[3:]:
-        ld[n] = pltpu.make_async_copy(R_[n], R_["v_" + n], isem.at[len(ld)])
-        ld[n].start()
-    for part in range(3):
-        for n in ("tw", "tn", "tv", "gt"):
-            q = pl.ds(832 * part, 832)
-            ld[n, part] = pltpu.make_async_copy(R_[n].at[q], R_["v_" + n].at[q], isem.at[len(ld)])
-            ld[n, part].start()
+    return w - rate * ((mn * IC5) / (jnp.sqrt(vn * IC5) + EPSILON) + WEIGHT_DECAY * w), mn, vn
+
+
+def update_body(rc, *refs):
+    hbm, gt, MO, sums, refs = refs[:18], refs[18], refs[19], refs[20:25], refs[25:]
+    dst, loss, vin, vg, vout, refs = refs[:24], refs[24], refs[25:43], refs[43], refs[44:68], refs[68:]
+    near, isem, osem = refs[:6], refs[6], refs[7]
+    n_in, n_out = [0], [0]
+
+    def load(src, to):
+        c = pltpu.make_async_copy(src, to, isem.at[n_in[0]])
+        n_in[0] += 1
+        c.start()
+        return c
+
     outs = []
 
-    def out(name, rows=None):
-        i = len(outs)
-        s, d = R_["u_" + name], R_["o_" + name]
-        if rows is not None:
-            s, d = s.at[rows], d.at[rows]
-        c = pltpu.make_async_copy(s, d, osem.at[i])
-        c.start()
-        outs.append(c)
-
-    for n in SMALL:
-        ld[n].wait()
-    MO = R_["MO"]
-    R_["o_loss"][0, 0] = jnp.max(MO[6:7, 0:128])
-    k = lax.axis_index("dp") * 2 + lax.axis_index("rep")
-    gb = jnp.concatenate([MO[0:1, :WIDTH], MO[1:2, :WIDTH], MO[2:3, :WIDTH], MO[3:4, :1024], MO[4:5, :1024], MO[7:8, :1]], axis=1)
-    gh = pltpu.roll(MO[5:6, 0:1024], 1024 - 32 * k, 1)[:, 0:32]
-    for kk, g, rate in (("h", gh, RATE_DENSE), ("b", gb, RATE_BIAS)):
-        n = g.shape[1]
-        w, m, v = adamw(*(R_["v_" + kk + q][...].reshape(1, n) for q in "wnv"), g, rate)
-        for q, a in (("w", w), ("n", m), ("v", v), ("l", w.astype(BF))):
-            R_["u_" + kk + q][...] = a.reshape(n)
-            out(kk + q)
-    rows = {"c": [("c0", 0, 16), ("c1", 16, 16), ("c2", 32, 16)], "i": [("i", 0, 32)], "m": [("m", 0, 32)]}
-    for k in "imc":
-        for q in "wnv":
-            ld[k + q].wait()
-        for n, lo, nb in rows[k]:
-            L = R_["v_" + k + "w"].shape[1]
+    def out(k, rows=None):
+        for i in range(4 * k, 4 * k + 4):
+            s, d = vout[i], dst[i]
+            if rows is not None:
+                s, d = s.at[rows], d.at[rows]
+            c = pltpu.make_async_copy(s, d, osem.at[n_out[0]])
+            n_out[0] += 1
+            c.start()
+            outs.append(c)
+
+    span = lambda part: pl.ds(832 * part, 832)
+    dense = {k: [load(hbm[3 * k + j], vin[3 * k + j]) for j in range(3)] for k in (2, 3, 1)}
+    gradients = [load(a, b) for a, b in zip((*sums, MO), near)]
+    sums, MO = near[:5], near[5]
+    table = [[load(a.at[span(part)], b.at[span(part)]) for a, b in ((hbm[0], vin[0]), (hbm[1], vin[1]), (hbm[2], vin[2]), (gt, vg))] for part in range(3)]
+    dense.update({k: [load(hbm[3 * k + j], vin[3 * k + j]) for j in range(3)] for k in (4, 5)})
+    for c in gradients:
+        c.wait()
+    for k, rows in ((2, [(1, 0, 32)]), (3, [(0, 0, 32)]), (1, [(4, 0, 16), (3, 16, 16), (2, 32, 16)])):
+        for c in dense[k]:
+            c.wait()
+        w_in, m_in, v_in = vin[3 * k : 3 * k + 3]
+        for n, lo, nb in rows:
             at = slice(lo, lo + nb)
-            w, m, v = adamw(R_["v_" + k + "w"][at], R_["v_" + k + "n"][at], R_["v_" + k + "v"][at], R_["g_" + n][:, 0:L], RATE_DENSE)
-            R_["u_" + k + "w"][at], R_["u_" + k + "n"][at], R_["u_" + k + "v"][at], R_["u_" + k + "l"][at] = w, m, v, w.astype(BF)
-        for q in "wnvl":
-            out(k + q)
+            w, m, v = adamw(w_in[at], m_in[at], v_in[at], sums[n][:, 0 : w_in.shape[1]], RATE_DENSE)
+            for o, a in zip(vout[4 * k : 4 * k + 4], (w, m, v, w.astype(BF))):
+                o[at] = a
+        out(k)
     row = lax.broadcasted_iota(jnp.int32, (64, 128), 0)
     lane = lax.broadcasted_iota(jnp.int32, (64, 128), 1)
     use = ((row // 2) * 128 + lane) < jnp.where(row % 2 == 0, rc[0], rc[1])
     for part in range(3):
-        for n in ("tw", "tn", "tv", "gt"):
-            ld[n, part].wait()
-
-        def tab(c, at):
-            q = pl.ds(pl.multiple_of(at + c * 64, 64), 64)
-            w, m, v = R_["v_tw"][q], R_["v_tn"][q], R_["v_tv"][q]
-            nw, nm, nv = adamw(w, m, v, R_["v_gt"][q], RATE_TABLE)
+        for c in table[part]:
+            c.wait()
+        for i in range(13):
+            q = pl.ds(832 * part + i * 64, 64)
+            w, m, v = vin[0][q], vin[1][q], vin[2][q]
+            nw, nm, nv = adamw(w, m, v, vg[q], RATE_TABLE)
             nw = jnp.where(use, nw, w)
-            R_["u_tw"][q] = nw
-            R_["u_tn"][q] = jnp.where(use, nm, m)
-            R_["u_tv"][q] = jnp.where(use, nv, v)
-            R_["u_tl"][q] = nw.astype(BF)
-
-        for c in range(13):
-            tab(c, 832 * part)
-        for q in "wnvl":
-            out("t" + q, pl.ds(832 * part, 832))
+            vout[0][q] = nw
+            vout[1][q] = jnp.where(use, nm, m)
+            vout[2][q] = jnp.where(use, nv, v)
+            vout[3][q] = nw.astype(BF)
+        out(0, span(part))
+    loss[0, 0] = jnp.max(MO[6:7, 0:128])
+    k = lax.axis_index("dp") * 2 + lax.axis_index("rep")
+    gb = jnp.concatenate([MO[0:1, :WIDTH], MO[1:2, :WIDTH], MO[2:3, :WIDTH], MO[3:4, :1024], MO[4:5, :1024], MO[7:8, :1]], axis=1)
+    gh = pltpu.roll(MO[5:6, 0:1024], 1024 - 32 * k, 1)[:, 0:32]
+    for k, g, rate in ((4, gh, RATE_DENSE), (5, gb, RATE_BIAS)):
+        for c in dense[k]:
+            c.wait()
+        n = g.shape[1]
+        w, m, v = adamw(*(a[...].reshape(1, n) for a in vin[3 * k : 3 * k + 3]), g, rate)
+        for o, a in zip(vout[4 * k : 4 * k + 4], (w, m, v, w.astype(BF))):
+            o[...] = a.reshape(n)
+        out(k)
     for c in outs:
         c.wait()
 
@@ -1020,33 +1099,15 @@
 def update(rc, g, state):
     V, S = pltpu.VMEM, jax.ShapeDtypeStruct
     vm, sm, an = pl.BlockSpec(memory_space=pltpu.VMEM), pl.BlockSpec(memory_space=pltpu.SMEM), pl.BlockSpec(memory_space=pl.ANY)
-    ins, specs = {"rc": rc}, [sm]
-    for k in "tcimhb":
-        for q, a in zip("wnv", state[k]):
-            ins[k + q] = a
-            specs.append(an)
-    ins["gt"], ins["MO"] = g["gt"], g["MO"]
-    specs += [an, vm]
-    for n in SUMS:
-        ins["g_" + n] = g["o_" + n]
-        specs.append(vm)
-    outs, scr = {}, {}
-    for k in "tcimhb":
-        for q in "wnvl":
-            shape, kind = state[k][0].shape, BF if q == "l" else F32
-            outs["o_" + k + q] = S(shape, kind)
-            scr["u_" + k + q] = V(shape, kind)
-            if q != "l":
-                scr["v_" + k + q] = V(shape, kind)
-    scr["v_gt"] = V((2496, 128), F32)
-    outs["o_loss"] = S((1, 1), F32)
-    scr["isem"] = pltpu.SemaphoreType.DMA((27,))
-    scr["osem"] = pltpu.SemaphoreType.DMA((32,))
+    flat = [a for kind in state for a in kind]
+    kinds = [S(kind[0].shape, t) for kind in state for t in (F32, F32, F32, BF)]
+    dma = pltpu.SemaphoreType.DMA
     return pl.pallas_call(
-        functools.partial(update_body, list(ins), list(outs), list(scr)), name="adamw_step",
-        out_shape=tuple(outs.values()), in_specs=specs, out_specs=(an,) * (len(outs) - 1) + (sm,), scratch_shapes=list(scr.values()),
+        update_body, name="adamw_step", out_shape=tuple(kinds) + (S((1, 1), F32),),
+        in_specs=[sm] + [an] * 25, out_specs=(an,) * 24 + (sm,),
+        scratch_shapes=[V(a.shape, F32) for a in flat] + [V((2496, 128), F32)] + [V(a.shape, a.dtype) for a in kinds] + [V(shape, F32) for shape in SUMS] + [V((8, LN), F32), dma((33,)), dma((32,))],
         compiler_params=pltpu.CompilerParams(vmem_limit_bytes=63 << 20),
-    )(*ins.values())
+    )(rc, *flat, *g)
 
 
 def tab_view(t):
@@ -1067,16 +1128,15 @@
     total = float(labels.shape[0] * lax.axis_size("dp") * lax.axis_size("rep"))
     turn = lambda a: jnp.transpose(a, (0, 1, 3, 2)).reshape(48, WIDTH)
     back = lambda a: jnp.transpose(a.reshape(LAYERS, 2, 8, WIDTH), (0, 1, 3, 2))
-    state = {
-        "t": [tab_view(a) for a in (tables, tables_m, tables_v)],
-        "c": [turn(a) for a in (cross_uv, cross_m, cross_v)],
-        "i": [a.T for a in (tower_in, tower_in_m, tower_in_v)],
-        "m": [a.T for a in (tower_mid, tower_mid_m, tower_mid_v)],
-    }
-    state["h"] = [head_weight, head_m, head_v]
-    state["b"] = [biases, biases_m, biases_v]
-    g = mega(total, table_slot, event_ids, state["t"][0], state["c"][0], state["i"][0], state["m"][0],
-             head_weight, dense_input.T, labels, biases)
+    state = [
+        [tab_view(a) for a in (tables, tables_m, tables_v)],
+        [turn(a) for a in (cross_uv, cross_m, cross_v)],
+        [a.T for a in (tower_in, tower_in_m, tower_in_v)],
+        [a.T for a in (tower_mid, tower_mid_m, tower_mid_v)],
+        [head_weight, head_m, head_v],
+        [biases, biases_m, biases_v],
+    ]
+    g = mega(total, table_slot, event_ids, *(kind[0] for kind in state[:5]), dense_input.T, labels, biases)
     o = update(row_counts, g, state)
     return (
         o[24].reshape(()),

time: 134 us -> 132 us (0.985)
  Pallas kernels: 133 us -> 131 us
    pallas_call x2, Pallas kernels: 133 us -> 131 us  [the longest x1 123 us: mega(): pl.pallas_call(functools.partial(mega_body, total, list(ins) + list(outs)...]
where the time goes in v4:
time: 132 us
  Pallas kernels  131 us (99%)
    pallas_call x1, Pallas kernels, mega(): pl.pallas_call(functools.partial(mega_body, total, list(ins) + list(outs)...  123 us
    pallas_call x1, Pallas kernels, update(): pl.pallas_call(update_body, name='adamw_step', out_shape=tuple(kinds) + (...  7.91 us

profile of v4, /device:TPU:0, one launch (start us, length us, event | category | flops | bytes accessed | tf_op | source)
XLA Modules:
  0.0 132.0 jit_solution(14888473741942342421)
XLA Ops:
  0.7 123.2 %train_step.1 = (f32[2496,128]{1,0:T(8,128)}, f32[8,1152]{1,0:T(8,128)}, f32[32,1024]{1,0:T(8,128)}, f32[32,1152]{1,0:T(8,128)}, f32[16,1152]{1,0:T(8,128)}, /*index=5*/f32[16,1152]{1,0:T(8,128)}, f32[16,1152]{1,0:T(8,128)}) custom-call(s32[26]{0:T(128)} %refs_0_.1, s32[2,12288]{1,0:T(2,128)} %refs_1_.1, f32[2496,128]{1,0:T(8,128)} %bitcast.86, ...), custom_call_target="tpu_custom_call" | custom-call | tf_op jit(solution)/shard_map/train_step/pallas_call | solution.py:1008
  123.9 7.9 %adamw_step.1 = (f32[2496,128]{1,0:T(8,128)}, f32[2496,128]{1,0:T(8,128)}, f32[2496,128]{1,0:T(8,128)}, bf16[2496,128]{1,0:T(8,128)(2,1)}, f32[48,1027]{1,0:T(8,...) custom-call(s32[2]{0:T(128)} %rc.1, ...), custom_call_target="tpu_custom_call" | custom-call | tf_op jit(solution)/shard_map/adamw_step/pallas_call | solution.py:1105

commit v5 on v4

--- a/solution.py
+++ b/solution.py
@@ -331,12 +331,12 @@
 ITEMS = [
     (16, 1024, True, 0, 0),
     (16, 1024, False, 0, 16),
-    (32, LN, True, 1, 0),
-    (16, LN, False, 2, 0),
-    (16, LN, True, 3, 0),
+    (32, 1024, True, 1, 0),
+    (16, LN, True, 2, 0),
+    (16, LN, False, 3, 0),
     (16, LN, False, 4, 0),
 ]
-SUMS = [(32, 1024), (32, LN), (16, LN), (16, LN), (16, LN)]
+SUMS = [(32, 1024), (32, 1024), (16, LN), (16, LN), (16, LN)]
 A, I, U = range(3)
 PARTS = [(0, 48, True), (48, 48, False), (96, 16, False)]
 
@@ -404,13 +404,13 @@
     for c in loads[:4]:
         c.wait()
     G[own, 0:48, 0:1024] = cr[:, 0:1024].astype(BF)
-    G[own, 0:48, 1024:LN] = jnp.concatenate([cr[:, 1024:1027], jnp.zeros((48, 125), F32)], axis=1).astype(BF)
     G[own, 48:80, 0:1024] = ti[:, 0:1024].astype(BF)
-    G[own, 48:80, 1024:LN] = jnp.concatenate([ti[:, 1024:1027], jnp.zeros((32, 125), F32)], axis=1).astype(BF)
     G[own, 80:112, 0:1024] = tm[...].astype(BF)
     eye = lax.broadcasted_iota(jnp.int32, (32, 32), 0) == lax.broadcasted_iota(jnp.int32, (32, 32), 1)
     hcol = jnp.sum(jnp.where(eye, jnp.broadcast_to(hd[...].reshape(1, 32), (32, 32)), 0.0), axis=1, keepdims=True)
-    G[own, 80:112, 1024:LN] = jnp.broadcast_to(hcol, (32, 128)).astype(BF)
+    more = jnp.concatenate([jnp.zeros((32, 3), F32), ti[:, 1024:1027], jnp.zeros((32, 58), F32), jnp.broadcast_to(hcol, (32, 64))], axis=1)
+    ends = jnp.concatenate([cr[:, 1024:1027], jnp.zeros((48, 125), F32)], axis=1) + jnp.concatenate([more, jnp.zeros((16, 128), F32)], axis=0)
+    G[own, 0:48, 1024:LN] = ends.astype(BF)
     pl.semaphore_wait(bar, 16)
 
     cnt = [0, 0, 0]
@@ -418,8 +418,9 @@
 
     def wcopy(p, k, dst, si):
         lo, n, _ = PARTS[p]
+        at = (k, pl.ds(lo, n), pl.ds(0, LN if p == A else 1024))
         return pltpu.make_async_remote_copy(
-            src_ref=G.at[k, pl.ds(lo, n)], dst_ref=G.at[k, pl.ds(lo, n)],
+            src_ref=G.at[at], dst_ref=G.at[at],
             send_sem=B.wss.at[p, si], recv_sem=B.wrs.at[p, k], device_id=dst, device_id_type=MESH)
 
     def wsend(p, k, dst):
@@ -591,6 +592,8 @@
         for l in range(3):
             for lo, n in CH:
                 w = G[:, 16 * l : 16 * l + 16, lo : lo + n].astype(F32).reshape(32, 2, 8, n)
+                if lo == 1024:
+                    w = jnp.where(lax.broadcasted_iota(jnp.int32, w.shape, 3) < 3, w, 0.0)
                 VT[l, :, lo : lo + n] = w[:, 0].reshape(256, n).astype(BF)
                 UT[l, :, lo : lo + n] = w[:, 1].reshape(256, n).astype(BF)
 
@@ -607,9 +610,11 @@
 
     def f_tower_one():
         core_wait(I)
+        x_end = pltpu.roll(xl[3, :, 1024:LN].astype(F32), 3, 1).astype(BF)
         for n in range(4):
             c = slice(256 * n, 256 * n + 256)
-            a = nt(xl[3], G[8 * n : 8 * n + 8, 48:80, :].reshape(256, LN)) + bia[3:4, c]
+            a = nt(xl[3, :, 0:1024], G[8 * n : 8 * n + 8, 48:80, 0:1024].reshape(256, 1024)) + bia[3:4, c]
+            a = a + nt(x_end, G[8 * n : 8 * n + 8, 0:32, 1024:LN].reshape(256, 128))
             a1[:, c] = a
             h1[:, c] = (a * sig(a)).astype(BF)
 
@@ -621,82 +626,83 @@
             a2[:, c] = a
             h2[:, c] = (a * sig(a)).astype(BF)
 
-    f_own(U)
     f_own(I)
-    f_own(A)
     f_prep()
     looks(0, 1)
+    f_core(U)
+    f_own(A)
+    f_own(U)
+    fwd_z(I, 0)
     looks(1, 2)
+    fwd_1(A, -1)
+    fwd_2(U, -1, 0)
     fwd_1(I, -1)
+    fwd_z(A, 0)
     fwd_1(U, -1)
-    f_core(U)
-    fwd_z(I, 0)
-    fwd_z(A, 0)
     fwd_z(I, 1)
     fwd_z(A, 1)
-    fwd_1(A, -1)
+    fwd_1(A, 0)
+    fwd_2(I, -1, 0)
+    fwd_1(I, 0)
+    fwd_z(I, 2)
+    fwd_2(A, -1, 1)
     looks(2, 3)
+    fwd_2(A, 0, 0)
+    f_core(I)
+    f_core(A)
+    fwd_2(U, -1, 1)
+    fwd_2(I, -1, 1)
     looks(3, 4)
-    fwd_2(U, -1, 1)
-    fwd_2(U, -1, 0)
-    fwd_z(I, 2)
-    fwd_1(A, 0)
-    f_core(I)
-    fwd_1(I, 1)
+    fwd_z(A, 2)
     looks(4, 5)
     looks(5, 6)
-    looks(6, 7)
-    fwd_z(A, 2)
-    fwd_1(A, 1)
     for c in range(4):
         fwd_zl(U, 1, c)
+    looks(6, 7)
+    fwd_2(A, 0, 1)
+    fwd_1(I, 2)
+    fwd_1(A, 1)
+    fwd_2(I, 1, 0)
+    fwd_2(A, 1, 0)
+    fwd_1(I, 1)
+    looks(7, 8)
+    looks(8, 9)
+    fwd_2(A, -1, 0)
+    fwd_2(A, 2, 0)
+    fwd_1(A, 2)
+    looks(9, 10)
     for c in range(4):
         fwd_zl(U, 0, c)
-    fwd_2(A, 0, 0)
-    fwd_2(I, -1, 0)
-    looks(7, 8)
-    looks(8, 9)
-    fwd_1(I, 0)
-    fwd_1(I, 2)
-    fwd_2(I, 1, 0)
-    f_core(A)
-    looks(9, 10)
+    fwd_2(I, 0, 0)
+    looks(10, 11)
+    looks(11, 12)
+    looks(12, 13)
+    looks(13, 14)
+    fwd_2(I, 2, 1)
+    fwd_2(A, 1, 1)
+    looks(14, 15)
+    fwd_2(I, 0, 1)
+    looks(15, 16)
+    fwd_2(I, 2, 0)
     for c in range(4):
         fwd_zl(U, 2, c)
-    fwd_2(A, 2, 0)
-    looks(10, 11)
-    fwd_1(A, 2)
-    fwd_2(A, 1, 0)
-    fwd_2(A, -1, 0)
-    fwd_2(A, 1, 1)
-    looks(11, 12)
-    fwd_2(I, -1, 1)
-    fwd_2(I, 2, 0)
-    looks(12, 13)
-    looks(13, 14)
-    looks(14, 15)
-    fwd_2(I, 0, 1)
-    fwd_2(A, -1, 1)
-    fwd_2(A, 0, 1)
-    looks(15, 16)
+    fwd_2(A, 2, 1)
     fwd_2(I, 1, 1)
-    fwd_2(A, 2, 1)
-    fwd_2(I, 2, 1)
     f_split()
-    fwd_2(I, 0, 0)
     f_rows()
     f_cross()
     f_tower_one()
     f_tower_two()
-    hc = G[:, 80:112, 1024:LN].reshape(1024, 128)
-    zl = nn(h2[...], hc) + bia[5:6, 0:128]
+    hc = G[:, 0:32, 1024:LN].reshape(1024, 128)
+    zl = nn(h2[...], hc)
+    zl = jnp.where(lax.broadcasted_iota(jnp.int32, zl.shape, 1) < 64, pltpu.roll(zl, 64, 1), zl) + bia[5:6, 0:128]
     yl = jnp.broadcast_to(B.lab_v[...].reshape(1, 384).astype(F32), (128, 384)).T
     lossv = jnp.maximum(zl, 0.0) + jnp.log1p(jnp.exp(-jnp.abs(zl))) - yl * zl
     dz = (sig(zl) - yl) / total
     M[...] = jnp.zeros_like(M)
     M[6:7, 0:128] = jnp.sum(lossv, axis=0, keepdims=True)
     M[7:8, 0:128] = jnp.sum(dz, axis=0, keepdims=True)
-    hrow = hc.astype(F32).T[0:1]
+    hrow = hc.astype(F32).T[64:65]
     for n in range(8):
         c = slice(128 * n, 128 * n + 128)
         M[5:6, c] = jnp.sum(dz * h2[:, c].astype(F32), axis=0, keepdims=True)
@@ -800,13 +806,17 @@
 
     def grad_in():
         for n in range(4):
-            put(1, 8 * n, tn(d1[:, 256 * n : 256 * n + 256], xl[3]))
+            g = d1[:, 256 * n : 256 * n + 256]
+            put(1, 8 * n, tn(g, xl[3, :, 0:1024]))
+            B.TE[256 * n : 256 * n + 256] = pltpu.roll(tn(g, xl[3, :, 1024:LN]), 3, 1)
         for n in parts_of(1):
             s0(n)
 
     def down_x():
-        for lo, n in CH:
+        for lo, n in CH[:4]:
             dx[:, lo : lo + n] = nn(d1[...], G[:, 48:80, lo : lo + n].reshape(1024, n))
+        g = pltpu.roll(nn(d1[...], G[:, 0:32, 1024:LN].reshape(1024, 128)), 125, 1)
+        dx[:, 1024:LN] = jnp.where(lax.broadcasted_iota(jnp.int32, g.shape, 1) < 3, g, 0.0)
 
     def chain(l):
         dq_ref = dql.at[l]
@@ -833,7 +843,11 @@
         for lo, n in CH:
             gu = tn(pr[l], dql[l, :, lo : lo + n]).reshape(32, 8, n)
             gv = tn(dpr[l], xl[l, :, lo : lo + n]).reshape(32, 8, n)
-            gg = jnp.concatenate([gv, gu], axis=1).astype(BF)
+            gg = jnp.concatenate([gv, gu], axis=1)
+            if lo == 1024 and l:
+                te = B.TE[...].reshape(32, 32, 128)
+                gg = gg + (te[:, 0:16] if l == 2 else te[:, 16:32])
+            gg = gg.astype(BF)
             for k in range(32):
                 rep, xx, yy, zz = place(k)
                 a, b = (yy, xx) if yfirst else (xx, yy)
@@ -921,49 +935,49 @@
     s1(M0)
     s1(M1)
     chain(2)
-    cross_grads(2)
+    grad_in()
     chain(1)
     chain(0)
+    s2(M1)
+    s2(M0)
+    rows_out()
     cross_grads(0)
-    s2(M1)
+    s1(IN)
+    cross_grads(2)
+    rows_in(0)
+    cross_grads(1)
     small(1)
-    rows_out()
-    grad_in()
+    s1(C0)
+    rows_in(1)
+    rows_in(2)
     s3(M1)
     small(2)
-    s1(C2)
-    s1(IN)
-    cross_grads(1)
-    s2(M0)
-    small(3)
-    s2(IN)
-    s3(M0)
-    s1(C0)
-    s2(C2)
-    s1(C1)
-    s3(IN)
-    rows_in(0)
-    rows_in(1)
-    s4(M1)
-    rows_in(2)
     rows_in(3)
     rows_in(4)
+    s2(IN)
+    rows_in(5)
+    s2(C0)
+    s1(C2)
+    rows_in(6)
+    s3(M0)
+    rows_in(7)
+    s4(M1)
+    s1(C1)
+    small(3)
+    s3(IN)
+    s2(C1)
+    table_sum()
+    s2(C2)
+    small(4)
+    s3(C0)
+    s3(C2)
+    table_both()
+    s4(IN)
+    s3(C1)
+    s4(C0)
     s4(M0)
-    s3(C2)
-    s2(C1)
-    s2(C0)
-    s3(C1)
-    rows_in(5)
-    rows_in(6)
-    s3(C0)
-    rows_in(7)
     s4(C2)
-    table_sum()
-    small(4)
     s4(C1)
-    s4(IN)
-    table_both()
-    s4(C0)
 
     def dw(i, _):
         d = (me + i) % 16
@@ -997,7 +1011,7 @@
         xT=V((LN, 384), F32), dx=V((384, LN), F32), xl=V((4, 384, LN), BF), qc=V((3, 384, LN), F32), pr=V((3, 384, 256), BF),
         VT=V((3, 256, LN), BF), UT=V((3, 256, LN), BF), h1=V((384, 1024), BF), h2=V((384, 1024), BF),
         d0=V((384, LN), F32), dql=V((3, 384, LN), BF), dpr=V((3, 384, 256), BF), DE=V((27, 40, 384), F32), M=V((8, LN), F32), R=V((2, 320, 512), F32),
-        MC=V((8, LN), F32), MS=V((3, 8, LN), F32), MX=V((5, 8, LN), F32), gg=V((2496, 128), F32), gtc=V((2496, 128), F32), bia=V((8, LN), F32),
+        MC=V((8, LN), F32), MS=V((3, 8, LN), F32), MX=V((5, 8, LN), F32), TE=V((1024, 128), F32), gg=V((2496, 128), F32), gtc=V((2496, 128), F32), bia=V((8, LN), F32),
         inv=pltpu.SMEM((32,), jnp.int32), lsem=dma((9,)), wss=dma((3, 40)), wrs=dma((3, 32)), ess=dma((16,)), ers=dma((16,)), dss=dma((16,)), drs=dma((16,)),
         rss=dma((64,)), rrs=dma((64,)), osem=dma((9,)))
     for n, shape in enumerate(SUMS):
@@ -1059,8 +1073,12 @@
             c.wait()
         w_in, m_in, v_in = vin[3 * k : 3 * k + 3]
         for n, lo, nb in rows:
+            g = sums[n][:, 0 : w_in.shape[1]]
+            if k == 2:
+                ends = [a[:, WIDTH : WIDTH + 3] for a in (sums[2], sums[3])]
+                g = jnp.concatenate([g, jnp.concatenate(ends, axis=0)], axis=1)
             at = slice(lo, lo + nb)
-            w, m, v = adamw(w_in[at], m_in[at], v_in[at], sums[n][:, 0 : w_in.shape[1]], RATE_DENSE)
+            w, m, v = adamw(w_in[at], m_in[at], v_in[at], g, RATE_DENSE)
             for o, a in zip(vout[4 * k : 4 * k + 4], (w, m, v, w.astype(BF))):
                 o[at] = a
         out(k)

time: 132 us -> 127 us (0.962)
  Pallas kernels: 131 us -> 126 us
    pallas_call x1, Pallas kernels: 123 us -> 118 us  [mega(): pl.pallas_call(functools.partial(mega_body, total, list(ins) + list(outs)...]
where the time goes in v5:
time: 127 us
  Pallas kernels  126 us (99%)
    pallas_call x1, Pallas kernels, mega(): pl.pallas_call(functools.partial(mega_body, total, list(ins) + list(outs)...  118 us
    pallas_call x1, Pallas kernels, update(): pl.pallas_call(update_body, name='adamw_step', out_shape=tuple(kinds) + (...  7.78 us

profile of v5, /device:TPU:0, one launch (start us, length us, event | category | flops | bytes accessed | tf_op | source)
XLA Modules:
  0.0 126.6 jit_solution(1451508923675257636)
XLA Ops:
  0.7 117.9 %train_step.1 = (f32[2496,128]{1,0:T(8,128)}, f32[8,1152]{1,0:T(8,128)}, f32[32,1024]{1,0:T(8,128)}, f32[32,1024]{1,0:T(8,128)}, f32[16,1152]{1,0:T(8,128)}, /*index=5*/f32[16,1152]{1,0:T(8,128)}, f32[16,1152]{1,0:T(8,128)}) custom-call(s32[26]{0:T(128)} %refs_0_.1, s32[2,12288]{1,0:T(2,128)} %refs_1_.1, f32[2496,128]{1,0:T(8,128)} %bitcast.86, ...), custom_call_target="tpu_custom_call" | custom-call | tf_op jit(solution)/shard_map/train_step/pallas_call | solution.py:1022
  118.6 7.8 %adamw_step.1 = (f32[2496,128]{1,0:T(8,128)}, f32[2496,128]{1,0:T(8,128)}, f32[2496,128]{1,0:T(8,128)}, bf16[2496,128]{1,0:T(8,128)(2,1)}, f32[48,1027]{1,0:T(8,...) custom-call(s32[2]{0:T(128)} %rc.1, ...), custom_call_target="tpu_custom_call" | custom-call | tf_op jit(solution)/shard_map/adamw_step/pallas_call | solution.py:1123

commit v6 on v5

--- a/solution.py
+++ b/solution.py
@@ -627,68 +627,68 @@
             h2[:, c] = (a * sig(a)).astype(BF)
 
     f_own(I)
-    f_prep()
-    looks(0, 1)
-    f_core(U)
     f_own(A)
     f_own(U)
     fwd_z(I, 0)
+    fwd_z(I, 1)
+    f_prep()
+    fwd_z(A, 0)
+    fwd_z(A, 1)
+    fwd_1(U, -1)
+    looks(0, 1)
+    fwd_1(I, 0)
+    f_core(A)
+    fwd_1(A, -1)
     looks(1, 2)
-    fwd_1(A, -1)
+    fwd_2(A, -1, 0)
+    looks(2, 3)
+    fwd_z(A, 2)
+    fwd_1(A, 0)
+    fwd_z(I, 2)
+    fwd_1(A, 1)
     fwd_2(U, -1, 0)
+    fwd_2(U, -1, 1)
+    fwd_1(I, 1)
+    looks(3, 4)
+    fwd_2(I, -1, 0)
     fwd_1(I, -1)
-    fwd_z(A, 0)
-    fwd_1(U, -1)
-    fwd_z(I, 1)
-    fwd_z(A, 1)
-    fwd_1(A, 0)
-    fwd_2(I, -1, 0)
-    fwd_1(I, 0)
-    fwd_z(I, 2)
+    looks(4, 5)
     fwd_2(A, -1, 1)
-    looks(2, 3)
-    fwd_2(A, 0, 0)
-    f_core(I)
-    f_core(A)
-    fwd_2(U, -1, 1)
-    fwd_2(I, -1, 1)
-    looks(3, 4)
-    fwd_z(A, 2)
-    looks(4, 5)
-    looks(5, 6)
     for c in range(4):
         fwd_zl(U, 1, c)
+    fwd_1(A, 2)
+    looks(5, 6)
     looks(6, 7)
-    fwd_2(A, 0, 1)
     fwd_1(I, 2)
-    fwd_1(A, 1)
+    fwd_2(I, 2, 0)
+    fwd_2(I, 0, 0)
+    fwd_2(I, 1, 1)
+    fwd_2(A, 0, 0)
+    fwd_2(A, 2, 0)
     fwd_2(I, 1, 0)
     fwd_2(A, 1, 0)
-    fwd_1(I, 1)
+    fwd_2(A, 0, 1)
     looks(7, 8)
     looks(8, 9)
-    fwd_2(A, -1, 0)
-    fwd_2(A, 2, 0)
-    fwd_1(A, 2)
+    fwd_2(A, 1, 1)
     looks(9, 10)
+    looks(10, 11)
+    looks(11, 12)
+    fwd_2(I, -1, 1)
+    looks(12, 13)
+    f_core(I)
+    looks(13, 14)
     for c in range(4):
         fwd_zl(U, 0, c)
-    fwd_2(I, 0, 0)
-    looks(10, 11)
-    looks(11, 12)
-    looks(12, 13)
-    looks(13, 14)
+    fwd_2(I, 0, 1)
+    looks(14, 15)
     fwd_2(I, 2, 1)
-    fwd_2(A, 1, 1)
-    looks(14, 15)
-    fwd_2(I, 0, 1)
     looks(15, 16)
-    fwd_2(I, 2, 0)
+    fwd_2(A, 2, 1)
+    f_core(U)
+    f_split()
     for c in range(4):
         fwd_zl(U, 2, c)
-    fwd_2(A, 2, 1)
-    fwd_2(I, 1, 1)
-    f_split()
     f_rows()
     f_cross()
     f_tower_one()
@@ -1061,11 +1061,32 @@
             outs.append(c)
 
     span = lambda part: pl.ds(832 * part, 832)
+    third = lambda part: [load(a.at[span(part)], b.at[span(part)]) for a, b in ((hbm[0], vin[0]), (hbm[1], vin[1]), (hbm[2], vin[2]), (gt, vg))]
+    table = [third(0), third(1)]
     dense = {k: [load(hbm[3 * k + j], vin[3 * k + j]) for j in range(3)] for k in (2, 3, 1)}
     gradients = [load(a, b) for a, b in zip((*sums, MO), near)]
     sums, MO = near[:5], near[5]
-    table = [[load(a.at[span(part)], b.at[span(part)]) for a, b in ((hbm[0], vin[0]), (hbm[1], vin[1]), (hbm[2], vin[2]), (gt, vg))] for part in range(3)]
+    table.append(third(2))
     dense.update({k: [load(hbm[3 * k + j], vin[3 * k + j]) for j in range(3)] for k in (4, 5)})
+    row = lax.broadcasted_iota(jnp.int32, (64, 128), 0)
+    lane = lax.broadcasted_iota(jnp.int32, (64, 128), 1)
+    use = ((row // 2) * 128 + lane) < jnp.where(row % 2 == 0, rc[0], rc[1])
+    def update_third(part):
+        for c in table[part]:
+            c.wait()
+        for i in range(13):
+            q = pl.ds(832 * part + i * 64, 64)
+            w, m, v = vin[0][q], vin[1][q], vin[2][q]
+            nw, nm, nv = adamw(w, m, v, vg[q], RATE_TABLE)
+            nw = jnp.where(use, nw, w)
+            vout[0][q] = nw
+            vout[1][q] = jnp.where(use, nm, m)
+            vout[2][q] = jnp.where(use, nv, v)
+            vout[3][q] = nw.astype(BF)
+        out(0, span(part))
+
+    update_third(0)
+    update_third(1)
     for c in gradients:
         c.wait()
     for k, rows in ((2, [(1, 0, 32)]), (3, [(0, 0, 32)]), (1, [(4, 0, 16), (3, 16, 16), (2, 32, 16)])):
@@ -1082,22 +1103,7 @@
             for o, a in zip(vout[4 * k : 4 * k + 4], (w, m, v, w.astype(BF))):
                 o[at] = a
         out(k)
-    row = lax.broadcasted_iota(jnp.int32, (64, 128), 0)
-    lane = lax.broadcasted_iota(jnp.int32, (64, 128), 1)
-    use = ((row // 2) * 128 + lane) < jnp.where(row % 2 == 0, rc[0], rc[1])
-    for part in range(3):
-        for c in table[part]:
-            c.wait()
-        for i in range(13):
-            q = pl.ds(832 * part + i * 64, 64)
-            w, m, v = vin[0][q], vin[1][q], vin[2][q]
-            nw, nm, nv = adamw(w, m, v, vg[q], RATE_TABLE)
-            nw = jnp.where(use, nw, w)
-            vout[0][q] = nw
-            vout[1][q] = jnp.where(use, nm, m)
-            vout[2][q] = jnp.where(use, nv, v)
-            vout[3][q] = nw.astype(BF)
-        out(0, span(part))
+    update_third(2)
     loss[0, 0] = jnp.max(MO[6:7, 0:128])
     k = lax.axis_index("dp") * 2 + lax.axis_index("rep")
     gb = jnp.concatenate([MO[0:1, :WIDTH], MO[1:2, :WIDTH], MO[2:3, :WIDTH], MO[3:4, :1024], MO[4:5, :1024], MO[7:8, :1]], axis=1)

time: 127 us -> 129 us (1.016)
  Pallas kernels: 126 us -> 128 us
    pallas_call x1, Pallas kernels: 118 us -> 121 us  [mega(): pl.pallas_call(functools.partial(mega_body, total, list(ins) + list(outs)...]
where the time goes in v6:
time: 129 us
  Pallas kernels  128 us (99%)
    pallas_call x1, Pallas kernels, mega(): pl.pallas_call(functools.partial(mega_body, total, list(ins) + list(outs)...  121 us
    pallas_call x1, Pallas kernels, update(): pl.pallas_call(update_body, name='adamw_step', out_shape=tuple(kinds) + (...  7.24 us

profile of v6, /device:TPU:0, one launch (start us, length us, event | category | flops | bytes accessed | tf_op | source)
XLA Modules:
  0.0 129.2 jit_solution(2634100945438719186)
XLA Ops:
  0.7 121.1 %train_step.1 = (f32[2496,128]{1,0:T(8,128)}, f32[8,1152]{1,0:T(8,128)}, f32[32,1024]{1,0:T(8,128)}, f32[32,1024]{1,0:T(8,128)}, f32[16,1152]{1,0:T(8,128)}, /*index=5*/f32[16,1152]{1,0:T(8,128)}, f32[16,1152]{1,0:T(8,128)}) custom-call(s32[26]{0:T(128)} %refs_0_.1, s32[2,12288]{1,0:T(2,128)} %refs_1_.1, f32[2496,128]{1,0:T(8,128)} %bitcast.86, ...), custom_call_target="tpu_custom_call" | custom-call | tf_op jit(solution)/shard_map/train_step/pallas_call | solution.py:1022
  121.8 7.2 %adamw_step.1 = (f32[2496,128]{1,0:T(8,128)}, f32[2496,128]{1,0:T(8,128)}, f32[2496,128]{1,0:T(8,128)}, bf16[2496,128]{1,0:T(8,128)(2,1)}, f32[48,1027]{1,0:T(8,...) custom-call(s32[2]{0:T(128)} %rc.1, ...), custom_call_target="tpu_custom_call" | custom-call | tf_op jit(solution)/shard_map/adamw_step/pallas_call | solution.py:1129
